TPU v7x, 512 devices: a whole 4x8x8 slice. The times are simulated.
512 devices in a mesh: dp: 4 (over y_hi), expert: 128 (over y_lo, x, z, core).
Axes of the slice: x: 4, y: 8 (y_hi: 4, y_lo: 2; y = y_hi * 2 + y_lo), z: 8, core: 2. Of those that a mesh axis runs over, the one named last changes fastest.
Arguments:
- tokens: bfloat16 [512, 196, 768], P(('dp', 'expert')), may hold values from -100 to 100
- router: bfloat16 [768, 128], replicated
- up_weight: bfloat16 [128, 768, 3072], P('expert', None, 'dp'), may hold values from -0.21875 to 0.21875
- down_weight: bfloat16 [128, 3072, 768], P('expert', 'dp'), may hold values from -0.109375 to 0.109375
- cotangent: bfloat16 [512, 196, 768], P(('dp', 'expert')), may hold values from -6 to 6
Outputs:
- grad_tokens: bfloat16 [512, 196, 768], P(('dp', 'expert'))
- grad_router: float32 [768, 128], replicated
- grad_down: bfloat16 [128, 3072, 768], P('expert', 'dp')
All inputs are finite; a program needn't handle non-finite values.
Results may differ from a plain program's by a relative error of at most 0.008.
Values may be sent and summed in bfloat16 or wider, within the bound.
No kernel may reach another device: no remote copies, remote signals or barrier semaphores. Data moves between devices by JAX's collectives and lax.ppermute only.
A program may use at most 64 MiB of HBM per device.

v0:
```python
import math

import jax
import jax.numpy as jnp
from jax import lax
from jax.sharding import PartitionSpec as P

GELU_SCALE = math.sqrt(2.0 / math.pi)
GELU_CUBIC = 0.044715


def gelu_tanh(values):
    return (
        0.5
        * values
        * (1.0 + jnp.tanh(GELU_SCALE * (values + GELU_CUBIC * values * values * values)))
    )


def gelu_slope(values):
    inner = jnp.tanh(GELU_SCALE * (values + GELU_CUBIC * values * values * values))
    return 0.5 * (1.0 + inner) + 0.5 * values * (1.0 - inner * inner) * GELU_SCALE * (
        1.0 + 3.0 * GELU_CUBIC * values * values
    )


def route_in(stacked_rows, row_work):
    own_slots = lax.all_to_all(stacked_rows, "expert", split_axis=2, concat_axis=1, tiled=True)
    return row_work(lax.all_gather(own_slots, "dp", axis=1, tiled=True), jnp.int32(0))


def route_back(term_fn, own_rows):
    summed = lax.psum_scatter(
        term_fn(jnp.int32(0), own_rows * lax.axis_size("dp")), "dp", scatter_dimension=0, tiled=True
    )
    return lax.all_to_all(
        summed.astype(jnp.bfloat16), "expert", split_axis=0, concat_axis=2, tiled=True
    )


def shards(tokens, router, up_weight, down_weight, cotangent):
    logits = jnp.einsum("bmd,ds->bms", tokens, router, preferred_element_type=jnp.float32)
    dispatch = jax.nn.softmax(logits, axis=1)
    combine = jax.nn.softmax(logits, axis=2)
    dispatch_low = dispatch.astype(jnp.bfloat16)
    combine_low = combine.astype(jnp.bfloat16)
    slot_inputs = jnp.einsum(
        "bms,bmd->bsd", dispatch_low, tokens, preferred_element_type=jnp.float32
    ).astype(jnp.bfloat16)
    slot_cotangent = jnp.einsum(
        "bms,bmd->bsd", combine_low, cotangent, preferred_element_type=jnp.float32
    ).astype(jnp.bfloat16)

    def project_up(block_rows, first_row):
        return (
            jnp.einsum(
                "red,edf->ref", block_rows[0], up_weight, preferred_element_type=jnp.float32
            ),
        )

    (hidden_pre,) = route_in(slot_inputs[None], project_up)
    activation = gelu_tanh(hidden_pre).astype(jnp.bfloat16)
    own_rows = hidden_pre.shape[0] // lax.axis_size("dp")

    def project_down(first_row, row_count):
        return jnp.einsum(
            "ref,efd->red", activation, down_weight, preferred_element_type=jnp.float32
        )[:, None]

    slot_outputs = route_back(project_down, own_rows)[:, 0]

    def project_back(block_rows, first_row):
        upstream = jnp.einsum(
            "red,efd->ref", block_rows[0], down_weight, preferred_element_type=jnp.float32
        )
        return (block_rows[0], (upstream * gelu_slope(hidden_pre)).astype(jnp.bfloat16))

    grad_rows, hidden_grad = route_in(slot_cotangent[None], project_back)

    def project_input(first_row, row_count):
        return jnp.einsum(
            "ref,edf->red", hidden_grad, up_weight, preferred_element_type=jnp.float32
        )[:, None]

    input_grads = route_back(project_input, own_rows)[:, 0]
    grad_down = jnp.einsum(
        "ref,red->efd", activation, grad_rows, preferred_element_type=jnp.float32
    ).astype(jnp.bfloat16)
    combine_grad = jnp.einsum(
        "bmd,bsd->bms", cotangent, slot_outputs, preferred_element_type=jnp.float32
    )
    dispatch_grad = jnp.einsum(
        "bmd,bsd->bms", tokens, input_grads, preferred_element_type=jnp.float32
    )
    logit_grad = combine * (combine_grad - jnp.sum(combine * combine_grad, axis=2, keepdims=True))
    logit_grad = logit_grad + dispatch * (
        dispatch_grad - jnp.sum(dispatch * dispatch_grad, axis=1, keepdims=True)
    )
    logit_low = logit_grad.astype(jnp.bfloat16)
    grad_tokens = jnp.einsum(
        "bms,bsd->bmd", dispatch_low, input_grads, preferred_element_type=jnp.float32
    )
    grad_tokens = grad_tokens + jnp.einsum(
        "bms,ds->bmd", logit_low, router, preferred_element_type=jnp.float32
    )
    router_term = jnp.einsum("bmd,bms->ds", tokens, logit_low, preferred_element_type=jnp.float32)
    grad_router = lax.psum(router_term, ("dp", "expert"))
    return (grad_tokens.astype(jnp.bfloat16), grad_router, grad_down)


def solution(mesh):
    placed = (
        P(("dp", "expert"), None, None),
        P(),
        P("expert", None, "dp"),
        P("expert", "dp", None),
        P(("dp", "expert"), None, None),
    )
    return jax.shard_map(
        shards,
        mesh=mesh,
        in_specs=placed,
        out_specs=(P(("dp", "expert"), None, None), P(), P("expert", "dp", None)),
        check_vma=False,
    )
```

profile of v0, /device:TPU:1, one launch (start us, length us, event | category | flops | bytes accessed | tf_op | source)
XLA Modules:
  0.0 482.1 jit_solution(16856911164849701542)
XLA Ops:
  7.2 1.5 fusion.68
  8.6 0.2 fusion.46
  8.8 1.2 fusion.17
  10.1 0.3 copy.39
  10.4 0.5 broadcast.78
  10.9 1.8 reduce.12
  12.7 0.7 reshape.154
  13.4 16.6 %all-to-all-start.1 = ((bf16[128,2,384]{2,1,0:T(2,128)(2,1)}), bf16[128,2,384]{2,1,0:T(2,128)(2,1)S(1)}, u32[]{:S(2)}, u32[]{:S(2)}) async-start(bf16[128,2,384]{2,1,0:T(2,128)(2,1)} %reshape.154), calls=%async_computation.1 | async-start | bytes 393216 | tf_op jit(solution)/shard_map/all_to_all | solution.py:28
  30.1 0.3 fusion.16
  30.4 0.3 copy.40
  30.7 1.8 reduce.13
  32.5 0.7 reshape.156
  33.3 8.9 %all-to-all-done.1 = bf16[128,2,384]{2,1,0:T(2,128)(2,1)S(1)} async-done(((bf16[128,2,384]{2,1,0:T(2,128)(2,1)}), bf16[128,2,384]{2,1,0:T(2,128)(2,1)S(1)}, u32[]{:S(2)}, u32[]{:S(2)}) %all-to-all-start.1) | async-done | bytes 196640 | tf_op jit(solution)/shard_map/all_to_all | solution.py:28
  42.2 5.7 %all-to-all-start = ((bf16[128,2,384]{2,1,0:T(2,128)(2,1)}), bf16[128,2,384]{2,1,0:T(2,128)(2,1)S(1)}, u32[]{:S(2)}, u32[]{:S(2)}) async-start(bf16[128,2,384]{2,1,0:T(2,128)(2,1)} %reshape.156), calls=%async_computation | async-start | bytes 393216 | tf_op jit(solution)/shard_map/all_to_all | solution.py:28
  47.9 0.0 reduce-scatter.3.cloned.1.call-start
  47.9 0.1 reshape.155
  48.1 18.3 %all-gather.1 = bf16[1,1,512,768]{3,2,1,0:T(8,128)(2,1)} all-gather(bf16[1,1,128,768]{3,2,1,0:T(8,128)(2,1)S(1)} %copy.17), channel_id=3, replica_groups=mesh['dp'=4,'expert'=128] {'dp'}, dimensions={2}, use_global_device_ids=true | all-gather | bytes 983040 | tf_op jit(solution)/shard_map/all_gather | solution.py:29
  66.4 0.1 reshape.157
  66.6 15.7 %all-gather = bf16[1,1,512,768]{3,2,1,0:T(8,128)(2,1)S(1)} all-gather(bf16[1,1,128,768]{3,2,1,0:T(8,128)(2,1)S(1)} %copy.15), channel_id=2, replica_groups=mesh['dp'=4,'expert'=128] {'dp'}, dimensions={2}, use_global_device_ids=true | all-gather | bytes 983040 | tf_op jit(solution)/shard_map/all_gather | solution.py:29
  82.3 1.9 fusion.12
  84.2 4.8 %convolution_bitcast_fusion.1 = f32[512,1,1,768]{3,0,2,1:T(8,128)} fusion(bf16[1,768,768]{2,1,0:T(8,128)(2,1)S(1)} %copy-done, f32[512,768]{1,0:T(8,128)} %fusion.12, bf16[1,768,768]{2,1,0:T(8,128)(2,1)} %param.8, bf16[1,1,512,768]{3,2,1,0:T(8,128)(2,1)S(1)} %all-gather), kind=kOutput, calls=%fused_computation.13 | convolution fusion | flops 1215430656 | bytes 6291456 | tf_op jit(solution)/shard_map/ref,edf->red/dot_general | solution.py:81
  89.0 0.0 reduce-scatter.3.cloned.1.call-update
  89.1 0.0 reduce-scatter.5.cloned.1.call-start
  89.1 3.9 convolution_bitcast_fusion
  93.1 0.0 reduce-scatter.5.cloned.1.call-update
  93.1 44.5 %reduce-scatter.3.cloned.1.call-done = f32[128,1,1,768]{3,0,2,1:T(8,128)} async-done(((f32[512,1,1,768]{3,0,2,1:T(8,128)}), f32[128,1,1,768]{3,0,2,1:T(8,128)}) %reduce-scatter.3.cloned.1.call-update) | async-done | bytes 393232 | tf_op jit(solution)/shard_map/reduce_scatter | solution.py:33
  137.6 1.0 convert_element_type.49
  138.6 0.7 reduce.14
  139.3 0.7 reshape.158
  140.1 12.2 %all-to-all-start.2 = ((bf16[128,2,384]{2,1,0:T(2,128)(2,1)}), bf16[128,2,384]{2,1,0:T(2,128)(2,1)S(1)}, u32[]{:S(2)}, u32[]{:S(2)}) async-start(bf16[128,2,384]{2,1,0:T(2,128)(2,1)} %reshape.158), calls=%async_computation.3 | async-start | bytes 393216 | tf_op jit(solution)/shard_map/all_to_all | solution.py:36
  152.2 32.5 %reduce-scatter.5.cloned.1.call-done = f32[128,1,1,768]{3,0,2,1:T(8,128)} async-done(((f32[512,1,1,768]{3,0,2,1:T(8,128)}), f32[128,1,1,768]{3,0,2,1:T(8,128)}) %reduce-scatter.5.cloned.1.call-update) | async-done | bytes 393232 | tf_op jit(solution)/shard_map/reduce_scatter | solution.py:33
  184.7 1.0 convert_element_type.51
  185.8 0.7 reduce.15
  186.5 0.7 reshape.160
  187.2 11.6 %all-to-all-start.3 = ((bf16[128,2,384]{2,1,0:T(2,128)(2,1)}), bf16[128,2,384]{2,1,0:T(2,128)(2,1)S(1)}, u32[]{:S(2)}, u32[]{:S(2)}) async-start(bf16[128,2,384]{2,1,0:T(2,128)(2,1)} %reshape.160), calls=%async_computation.5 | async-start | bytes 393216 | tf_op jit(solution)/shard_map/all_to_all | solution.py:36
  198.9 0.0 all-reduce.2.cloned.1.call-start
  198.9 3.4 fusion.7
  202.3 0.1 reshape.159
  202.5 0.2 convolution_bitcast_fusion.3
  202.7 8.2 %all-to-all-done.3 = bf16[128,2,384]{2,1,0:T(2,128)(2,1)S(1)} async-done(((bf16[128,2,384]{2,1,0:T(2,128)(2,1)}), bf16[128,2,384]{2,1,0:T(2,128)(2,1)S(1)}, u32[]{:S(2)}, u32[]{:S(2)}) %all-to-all-start.3) | async-done | bytes 196640 | tf_op jit(solution)/shard_map/all_to_all | solution.py:36
  210.9 0.1 reshape.161
  211.1 0.3 multiply_reduce_fusion.1
  211.4 0.2 add_convert_fusion
  211.6 1.0 convolution_bitcast_fusion.2
  212.6 0.2 fusion.41
  212.9 1.0 fusion.10
  213.9 259.8 %all-reduce.2.cloned.1.call-done = f32[768,128]{0,1:T(8,128)} async-done(((f32[768,128]{0,1:T(8,128)}), f32[768,128]{0,1:T(8,128)}) %all-reduce.2.cloned.1.call-update) | async-done | bytes 393232 | tf_op jit(solution)/shard_map/psum | solution.py:107
  473.7 1.9 copy.20
  (15 shorter events, 0.1 us)
Async XLA Ops:
  7.2 75.1 %copy-start = (bf16[1,768,768]{2,1,0:T(8,128)(2,1)S(1)}, bf16[1,768,768]{2,1,0:T(8,128)(2,1)}, u32[]{:S(2)}) copy-start(bf16[1,768,768]{2,1,0:T(8,128)(2,1)} %param.7) | copy-start | bytes 3538948
  7.2 22.9 %copy-start.4 = (bf16[1,196,768]{2,1,0:T(8,128)(2,1)S(1)}, bf16[1,196,768]{2,1,0:T(8,128)(2,1)}, u32[]{:S(2)}) copy-start(bf16[1,196,768]{2,1,0:T(8,128)(2,1)} %param.9) | copy-start | bytes 903172
  13.4 28.7 %all-to-all-start.1 = ((bf16[128,2,384]{2,1,0:T(2,128)(2,1)}), bf16[128,2,384]{2,1,0:T(2,128)(2,1)S(1)}, u32[]{:S(2)}, u32[]{:S(2)}) async-start(bf16[128,2,384]{2,1,0:T(2,128)(2,1)} %reshape.154), calls=%async_computation.1 | async-start | bytes 393216 | tf_op jit(solution)/shard_map/all_to_all | solution.py:28
  42.2 24.2 %all-to-all-start = ((bf16[128,2,384]{2,1,0:T(2,128)(2,1)}), bf16[128,2,384]{2,1,0:T(2,128)(2,1)S(1)}, u32[]{:S(2)}, u32[]{:S(2)}) async-start(bf16[128,2,384]{2,1,0:T(2,128)(2,1)} %reshape.156), calls=%async_computation | async-start | bytes 393216 | tf_op jit(solution)/shard_map/all_to_all | solution.py:28
  47.9 89.7 %reduce-scatter.3.cloned.1.call-start = ((), (), s32[]{:S(2)}) async-start(), calls=%async_computation.6 | async-start | bytes 1966080 | tf_op jit(solution)/shard_map/reduce_scatter | solution.py:33
  66.6 15.7 %copy-start.3 = (bf16[1,1,512,768]{3,2,1,0:T(8,128)(2,1)S(1)}, bf16[1,1,512,768]{3,2,1,0:T(8,128)(2,1)}, u32[]{:S(2)}) copy-start(bf16[1,1,512,768]{3,2,1,0:T(8,128)(2,1)} %all-gather.1) | copy-start | bytes 2359300
  89.1 95.7 %reduce-scatter.5.cloned.1.call-start = ((), (), s32[]{:S(2)}) async-start(), calls=%async_computation.7 | async-start | bytes 1966080 | tf_op jit(solution)/shard_map/reduce_scatter | solution.py:33
  140.1 47.2 %all-to-all-start.2 = ((bf16[128,2,384]{2,1,0:T(2,128)(2,1)}), bf16[128,2,384]{2,1,0:T(2,128)(2,1)S(1)}, u32[]{:S(2)}, u32[]{:S(2)}) async-start(bf16[128,2,384]{2,1,0:T(2,128)(2,1)} %reshape.158), calls=%async_computation.3 | async-start | bytes 393216 | tf_op jit(solution)/shard_map/all_to_all | solution.py:36
  187.2 23.7 %all-to-all-start.3 = ((bf16[128,2,384]{2,1,0:T(2,128)(2,1)}), bf16[128,2,384]{2,1,0:T(2,128)(2,1)S(1)}, u32[]{:S(2)}, u32[]{:S(2)}) async-start(bf16[128,2,384]{2,1,0:T(2,128)(2,1)} %reshape.160), calls=%async_computation.5 | async-start | bytes 393216 | tf_op jit(solution)/shard_map/all_to_all | solution.py:36
  198.8 3.6 copy-start.1
  198.9 274.8 %all-reduce.2.cloned.1.call-start = ((), (), s32[]{:S(2)}) async-start(), calls=%async_computation.8 | async-start | bytes 786432 | tf_op jit(solution)/shard_map/psum | solution.py:107
  211.1 1.8 copy-start.2
Sparse Core Ops, SparseCore 0:
  89.2 48.3 reduce-scatter.2
  140.4 44.2 reduce-scatter.4
  212.7 260.8 all-reduce.1
where the time goes:
time: 483 us; the launch traced here: 482 us
  waiting for transfers between devices  354 us (73%)
  starting transfers between devices  46.3 us (10%)
  blocking collectives  33.9 us (7%)
  matrix products  20 us (4%)
  between operations  14 us (3%)
  other arithmetic  7.44 us (2%)
  local copies, waits for them, and re-layouts  6.61 us (1%)
    psum x1, waiting for transfers between devices, shards(): grad_router = lax.psum(router_term, ('dp', 'expert'))  260 us
    reduce_scatter x2, waiting for transfers between devices, route_back(): lax.psum_scatter(term_fn(jnp.int32(0), own_rows * lax.axis_size('dp')), '...  77 us
    all_gather x2, blocking collectives, route_in(): lax.all_gather(own_slots, 'dp', axis=1, tiled=True)  33.9 us
    all_to_all x2, starting transfers between devices, route_back(): lax.all_to_all(summed.astype(jnp.bfloat16), 'expert', split_axis=0, conca...  23.8 us
    all_to_all x2, starting transfers between devices, route_in(): lax.all_to_all(stacked_rows, 'expert', split_axis=2, concat_axis=1, tiled...  22.4 us
  transfers between devices with their start and end apart: 7, of which 5 were waited for; matrix products, arithmetic and copies ran while one was open for 4% of the time, Pallas kernels for 0%

commit v1 on v0

v1 whole, which is shorter than its diff:
```python
import math

import jax
import jax.numpy as jnp
from jax import lax
from jax.sharding import PartitionSpec as P

GELU_SCALE = math.sqrt(2.0 / math.pi)
GELU_CUBIC = 0.044715
LOW = jnp.bfloat16
WIDE = jnp.float32


def gelu_parts(values):
    squared = values * values
    inner = jnp.tanh(GELU_SCALE * (values + GELU_CUBIC * squared * values))
    activation = 0.5 * values * (1.0 + inner)
    slope = 0.5 * (1.0 + inner) + 0.5 * values * (1.0 - inner * inner) * GELU_SCALE * (
        1.0 + 3.0 * GELU_CUBIC * squared
    )
    return activation, slope


def wide_einsum(spec, left, right):
    return jnp.einsum(spec, left, right, preferred_element_type=WIDE)


def expert_rows(rows, up, down):
    hidden_pre = wide_einsum("rd,df->rf", rows[0], up)
    activation, slope = gelu_parts(hidden_pre)
    activation = activation.astype(LOW)
    upstream = wide_einsum("rd,fd->rf", rows[1], down)
    hidden_grad = (upstream * slope).astype(LOW)
    outputs = wide_einsum("rf,fd->rd", activation, down)
    input_grads = wide_einsum("rf,df->rd", hidden_grad, up)
    return outputs, input_grads, activation


def shards(tokens, router, up_weight, down_weight, cotangent):
    tokens, cotangent = tokens[0], cotangent[0]
    up, down = up_weight[0], down_weight[0]
    dp = lax.axis_size("dp")
    here = lax.axis_index("dp")
    to_right = [(i, (i + 1) % dp) for i in range(dp)]
    to_left = [(i, (i - 1) % dp) for i in range(dp)]

    logits = wide_einsum("md,ds->ms", tokens, router)
    dispatch = jax.nn.softmax(logits, axis=0)
    combine = jax.nn.softmax(logits, axis=1)
    dispatch_low = dispatch.astype(LOW)
    combine_low = combine.astype(LOW)
    slot_inputs = wide_einsum("ms,md->sd", dispatch_low, tokens).astype(LOW)
    slot_cotangent = wide_einsum("ms,md->sd", combine_low, cotangent).astype(LOW)

    sent = jnp.stack([slot_inputs, slot_cotangent], axis=1)
    own_slots = lax.all_to_all(sent, "expert", split_axis=0, concat_axis=0, tiled=True)
    own_slots = jnp.swapaxes(own_slots, 0, 1)
    blocks = lax.all_gather(own_slots, "dp", axis=0)

    def block_of(offset):
        return lax.dynamic_index_in_dim(blocks, (here + offset) % dp, 0, keepdims=False)

    far_rows, right_rows, left_rows, own_rows = (block_of(k) for k in (2, 1, 3, 0))
    far_out, far_in, far_act = expert_rows(far_rows, up, down)
    from_left_far = lax.ppermute(far_out.astype(LOW), "dp", to_right)
    from_right_far = lax.ppermute(far_in.astype(LOW), "dp", to_left)
    right_out, right_in, right_act = expert_rows(right_rows, up, down)
    left_out, left_in, left_act = expert_rows(left_rows, up, down)
    own_out, own_in, own_act = expert_rows(own_rows, up, down)
    from_left = lax.ppermute(
        jnp.stack([(right_out + from_left_far.astype(WIDE)).astype(LOW), right_in.astype(LOW)]),
        "dp",
        to_right,
    )
    from_right = lax.ppermute(
        jnp.stack([left_out.astype(LOW), (left_in + from_right_far.astype(WIDE)).astype(LOW)]),
        "dp",
        to_left,
    )
    all_act = jnp.concatenate([far_act, right_act, left_act, own_act])
    all_grad = jnp.concatenate([far_rows[1], right_rows[1], left_rows[1], own_rows[1]])
    grad_down = wide_einsum("rf,rd->fd", all_act, all_grad).astype(LOW)
    summed = (
        jnp.stack([own_out, own_in]) + from_left.astype(WIDE) + from_right.astype(WIDE)
    ).astype(LOW)

    back = lax.all_to_all(
        jnp.swapaxes(summed, 0, 1), "expert", split_axis=0, concat_axis=0, tiled=True
    )
    slot_outputs, input_grads = back[:, 0], back[:, 1]

    combine_grad = wide_einsum("md,sd->ms", cotangent, slot_outputs)
    dispatch_grad = wide_einsum("md,sd->ms", tokens, input_grads)
    logit_grad = combine * (combine_grad - jnp.sum(combine * combine_grad, axis=1, keepdims=True))
    logit_grad = logit_grad + dispatch * (
        dispatch_grad - jnp.sum(dispatch * dispatch_grad, axis=0, keepdims=True)
    )
    logit_low = logit_grad.astype(LOW)

    router_term = wide_einsum("ms,md->sd", logit_low, tokens)
    by_slot = lax.all_to_all(router_term, "expert", split_axis=0, concat_axis=0, tiled=True)
    slot_sum = lax.psum(jnp.sum(by_slot, axis=0).reshape(6, 128), "dp").reshape(1, -1)
    everywhere = lax.all_to_all(
        jnp.broadcast_to(slot_sum, router_term.shape), "expert", split_axis=0, concat_axis=0, tiled=True
    )
    grad_router = everywhere.T

    grad_tokens = wide_einsum("ms,sd->md", dispatch_low, input_grads)
    grad_tokens = grad_tokens + wide_einsum("ms,ds->md", logit_low, router)
    return (grad_tokens.astype(LOW)[None], grad_router, grad_down[None])


def solution(mesh):
    placed = (
        P(("dp", "expert"), None, None),
        P(),
        P("expert", None, "dp"),
        P("expert", "dp", None),
        P(("dp", "expert"), None, None),
    )
    return jax.shard_map(
        shards,
        mesh=mesh,
        in_specs=placed,
        out_specs=(P(("dp", "expert"), None, None), P(), P("expert", "dp", None)),
        check_vma=False,
    )
```

time: 483 us -> 234 us (0.48)
  waiting for transfers between devices: 354 us -> 69.5 us
  blocking collectives: 33.9 us -> 90.1 us
  starting transfers between devices: 46.3 us -> 21.6 us
  matrix products: 20 us -> 28 us
    psum x1 -> x0, waiting for transfers between devices: 260 us -> none  [shards(): grad_router = lax.psum(router_term, ('dp', 'expert'))]
    all_to_all x0 -> x3, blocking collectives: none -> 83.2 us  [the longest x1 32 us: shards(): lax.all_to_all(sent, 'expert', split_axis=0, concat_axis=0, tiled=True)]
    reduce_scatter x2 -> x0, waiting for transfers between devices: 77 us -> none  [route_back(): lax.psum_scatter(term_fn(jnp.int32(0), own_rows * lax.axis_size('dp')), '...]
    all_gather x0 -> x1, waiting for transfers between devices: none -> 40.3 us  [shards(): blocks = lax.all_gather(own_slots, 'dp', axis=0)]
    all_to_all x4 -> x1, starting transfers between devices: 46.1 us -> 8.42 us  [shards(): lax.all_to_all(jnp.broadcast_to(slot_sum, router_term.shape), 'expert', s...]
    all_gather x2 -> x0, blocking collectives: 33.9 us -> none  [route_in(): lax.all_gather(own_slots, 'dp', axis=1, tiled=True)]
    ppermute x0 -> x4, waiting for transfers between devices: none -> 17.7 us  [the longest x1 9.72 us: shards(): lax.ppermute(jnp.stack([left_out.astype(LOW), (left_in + from_right_far.a...]
    ppermute x0 -> x4, starting transfers between devices: none -> 13.2 us  [the longest x1 5.09 us: shards(): lax.ppermute(jnp.stack([left_out.astype(LOW), (left_in + from_right_far.a...]
  transfers between devices with their start and end apart: 7 -> 6, of which waited for: 5 -> 5; matrix products, arithmetic and copies ran while one was open for 4% -> 8% of each run, Pallas kernels for 0% -> 0%
where the time goes in v1:
time: 234 us
  blocking collectives  90.1 us (39%)
  waiting for transfers between devices  69.5 us (30%)
  matrix products  28 us (12%)
  starting transfers between devices  21.6 us (9%)
  between operations  14.6 us (6%)
  local copies, waits for them, and re-layouts  6.1 us (3%)
  other arithmetic  3.84 us (2%)
    all_gather x1, waiting for transfers between devices, shards(): blocks = lax.all_gather(own_slots, 'dp', axis=0)  40.3 us
    all_to_all x1, blocking collectives, shards(): lax.all_to_all(sent, 'expert', split_axis=0, concat_axis=0, tiled=True)  32 us
    all_to_all x1, blocking collectives, shards(): lax.all_to_all(jnp.swapaxes(summed, 0, 1), 'expert', split_axis=0, concat...  29.2 us
    dot_general x21, matrix products, wide_einsum(): return jnp.einsum(spec, left, right, preferred_element_type=WIDE)  28 us
    all_to_all x1, blocking collectives, shards(): lax.all_to_all(router_term, 'expert', split_axis=0, concat_axis=0, tiled=...  22 us
    all_to_all x1, waiting for transfers between devices, shards(): lax.all_to_all(jnp.broadcast_to(slot_sum, router_term.shape), 'expert', s...  11.4 us
    ppermute x1, waiting for transfers between devices, shards(): lax.ppermute(jnp.stack([left_out.astype(LOW), (left_in + from_right_far.a...  9.72 us
    all_to_all x1, starting transfers between devices, shards(): lax.all_to_all(jnp.broadcast_to(slot_sum, router_term.shape), 'expert', s...  8.42 us
  transfers between devices with their start and end apart: 6, of which 5 were waited for; matrix products, arithmetic and copies ran while one was open for 8% of the time, Pallas kernels for 0%

profile of v1, /device:TPU:1, one launch (start us, length us, event | category | flops | bytes accessed | tf_op | source)
XLA Modules:
  0.0 233.7 jit_solution(4624274765780072615)
XLA Ops:
  7.2 1.5 fusion.221
  8.9 1.2 fusion.62
  10.2 0.3 fusion.63
  10.6 0.4 copy.13
  11.0 32.0 %all_to_all.28 = bf16[128,2,768]{2,1,0:T(2,128)(2,1)S(1)} all-to-all(bf16[128,2,768]{2,1,0:T(2,128)(2,1)S(1)} %copy.13), channel_id=1, replica_groups=mesh['dp'=4,'expert'=128] {'expert'}, dimensions={0} | all-to-all | bytes 786432 | tf_op jit(solution)/shard_map/all_to_all | solution.py:56
  43.0 0.8 copy.14
  43.9 40.3 %all-gather.3.cloned.1.call-done = bf16[8,128,768]{2,1,0:T(8,128)(2,1)} async-done(((bf16[2,128,768]{2,1,0:T(8,128)(2,1)}), bf16[8,128,768]{2,1,0:T(8,128)(2,1)}) %all-gather.3.cloned.1.call-update) | async-done | bytes 1572880 | tf_op jit(solution)/shard_map/all_gather | solution.py:58
  84.2 2.1 multiply_convert_fusion.1
  86.4 1.1 multiply_convert_fusion.2
  87.5 1.2 multiply_convert_fusion.3
  88.7 0.8 dynamic-slice_bitcast_fusion.9
  89.5 0.6 copy-done.1
  90.1 2.6 %fusion.32 = bf16[128,768]{1,0:T(8,128)(2,1)} fusion(bf16[1,768,768]{2,1,0:T(8,128)(2,1)S(1)} %copy-done, bf16[128,768]{1,0:T(8,128)(2,1)S(1)} %get-tuple-element.17, bf16[1,768,768]{2,1,0:T(8,128)(2,1)S(1)} %copy-done.1, f32[128,768]{1,0:T(8,128)} %get-tuple-element.27), kind=kOutput, calls=%fused_computation.39 | convolution fusion | flops 303857664 | bytes 3145728 | tf_op jit(solution)/shard_map/rf,df->rd/dot_general | solution.py:25
  92.7 4.0 %collective-permute-start.2 = (bf16[128,768]{1,0:T(8,128)(2,1)}, bf16[128,768]{1,0:T(8,128)(2,1)}, u32[]{:S(2)}, u32[]{:S(2)}) collective-permute-start(bf16[128,768]{1,0:T(8,128)(2,1)} %fusion.32), channel_id=1, source_target_pairs={{0,384},{128,0},{256,128},{384,256},{1,385},{129,1},{257,129},{385... | collective-permute-start | bytes 589832 | tf_op jit(solution)/shard_map/ppermute | solution.py:66
  96.7 1.0 fusion.35
  97.7 2.2 collective-permute-start
  99.9 2.6 %fusion.57 = bf16[1,128,768]{2,1,0:T(8,128)(2,1)} fusion(bf16[1,768,768]{2,1,0:T(8,128)(2,1)S(1)} %copy-done, bf16[128,768]{1,0:T(8,128)(2,1)S(1)} %copy-done.20, bf16[1,768,768]{2,1,0:T(8,128)(2,1)S(1)} %copy-done.1, f32[128,768]{1,0:T(8,128)} %get-tuple-element.25), kind=kOutput, calls=%fused_computation.48 | convolution fusion | flops 303857664 | bytes 3145728 | tf_op jit(solution)/shard_map/rf,df->rd/dot_general | solution.py:25
  102.5 2.0 multiply_convert_fusion
  104.6 0.3 fusion.66
  104.9 1.7 collective-permute-done.2
  106.6 2.7 %fusion.110 = bf16[1,128,768]{2,1,0:T(8,128)(2,1)} fusion(bf16[128,768]{1,0:T(8,128)(2,1)} %collective-permute-done.2, bf16[1,768,768]{2,1,0:T(8,128)(2,1)S(1)} %copy-done, bf16[128,768]{1,0:T(8,128)(2,1)S(1)} %get-tuple-element.16, bf16[1,768,768]{2,1,0:T(8,128)(2,1)S(1)} %copy-done.1, f32[128,768]{1,0:T(8,128)} %get-tuple-element.23), kind=kOutput, calls=%fused_computation.98 | convolution fusion | flops 304054272 | bytes 3342336 | tf_op jit(solution)/shard_map/rf,df->rd/dot_general | solution.py:25
  109.3 1.0 pad_maximum_fusion.2
  110.3 5.1 %collective-permute-start.3 = (bf16[2,128,768]{2,1,0:T(8,128)(2,1)S(1)}, bf16[2,128,768]{2,1,0:T(8,128)(2,1)}, u32[]{:S(2)}, u32[]{:S(2)}) collective-permute-start(bf16[2,128,768]{2,1,0:T(8,128)(2,1)S(1)} %pad_maximum_fusion.2), channel_id=1, source_target_pairs={{0,384},{128,0},{256,128},{384,256},{1,385},{129,1},{257,129},{385... | collective-permute-start | bytes 1179656 | tf_op jit(solution)/shard_map/ppermute | solution.py:75
  115.4 1.3 fusion.164
  116.7 0.8 pad_maximum_fusion.1
  117.5 1.9 collective-permute-start.1
  119.4 0.3 convolution_bitcast_fusion.2
  119.7 2.8 %convolution_bitcast_fusion.1 = f32[1,128,768]{2,1,0:T(8,128)} fusion(bf16[1,768,768]{2,1,0:T(8,128)(2,1)S(1)} %copy-done, bf16[128,768]{1,0:T(8,128)(2,1)} %get-tuple-element.15, bf16[1,768,768]{2,1,0:T(8,128)(2,1)S(1)} %copy-done.1, f32[128,768]{1,0:T(8,128)} %get-tuple-element.29), kind=kOutput, calls=%fused_computation.8 | convolution fusion | flops 303759360 | bytes 3342336 | tf_op jit(solution)/shard_map/rf,df->rd/dot_general | solution.py:25
  122.5 9.7 %collective-permute-done.3 = bf16[2,128,768]{2,1,0:T(8,128)(2,1)} collective-permute-done((bf16[2,128,768]{2,1,0:T(8,128)(2,1)S(1)}, bf16[2,128,768]{2,1,0:T(8,128)(2,1)}, u32[]{:S(2)}, u32[]{:S(2)}) %collective-permute-start.3) | collective-permute-done | bytes 393248 | tf_op jit(solution)/shard_map/ppermute | solution.py:75
  132.3 6.3 %collective-permute-done.1 = bf16[2,128,768]{2,1,0:T(8,128)(2,1)} collective-permute-done((bf16[2,128,768]{2,1,0:T(8,128)(2,1)}, bf16[2,128,768]{2,1,0:T(8,128)(2,1)}, u32[]{:S(2)}, u32[]{:S(2)}) %collective-permute-start.1) | collective-permute-done | bytes 393248 | tf_op jit(solution)/shard_map/ppermute | solution.py:70
  138.6 1.4 fusion.95
  140.0 0.4 copy.15
  140.4 29.2 %all_to_all.29 = bf16[128,2,768]{2,1,0:T(2,128)(2,1)S(1)} all-to-all(bf16[128,2,768]{2,1,0:T(2,128)(2,1)S(1)} %copy.15), channel_id=1, replica_groups=mesh['dp'=4,'expert'=128] {'expert'}, dimensions={0} | all-to-all | bytes 786432 | tf_op jit(solution)/shard_map/all_to_all | solution.py:87
  169.6 0.5 fusion.222
  170.2 0.2 convolution_bitcast_fusion.3
  170.5 0.3 multiply_reduce_fusion.1
  171.0 0.2 convolution_bitcast_fusion
  171.2 0.4 copy.18
  171.7 22.0 %all_to_all.30 = f32[128,1,768]{2,1,0:T(1,128)S(1)} all-to-all(f32[128,1,768]{2,1,0:T(1,128)S(1)} %copy.18), channel_id=1, replica_groups=mesh['dp'=4,'expert'=128] {'expert'}, dimensions={0} | all-to-all | bytes 786432 | tf_op jit(solution)/shard_map/all_to_all | solution.py:101
  193.7 0.3 reduce_sum.49
  194.0 6.9 %psum.7 = f32[768]{0:T(1024)S(1)} all-reduce(f32[768]{0:T(1024)S(1)} %reduce_sum.49), channel_id=1, replica_groups=mesh['dp'=4,'expert'=128] {'dp'}, use_global_device_ids=true, to_apply=%region_7.8 | all-reduce | flops 768 | bytes 6144 | tf_op jit(solution)/shard_map/psum | solution.py:102
  200.9 1.0 broadcast_in_dim.10
  201.8 8.4 %all-to-all-start.3 = ((f32[128,1,768]{2,1,0:T(1,128)}), f32[128,1,768]{2,1,0:T(1,128)S(1)}, u32[]{:S(2)}, u32[]{:S(2)}) async-start(f32[128,1,768]{2,1,0:T(1,128)} %broadcast_in_dim.10), calls=%async_computation.3 | async-start | bytes 786432 | tf_op jit(solution)/shard_map/all_to_all | solution.py:103
  210.4 2.8 %fusion = bf16[1,768,768]{2,1,0:T(8,128)(2,1)} fusion(bf16[128,768]{1,0:T(8,128)(2,1)S(1)} %copy-done.11, bf16[128,768]{1,0:T(8,128)(2,1)S(1)} %copy-done.13, bf16[128,768]{1,0:T(8,128)(2,1)S(1)} %copy-done.9, bf16[128,768]{1,0:T(8,128)(2,1)S(1)} %copy-done.7, bf16[128,768]{1,0:T(8,128)(2,1)S(1)} %copy-done.15, bf16[128,768]{1,0:T(8,128)(2,1)S(1)} %copy-done.17, ...), kind=kOutput, calls=%fused_computation.1 | convolution fusion | flops 610861056 | bytes 2752512 | tf_op jit(solution)/shard_map/rf,rd->fd/dot_general | solution.py:25
  213.2 0.2 fusion.189
  213.4 1.0 fusion.2
  214.4 11.4 %all-to-all-done.3 = f32[128,1,768]{2,1,0:T(1,128)S(1)} async-done(((f32[128,1,768]{2,1,0:T(1,128)}), f32[128,1,768]{2,1,0:T(1,128)S(1)}, u32[]{:S(2)}, u32[]{:S(2)}) %all-to-all-start.3) | async-done | bytes 393248 | tf_op jit(solution)/shard_map/all_to_all | solution.py:103
  225.8 1.1 copy.23
  (67 shorter events, 0.6 us)
Async XLA Ops:
  7.2 77.0 %copy-start = (bf16[1,768,768]{2,1,0:T(8,128)(2,1)S(1)}, bf16[1,768,768]{2,1,0:T(8,128)(2,1)}, u32[]{:S(2)}) copy-start(bf16[1,768,768]{2,1,0:T(8,128)(2,1)} %param.7) | copy-start | bytes 3538948
  7.2 3.0 %copy-start.5 = (bf16[1,196,768]{2,1,0:T(8,128)(2,1)S(1)}, bf16[1,196,768]{2,1,0:T(8,128)(2,1)}, u32[]{:S(2)}) copy-start(bf16[1,196,768]{2,1,0:T(8,128)(2,1)} %param.9) | copy-start | bytes 903172
  7.2 77.0 %all-gather.3.cloned.1.call-start = ((), (), s32[]{:S(2)}) async-start(), calls=%async_computation.4 | async-start | bytes 1966080 | tf_op jit(solution)/shard_map/all_gather | solution.py:58
  8.7 1.5 copy-start.21
  8.7 1.5 copy-start.23
  8.9 1.3 copy-start.26
  8.9 1.3 copy-start.28
  84.2 2.2 copy-start.4
  86.3 10.3 %copy-start.6 = (bf16[128,768]{1,0:T(8,128)(2,1)}, bf16[128,768]{1,0:T(8,128)(2,1)S(1)}, u32[]{:S(2)}) copy-start(bf16[128,768]{1,0:T(8,128)(2,1)S(1)} %get-tuple-element.26) | copy-start | bytes 589828
  87.5 27.9 %copy-start.8 = (bf16[128,768]{1,0:T(8,128)(2,1)}, bf16[128,768]{1,0:T(8,128)(2,1)S(1)}, u32[]{:S(2)}) copy-start(bf16[128,768]{1,0:T(8,128)(2,1)S(1)} %get-tuple-element.24) | copy-start | bytes 589828
  88.7 1.4 copy-start.1
  89.5 3.2 %copy-start.18 = (bf16[128,768]{1,0:T(8,128)(2,1)}, bf16[128,768]{1,0:T(8,128)(2,1)S(1)}, u32[]{:S(2)}) copy-start(bf16[128,768]{1,0:T(8,128)(2,1)S(1)} %get-tuple-element.17) | copy-start | bytes 589828
  89.5 17.1 %copy-start.16 = (bf16[128,768]{1,0:T(8,128)(2,1)}, bf16[128,768]{1,0:T(8,128)(2,1)S(1)}, u32[]{:S(2)}) copy-start(bf16[128,768]{1,0:T(8,128)(2,1)S(1)} %get-tuple-element.16) | copy-start | bytes 589828
  92.7 13.9 %collective-permute-start.2 = (bf16[128,768]{1,0:T(8,128)(2,1)}, bf16[128,768]{1,0:T(8,128)(2,1)}, u32[]{:S(2)}, u32[]{:S(2)}) collective-permute-start(bf16[128,768]{1,0:T(8,128)(2,1)} %fusion.32), channel_id=1, source_target_pairs={{0,384},{128,0},{256,128},{384,256},{1,385},{129,1},{257,129},{385... | collective-permute-start | bytes 589832 | tf_op jit(solution)/shard_map/ppermute | solution.py:66
  96.7 3.2 %copy-start.20 = (bf16[128,768]{1,0:T(8,128)(2,1)S(1)}, bf16[128,768]{1,0:T(8,128)(2,1)}, u32[]{:S(2)}) copy-start(bf16[128,768]{1,0:T(8,128)(2,1)} %get-tuple-element.18) | copy-start | bytes 589828
  97.7 17.7 %collective-permute-start = (bf16[128,768]{1,0:T(8,128)(2,1)}, bf16[128,768]{1,0:T(8,128)(2,1)}, u32[]{:S(2)}, u32[]{:S(2)}) collective-permute-start(bf16[128,768]{1,0:T(8,128)(2,1)} %fusion.35), channel_id=1, source_target_pairs={{0,128},{128,256},{256,384},{384,0},{1,129},{129,257},{257,385},{3... | collective-permute-start | bytes 589832 | tf_op jit(solution)/shard_map/ppermute | solution.py:65
  104.5 2.0 copy-start.12
  109.3 7.4 %copy-start.14 = (bf16[1,128,768]{2,1,0:T(8,128)(2,1)S(1)}, bf16[1,128,768]{2,1,0:T(8,128)(2,1)}, u32[]{:S(2)}) copy-start(bf16[1,128,768]{2,1,0:T(8,128)(2,1)} %fusion.57) | copy-start | bytes 589828
  110.3 22.0 %collective-permute-start.3 = (bf16[2,128,768]{2,1,0:T(8,128)(2,1)S(1)}, bf16[2,128,768]{2,1,0:T(8,128)(2,1)}, u32[]{:S(2)}, u32[]{:S(2)}) collective-permute-start(bf16[2,128,768]{2,1,0:T(8,128)(2,1)S(1)} %pad_maximum_fusion.2), channel_id=1, source_target_pairs={{0,384},{128,0},{256,128},{384,256},{1,385},{129,1},{257,129},{385... | collective-permute-start | bytes 1179656 | tf_op jit(solution)/shard_map/ppermute | solution.py:75
  115.4 4.0 %copy-start.10 = (bf16[128,768]{1,0:T(8,128)(2,1)S(1)}, bf16[128,768]{1,0:T(8,128)(2,1)}, u32[]{:S(2)}) copy-start(bf16[128,768]{1,0:T(8,128)(2,1)} %get-tuple-element.28) | copy-start | bytes 589828
  117.5 21.1 %collective-permute-start.1 = (bf16[2,128,768]{2,1,0:T(8,128)(2,1)}, bf16[2,128,768]{2,1,0:T(8,128)(2,1)}, u32[]{:S(2)}, u32[]{:S(2)}) collective-permute-start(bf16[2,128,768]{2,1,0:T(8,128)(2,1)} %pad_maximum_fusion.1), channel_id=1, source_target_pairs={{0,128},{128,256},{256,384},{384,0},{1,129},{129,257},{257,385},{3... | collective-permute-start | bytes 1179656 | tf_op jit(solution)/shard_map/ppermute | solution.py:70
  140.4 29.8 %copy-start.2 = (bf16[1,196,768]{2,1,0:T(8,128)(2,1)S(1)}, bf16[1,196,768]{2,1,0:T(8,128)(2,1)}, u32[]{:S(2)}) copy-start(bf16[1,196,768]{2,1,0:T(8,128)(2,1)} %param.5) | copy-start | bytes 903172
  169.6 0.8 copy-start.22
  169.6 0.8 copy-start.24
  169.6 0.8 copy-start.27
  169.6 0.9 copy-start.29
  171.7 38.6 %copy-start.7 = (bf16[128,768]{1,0:T(8,128)(2,1)S(1)}, bf16[128,768]{1,0:T(8,128)(2,1)}, u32[]{:S(2)}) copy-start(bf16[128,768]{1,0:T(8,128)(2,1)} %copy-done.6) | copy-start | bytes 589828
  171.7 38.6 %copy-start.9 = (bf16[128,768]{1,0:T(8,128)(2,1)S(1)}, bf16[128,768]{1,0:T(8,128)(2,1)}, u32[]{:S(2)}) copy-start(bf16[128,768]{1,0:T(8,128)(2,1)} %copy-done.8) | copy-start | bytes 589828
  171.7 38.6 %copy-start.11 = (bf16[128,768]{1,0:T(8,128)(2,1)S(1)}, bf16[128,768]{1,0:T(8,128)(2,1)}, u32[]{:S(2)}) copy-start(bf16[128,768]{1,0:T(8,128)(2,1)} %get-tuple-element.28) | copy-start | bytes 589828
  171.7 38.6 %copy-start.13 = (bf16[128,768]{1,0:T(8,128)(2,1)S(1)}, bf16[128,768]{1,0:T(8,128)(2,1)}, u32[]{:S(2)}) copy-start(bf16[128,768]{1,0:T(8,128)(2,1)} %copy-done.12) | copy-start | bytes 589828
  171.7 38.6 %copy-start.15 = (bf16[128,768]{1,0:T(8,128)(2,1)S(1)}, bf16[128,768]{1,0:T(8,128)(2,1)}, u32[]{:S(2)}) copy-start(bf16[128,768]{1,0:T(8,128)(2,1)} %get-tuple-element.15) | copy-start | bytes 589828
  171.7 38.6 %copy-start.17 = (bf16[128,768]{1,0:T(8,128)(2,1)S(1)}, bf16[128,768]{1,0:T(8,128)(2,1)}, u32[]{:S(2)}) copy-start(bf16[128,768]{1,0:T(8,128)(2,1)} %copy-done.16) | copy-start | bytes 589828
  171.7 38.6 %copy-start.19 = (bf16[128,768]{1,0:T(8,128)(2,1)S(1)}, bf16[128,768]{1,0:T(8,128)(2,1)}, u32[]{:S(2)}) copy-start(bf16[128,768]{1,0:T(8,128)(2,1)} %copy-done.18) | copy-start | bytes 589828
  201.8 24.0 %all-to-all-start.3 = ((f32[128,1,768]{2,1,0:T(1,128)}), f32[128,1,768]{2,1,0:T(1,128)S(1)}, u32[]{:S(2)}, u32[]{:S(2)}) async-start(f32[128,1,768]{2,1,0:T(1,128)} %broadcast_in_dim.10), calls=%async_computation.3 | async-start | bytes 786432 | tf_op jit(solution)/shard_map/all_to_all | solution.py:103
  210.3 2.8 %copy-start.25 = (f32[128]{0:T(128)S(1)}, f32[128]{0:T(128)}, u32[]{:S(2)}) copy-start(f32[128]{0:T(128)} %copy-done.23) | copy-start | bytes 1540
  210.3 2.8 %copy-start.30 = (f32[128]{0:T(128)S(1)}, f32[128]{0:T(128)}, u32[]{:S(2)}) copy-start(f32[128]{0:T(128)} %copy-done.28) | copy-start | bytes 1540
  210.4 3.0 %copy-start.3 = (bf16[768,128]{1,0:T(8,128)(2,1)S(1)}, bf16[768,128]{1,0:T(8,128)(2,1)}, u32[]{:S(2)}) copy-start(bf16[768,128]{1,0:T(8,128)(2,1)} %param.6) | copy-start | bytes 589828
Sparse Core Ops, SparseCore 0:
  43.9 40.2 all-gather.2

commit v2 on v1

v2 whole, which is shorter than its diff:
```python
import functools
import math

import jax
import jax.numpy as jnp
from jax import lax
from jax.experimental import pallas as pl
from jax.experimental.pallas import tpu as pltpu
from jax.sharding import Mesh
from jax.sharding import PartitionSpec as P

GELU_SCALE = math.sqrt(2.0 / math.pi)
GELU_CUBIC = 0.044715
LOW = jnp.bfloat16
WIDE = jnp.float32
EXPERT_SPLIT = {"yl": 2, "x": 4, "z": 8, "core": 2}
EXPERT = tuple(EXPERT_SPLIT)
EVERY = ("dp",) + EXPERT
NEAR = ("yl", "x", "core")
REST = ("dp", "z")
VMEM_BYTES = 48 * 2**20


def wide_einsum(spec, left, right):
    return jnp.einsum(spec, left, right, preferred_element_type=WIDE)


def wide_dot(left, right, left_dim, right_dim):
    return lax.dot_general(
        left, right, (((left_dim,), (right_dim,)), ((), ())), preferred_element_type=WIDE
    )


def in_vmem(count):
    return [pl.BlockSpec(memory_space=pltpu.VMEM)] * count


def cost(flops, bytes_accessed):
    return pl.CostEstimate(flops=flops, bytes_accessed=bytes_accessed, transcendentals=0)


def expert_kernel(rows_ref, grads_ref, up_ref, down_ref, out_ref, in_ref, act_ref):
    up, down = up_ref[...], down_ref[...]
    hidden_pre = wide_dot(rows_ref[...], up, 1, 0)
    squared = hidden_pre * hidden_pre
    inner = jnp.tanh(GELU_SCALE * (hidden_pre + GELU_CUBIC * squared * hidden_pre))
    half = 0.5 * (1.0 + inner)
    activation = (hidden_pre * half).astype(LOW)
    act_ref[...] = activation
    out_ref[...] = wide_dot(activation, down, 1, 0).astype(out_ref.dtype)
    slope = half + 0.5 * hidden_pre * (1.0 - inner * inner) * (
        GELU_SCALE + 3.0 * GELU_SCALE * GELU_CUBIC * squared
    )
    upstream = wide_dot(grads_ref[...], down, 1, 1)
    hidden_grad = (upstream * slope).astype(LOW)
    in_ref[...] = wide_dot(hidden_grad, up, 1, 1).astype(in_ref.dtype)


def expert_rows(rows, grads, up, down, out_type, in_type):
    count, width = rows.shape
    hidden = up.shape[1]
    return pl.pallas_call(
        expert_kernel,
        out_shape=(
            jax.ShapeDtypeStruct((count, width), out_type),
            jax.ShapeDtypeStruct((count, width), in_type),
            jax.ShapeDtypeStruct((count, hidden), LOW),
        ),
        in_specs=in_vmem(4),
        out_specs=tuple(in_vmem(3)),
        compiler_params=pltpu.CompilerParams(vmem_limit_bytes=VMEM_BYTES),
        cost_estimate=cost(8 * count * width * hidden, 4 * width * hidden + 14 * count * width),
    )(rows, grads, up, down)


def grad_kernel(pairs, *refs):
    total = None
    for k in range(pairs):
        term = wide_dot(refs[k][...], refs[pairs + k][...], 0, 0)
        total = term if total is None else total + term
    refs[2 * pairs][...] = total.astype(LOW)


def outer_sum(acts, grads):
    count, hidden = acts[0].shape
    width = grads[0].shape[1]
    pairs = len(acts)
    return pl.pallas_call(
        functools.partial(grad_kernel, pairs),
        out_shape=jax.ShapeDtypeStruct((hidden, width), LOW),
        in_specs=in_vmem(2 * pairs),
        out_specs=in_vmem(1)[0],
        compiler_params=pltpu.CompilerParams(vmem_limit_bytes=VMEM_BYTES),
        cost_estimate=cost(2 * pairs * count * width * hidden, 2 * hidden * width),
    )(*acts, *grads)


def all_to_all(value, axes):
    return lax.all_to_all(value, axes, split_axis=0, concat_axis=0, tiled=True)


def sum_everywhere(term):
    near = lax.axis_size(NEAR)
    rest = lax.axis_size(REST)
    depth, width = term.shape
    part = jnp.sum(all_to_all(term.reshape(near, depth // near, width), NEAR), axis=0)
    parts = jnp.broadcast_to(part.astype(LOW)[None], (rest,) + part.shape)
    part = jnp.sum(all_to_all(parts, REST).astype(WIDE), axis=0)
    whole = all_to_all(jnp.broadcast_to(part[None], (near,) + part.shape), NEAR)
    return whole.reshape(depth, width)


def shards(tokens, router, up_weight, down_weight, cotangent):
    tokens, cotangent = tokens[0], cotangent[0]
    up, down = up_weight[0], down_weight[0]
    dp = lax.axis_size("dp")

    def right(value):
        return lax.ppermute(value, "dp", [(i, (i + 1) % dp) for i in range(dp)])

    def left(value):
        return lax.ppermute(value, "dp", [(i, (i - 1) % dp) for i in range(dp)])

    logits = wide_einsum("md,ds->ms", tokens, router)
    dispatch = jax.nn.softmax(logits, axis=0)
    combine = jax.nn.softmax(logits, axis=1)
    dispatch_low = dispatch.astype(LOW)
    combine_low = combine.astype(LOW)
    slot_inputs = wide_einsum("ms,md->sd", dispatch_low, tokens).astype(LOW)
    slot_cotangent = wide_einsum("ms,md->sd", combine_low, cotangent).astype(LOW)

    sent = jnp.stack([slot_inputs, slot_cotangent], axis=1)
    own_slots = all_to_all(sent, EXPERT)
    own_rows, own_grads = own_slots[:, 0], own_slots[:, 1]

    left_rows, right_grads = right(own_rows), left(own_grads)
    left_grads, right_rows = right(own_grads), left(own_rows)
    far_rows, far_grads = right(left_rows), left(right_grads)

    own_out, own_in, own_act = expert_rows(own_rows, own_grads, up, down, WIDE, WIDE)
    right_out, right_in, right_act = expert_rows(right_rows, right_grads, up, down, WIDE, LOW)
    left_out, left_in, left_act = expert_rows(left_rows, left_grads, up, down, LOW, WIDE)
    from_left_in, from_right_out = right(right_in), left(left_out)
    far_out, far_in, far_act = expert_rows(far_rows, far_grads, up, down, LOW, LOW)
    via_left, via_right = right(far_out), left(far_in)
    grad_down = outer_sum(
        (own_act, right_act, left_act, far_act), (own_grads, right_grads, left_grads, far_grads)
    )
    from_left_out = right((right_out + via_left.astype(WIDE)).astype(LOW))
    from_right_in = left((left_in + via_right.astype(WIDE)).astype(LOW))
    summed_out = own_out + from_left_out.astype(WIDE) + from_right_out.astype(WIDE)
    summed_in = own_in + from_left_in.astype(WIDE) + from_right_in.astype(WIDE)

    back = all_to_all(jnp.stack([summed_out.astype(LOW), summed_in.astype(LOW)], axis=1), EXPERT)
    slot_outputs, input_grads = back[:, 0], back[:, 1]

    combine_grad = wide_einsum("md,sd->ms", cotangent, slot_outputs)
    dispatch_grad = wide_einsum("md,sd->ms", tokens, input_grads)
    logit_grad = combine * (combine_grad - jnp.sum(combine * combine_grad, axis=1, keepdims=True))
    logit_grad = logit_grad + dispatch * (
        dispatch_grad - jnp.sum(dispatch * dispatch_grad, axis=0, keepdims=True)
    )
    logit_low = logit_grad.astype(LOW)
    grad_router = sum_everywhere(wide_einsum("md,ms->ds", tokens, logit_low))

    grad_tokens = wide_einsum("ms,sd->md", dispatch_low, input_grads)
    grad_tokens = grad_tokens + wide_einsum("ms,ds->md", logit_low, router)
    return (grad_tokens.astype(LOW)[None], grad_router, grad_down[None])


def solution(mesh):
    fine = Mesh(mesh.devices.reshape((-1,) + tuple(EXPERT_SPLIT.values())), EVERY)
    placed = (P(EVERY, None, None), P(), P(EXPERT, None, "dp"), P(EXPERT, "dp", None), P(EVERY, None, None))
    return jax.shard_map(
        shards,
        mesh=fine,
        in_specs=placed,
        out_specs=(P(EVERY, None, None), P(), P(EXPERT, "dp", None)),
        check_vma=False,
    )
```

time: 234 us -> 189 us (0.81)
  waiting for transfers between devices: 69.5 us -> 32.3 us
  starting transfers between devices: 21.6 us -> 49.6 us
  matrix products: 28 us -> 3.91 us
  between operations: 14.6 us -> 0.98 us
  Pallas kernels: 0 us -> 7.52 us
  other arithmetic: 3.84 us -> 0.75 us
    all_gather x1 -> x0, waiting for transfers between devices: 40.3 us -> none  [shards(): blocks = lax.all_gather(own_slots, 'dp', axis=0)]
    ppermute x4 -> x12, starting transfers between devices: 13.2 us -> 41.7 us  [the longest x6 24.5 us: left(): return lax.ppermute(value, 'dp', [(i, (i - 1) % dp) for i in range(dp)])]
    dot_general x21 -> x8, matrix products: 28 us -> 3.91 us  [wide_einsum(): return jnp.einsum(spec, left, right, preferred_element_type=WIDE)]
    ppermute x4 -> x12, waiting for transfers between devices: 17.7 us -> 27.7 us  [the longest x6 16.4 us: right(): return lax.ppermute(value, 'dp', [(i, (i + 1) % dp) for i in range(dp)])]
    pallas_call x0 -> x5, Pallas kernels: none -> 7.52 us  [the longest x4 5.08 us: expert_rows(): pl.pallas_call(expert_kernel, out_shape=(jax.ShapeDtypeStruct((count, wid...]
    psum x1 -> x0, blocking collectives: 6.91 us -> none  [shards(): lax.psum(jnp.sum(by_slot, axis=0).reshape(6, 128), 'dp').reshape(1, -1)]
    all_to_all x1, waiting for transfers between devices: 11.4 us -> 4.68 us  [all_to_all(): return lax.all_to_all(value, axes, split_axis=0, concat_axis=0, tiled=True)]
    all_to_all x3 -> x4, blocking collectives: 83.2 us -> 88.3 us  [all_to_all(): return lax.all_to_all(value, axes, split_axis=0, concat_axis=0, tiled=True)]
  transfers between devices with their start and end apart: 6 -> 13, of which waited for: 5 -> 6; matrix products, arithmetic and copies ran while one was open for 8% -> 1% of each run, Pallas kernels for 0% -> 4%
where the time goes in v2:
time: 189 us; the launch traced here: 188 us
  blocking collectives  88.3 us (47%)
  starting transfers between devices  49.6 us (26%)
  waiting for transfers between devices  32.3 us (17%)
  Pallas kernels  7.52 us (4%)
  local copies, waits for them, and re-layouts  4.66 us (2%)
  matrix products  3.91 us (2%)
    all_to_all x4, blocking collectives, all_to_all(): return lax.all_to_all(value, axes, split_axis=0, concat_axis=0, tiled=True)  88.3 us
    ppermute x6, starting transfers between devices, left(): return lax.ppermute(value, 'dp', [(i, (i - 1) % dp) for i in range(dp)])  24.5 us
    ppermute x6, starting transfers between devices, right(): return lax.ppermute(value, 'dp', [(i, (i + 1) % dp) for i in range(dp)])  17.2 us
    ppermute x6, waiting for transfers between devices, right(): return lax.ppermute(value, 'dp', [(i, (i + 1) % dp) for i in range(dp)])  16.4 us
    ppermute x6, waiting for transfers between devices, left(): return lax.ppermute(value, 'dp', [(i, (i - 1) % dp) for i in range(dp)])  11.2 us
    all_to_all x1, starting transfers between devices, all_to_all(): return lax.all_to_all(value, axes, split_axis=0, concat_axis=0, tiled=True)  7.83 us
    pallas_call x4, Pallas kernels, expert_rows(): pl.pallas_call(expert_kernel, out_shape=(jax.ShapeDtypeStruct((count, wid...  5.08 us
    all_to_all x1, waiting for transfers between devices, all_to_all(): return lax.all_to_all(value, axes, split_axis=0, concat_axis=0, tiled=True)  4.68 us
  transfers between devices with their start and end apart: 13, of which 6 were waited for; matrix products, arithmetic and copies ran while one was open for 1% of the time, Pallas kernels for 4%

profile of v2, /device:TPU:1, one launch (start us, length us, event | category | flops | bytes accessed | tf_op | source)
XLA Modules:
  0.0 188.1 jit_solution(6961243276379932603)
XLA Ops:
  0.7 0.9 copy-done
  1.6 1.2 fusion.24
  2.9 0.2 fusion.14
  3.1 0.3 fusion.2
  3.3 0.3 fusion.3
  3.7 0.4 copy.21
  4.1 32.0 %all_to_all.25 = bf16[128,2,768]{2,1,0:T(2,128)(2,1)S(1)} all-to-all(bf16[128,2,768]{2,1,0:T(2,128)(2,1)S(1)} %copy.21), channel_id=1, replica_groups=mesh['dp'=4,'yl'=2,'x'=4,'z'=8,'core'=2] {'yl','x','z','core'}, dimensions={0} | all-to-all | bytes 786432 | tf_op jit(solution)/shard_map/all_to_all | solution.py:99
  36.1 0.5 fusion.26
  36.7 4.4 %collective-permute-start.2 = (bf16[128,768]{1,0:T(8,128)(2,1)S(1)}, bf16[128,768]{1,0:T(8,128)(2,1)S(1)}, u32[]{:S(2)}, u32[]{:S(2)}) collective-permute-start(bf16[128,768]{1,0:T(8,128)(2,1)S(1)} %bitcast.70), channel_id=1, source_target_pairs={{0,128},{128,256},{256,384},{384,0},{1,129},{129,257},{257,385},{3... | collective-permute-start | bytes 589832 | tf_op jit(solution)/shard_map/ppermute | solution.py:119
  41.1 3.2 %collective-permute-start.1 = (bf16[128,768]{1,0:T(8,128)(2,1)S(1)}, bf16[128,768]{1,0:T(8,128)(2,1)S(1)}, u32[]{:S(2)}, u32[]{:S(2)}) collective-permute-start(bf16[128,768]{1,0:T(8,128)(2,1)S(1)} %bitcast.66), channel_id=1, source_target_pairs={{0,384},{128,0},{256,128},{384,256},{1,385},{129,1},{257,129},{385... | collective-permute-start | bytes 589832 | tf_op jit(solution)/shard_map/ppermute | solution.py:122
  44.3 4.5 %collective-permute-done.2.rows_ref = bf16[128,768]{1,0:T(8,128)(2,1)S(1)} collective-permute-done((bf16[128,768]{1,0:T(8,128)(2,1)S(1)}, bf16[128,768]{1,0:T(8,128)(2,1)S(1)}, u32[]{:S(2)}, u32[]{:S(2)}) %collective-permute-start.2) | collective-permute-done | bytes 196640 | tf_op jit(solution)/shard_map/ppermute | solution.py:119
  48.8 3.3 %collective-permute-start.3 = (bf16[128,768]{1,0:T(8,128)(2,1)S(1)}, bf16[128,768]{1,0:T(8,128)(2,1)S(1)}, u32[]{:S(2)}, u32[]{:S(2)}) collective-permute-start(bf16[128,768]{1,0:T(8,128)(2,1)S(1)} %collective-permute-done.2.rows_ref), channel_id=1, source_target_pairs={{0,128},{128,256},{256,384},{384,0},{1,129},{129,257},{257,385},{3... | collective-permute-start | bytes 589832 | tf_op jit(solution)/shard_map/ppermute | solution.py:119
  52.1 2.7 %collective-permute-done.1.grads_ref.refs_5_ = bf16[128,768]{1,0:T(8,128)(2,1)S(1)} collective-permute-done((bf16[128,768]{1,0:T(8,128)(2,1)S(1)}, bf16[128,768]{1,0:T(8,128)(2,1)S(1)}, u32[]{:S(2)}, u32[]{:S(2)}) %collective-permute-start.1) | collective-permute-done | bytes 196640 | tf_op jit(solution)/shard_map/ppermute | solution.py:122
  54.8 4.1 %collective-permute-start.4 = (bf16[128,768]{1,0:T(8,128)(2,1)S(1)}, bf16[128,768]{1,0:T(8,128)(2,1)S(1)}, u32[]{:S(2)}, u32[]{:S(2)}) collective-permute-start(bf16[128,768]{1,0:T(8,128)(2,1)S(1)} %collective-permute-done.1.grads_ref.refs_5_), channel_id=1, source_target_pairs={{0,384},{128,0},{256,128},{384,256},{1,385},{129,1},{257,129},{385... | collective-permute-start | bytes 589832 | tf_op jit(solution)/shard_map/ppermute | solution.py:122
  58.9 2.9 %collective-permute-start = (bf16[128,768]{1,0:T(8,128)(2,1)S(1)}, bf16[128,768]{1,0:T(8,128)(2,1)S(1)}, u32[]{:S(2)}, u32[]{:S(2)}) collective-permute-start(bf16[128,768]{1,0:T(8,128)(2,1)S(1)} %bitcast.71), channel_id=1, source_target_pairs={{0,384},{128,0},{256,128},{384,256},{1,385},{129,1},{257,129},{385... | collective-permute-start | bytes 589832 | tf_op jit(solution)/shard_map/ppermute | solution.py:122
  61.8 3.3 %collective-permute-start.7 = (bf16[128,768]{1,0:T(8,128)(2,1)S(1)}, bf16[128,768]{1,0:T(8,128)(2,1)S(1)}, u32[]{:S(2)}, u32[]{:S(2)}) collective-permute-start(bf16[128,768]{1,0:T(8,128)(2,1)S(1)} %bitcast.67), channel_id=1, source_target_pairs={{0,128},{128,256},{256,384},{384,0},{1,129},{129,257},{257,385},{3... | collective-permute-start | bytes 589832 | tf_op jit(solution)/shard_map/ppermute | solution.py:119
  65.1 8.5 %collective-permute-done.4.grads_ref.refs_7_ = bf16[128,768]{1,0:T(8,128)(2,1)S(1)} collective-permute-done((bf16[128,768]{1,0:T(8,128)(2,1)S(1)}, bf16[128,768]{1,0:T(8,128)(2,1)S(1)}, u32[]{:S(2)}, u32[]{:S(2)}) %collective-permute-start.4) | collective-permute-done | bytes 196640 | tf_op jit(solution)/shard_map/ppermute | solution.py:122
  73.6 1.3 shard_map.78
  74.9 4.0 %collective-permute-start.10 = (bf16[128,768]{1,0:T(8,128)(2,1)S(1)}, bf16[128,768]{1,0:T(8,128)(2,1)S(1)}, u32[]{:S(2)}, u32[]{:S(2)}) collective-permute-start(bf16[128,768]{1,0:T(8,128)(2,1)S(1)} %get-tuple-element.22), channel_id=1, source_target_pairs={{0,384},{128,0},{256,128},{384,256},{1,385},{129,1},{257,129},{385... | collective-permute-start | bytes 589832 | tf_op jit(solution)/shard_map/ppermute | solution.py:122
  78.9 1.3 shard_map.76
  80.2 1.3 shard_map.77
  81.4 2.4 %collective-permute-start.9 = (bf16[128,768]{1,0:T(8,128)(2,1)S(1)}, bf16[128,768]{1,0:T(8,128)(2,1)S(1)}, u32[]{:S(2)}, u32[]{:S(2)}) collective-permute-start(bf16[128,768]{1,0:T(8,128)(2,1)S(1)} %get-tuple-element.20), channel_id=1, source_target_pairs={{0,128},{128,256},{256,384},{384,0},{1,129},{129,257},{257,385},{3... | collective-permute-start | bytes 589832 | tf_op jit(solution)/shard_map/ppermute | solution.py:119
  83.9 1.3 shard_map.79
  85.2 5.0 %collective-permute-start.8 = (bf16[128,768]{1,0:T(8,128)(2,1)S(1)}, bf16[128,768]{1,0:T(8,128)(2,1)S(1)}, u32[]{:S(2)}, u32[]{:S(2)}) collective-permute-start(bf16[128,768]{1,0:T(8,128)(2,1)S(1)} %get-tuple-element.18), channel_id=1, source_target_pairs={{0,384},{128,0},{256,128},{384,256},{1,385},{129,1},{257,129},{385... | collective-permute-start | bytes 589832 | tf_op jit(solution)/shard_map/ppermute | solution.py:122
  90.1 1.9 %collective-permute-start.5 = (bf16[128,768]{1,0:T(8,128)(2,1)S(1)}, bf16[128,768]{1,0:T(8,128)(2,1)S(1)}, u32[]{:S(2)}, u32[]{:S(2)}) collective-permute-start(bf16[128,768]{1,0:T(8,128)(2,1)S(1)} %get-tuple-element.17), channel_id=1, source_target_pairs={{0,128},{128,256},{256,384},{384,0},{1,129},{129,257},{257,385},{3... | collective-permute-start | bytes 589832 | tf_op jit(solution)/shard_map/ppermute | solution.py:119
  92.1 5.5 %collective-permute-start.11 = (bf16[128,768]{1,0:T(8,128)(2,1)S(1)}, bf16[128,768]{1,0:T(8,128)(2,1)S(1)}, u32[]{:S(2)}, u32[]{:S(2)}) collective-permute-start(bf16[128,768]{1,0:T(8,128)(2,1)S(1)} %add_convert_fusion.1), channel_id=1, source_target_pairs={{0,384},{128,0},{256,128},{384,256},{1,385},{129,1},{257,129},{385... | collective-permute-start | bytes 589832 | tf_op jit(solution)/shard_map/ppermute | solution.py:122
  97.6 3.7 %collective-permute-done.5 = bf16[128,768]{1,0:T(8,128)(2,1)S(1)} collective-permute-done((bf16[128,768]{1,0:T(8,128)(2,1)S(1)}, bf16[128,768]{1,0:T(8,128)(2,1)S(1)}, u32[]{:S(2)}, u32[]{:S(2)}) %collective-permute-start.5) | collective-permute-done | bytes 196640 | tf_op jit(solution)/shard_map/ppermute | solution.py:119
  101.3 1.9 %collective-permute-start.6 = (bf16[128,768]{1,0:T(8,128)(2,1)S(1)}, bf16[128,768]{1,0:T(8,128)(2,1)S(1)}, u32[]{:S(2)}, u32[]{:S(2)}) collective-permute-start(bf16[128,768]{1,0:T(8,128)(2,1)S(1)} %add_convert_fusion.3), channel_id=1, source_target_pairs={{0,128},{128,256},{256,384},{384,0},{1,129},{129,257},{257,385},{3... | collective-permute-start | bytes 589832 | tf_op jit(solution)/shard_map/ppermute | solution.py:119
  103.3 0.1 fusion.12
  103.4 8.2 %collective-permute-done.6 = bf16[128,768]{1,0:T(8,128)(2,1)S(1)} collective-permute-done((bf16[128,768]{1,0:T(8,128)(2,1)S(1)}, bf16[128,768]{1,0:T(8,128)(2,1)S(1)}, u32[]{:S(2)}, u32[]{:S(2)}) %collective-permute-start.6) | collective-permute-done | bytes 196640 | tf_op jit(solution)/shard_map/ppermute | solution.py:119
  111.6 0.1 fusion.11
  111.7 0.4 copy.24
  112.1 27.3 %all_to_all.26 = bf16[128,2,768]{2,1,0:T(2,128)(2,1)S(1)} all-to-all(bf16[128,2,768]{2,1,0:T(2,128)(2,1)S(1)} %copy.24), channel_id=1, replica_groups=mesh['dp'=4,'yl'=2,'x'=4,'z'=8,'core'=2] {'yl','x','z','core'}, dimensions={0} | all-to-all | bytes 786432 | tf_op jit(solution)/shard_map/all_to_all | solution.py:99
  139.4 0.5 fusion.25
  139.9 0.2 convolution_bitcast_fusion.1
  140.2 0.3 multiply_reduce_fusion.1
  140.5 0.2 add_convert_fusion.4
  140.7 0.2 convolution_bitcast_fusion
  140.9 0.2 copy.27
  141.1 12.6 %all_to_all.27 = f32[16,48,128]{2,1,0:T(8,128)S(1)} all-to-all(f32[16,48,128]{2,1,0:T(8,128)S(1)} %bitcast.74), channel_id=1, replica_groups=mesh['dp'=4,'yl'=2,'x'=4,'z'=8,'core'=2] {'yl','x','core'}, dimensions={0} | all-to-all | bytes 786432 | tf_op jit(solution)/shard_map/all_to_all | solution.py:99
  153.8 16.5 %all_to_all.28 = bf16[32,48,128]{2,1,0:T(8,128)(2,1)S(1)} all-to-all(bf16[32,48,128]{2,1,0:T(8,128)(2,1)S(1)} %broadcast_in_dim.9), channel_id=1, replica_groups=mesh['dp'=4,'yl'=2,'x'=4,'z'=8,'core'=2] {'dp','z'}, dimensions={0} | all-to-all | bytes 786432 | tf_op jit(solution)/shard_map/all_to_all | solution.py:99
  170.3 0.8 broadcast_in_dim.10
  171.1 7.8 %all-to-all-start.4 = ((f32[16,48,128]{2,1,0:T(8,128)}), f32[16,48,128]{2,1,0:T(8,128)S(1)}, u32[]{:S(2)}, u32[]{:S(2)}) async-start(f32[16,48,128]{2,1,0:T(8,128)} %broadcast_in_dim.10), calls=%async_computation.4 | async-start | bytes 786432 | tf_op jit(solution)/shard_map/all_to_all | solution.py:99
  178.9 2.4 %shard_map.80 = bf16[768,768]{1,0:T(8,128)(2,1)} custom-call(bf16[128,768]{1,0:T(8,128)(2,1)S(1)} %get-tuple-element.23.refs_0_, bf16[128,768]{1,0:T(8,128)(2,1)S(1)} %get-tuple-element.24.refs_1_, bf16[128,768]{1,0:T(8,128)(2,1)S(1)} %get-tuple-element.25.refs_2_, bf16[128,768]{1,0:T(8,128)(2,1)S(1)} %get-tuple-element.26.refs_3_, ...), custom_call_target="tpu_custom_call" | custom-call | flops 603979776 | bytes 1179648 | tf_op jit(solution)/shard_map/pallas_call | solution.py:88
  181.4 0.2 fusion.17
  181.6 1.0 fusion.1
  182.6 4.7 %all-to-all-done.4 = f32[16,48,128]{2,1,0:T(8,128)S(1)} async-done(((f32[16,48,128]{2,1,0:T(8,128)}), f32[16,48,128]{2,1,0:T(8,128)S(1)}, u32[]{:S(2)}, u32[]{:S(2)}) %all-to-all-start.4) | async-done | bytes 393248 | tf_op jit(solution)/shard_map/all_to_all | solution.py:99
  187.3 0.7 copy.44
  (25 shorter events, 0.4 us)
Async XLA Ops:
  0.6 1.0 copy-start
  0.6 2.7 %copy-start.4 = (bf16[1,196,768]{2,1,0:T(8,128)(2,1)S(1)}, bf16[1,196,768]{2,1,0:T(8,128)(2,1)}, u32[]{:S(2)}) copy-start(bf16[1,196,768]{2,1,0:T(8,128)(2,1)} %param.9) | copy-start | bytes 903172
  36.1 37.5 %copy-start.1 = (bf16[1,768,768]{2,1,0:T(8,128)(2,1)S(1)}, bf16[1,768,768]{2,1,0:T(8,128)(2,1)}, u32[]{:S(2)}) copy-start(bf16[1,768,768]{2,1,0:T(8,128)(2,1)} %param.7) | copy-start | bytes 3538948
  36.1 37.5 %copy-start.2 = (bf16[1,768,768]{2,1,0:T(8,128)(2,1)S(1)}, bf16[1,768,768]{2,1,0:T(8,128)(2,1)}, u32[]{:S(2)}) copy-start(bf16[1,768,768]{2,1,0:T(8,128)(2,1)} %param.8) | copy-start | bytes 3538948
  36.7 12.1 %collective-permute-start.2 = (bf16[128,768]{1,0:T(8,128)(2,1)S(1)}, bf16[128,768]{1,0:T(8,128)(2,1)S(1)}, u32[]{:S(2)}, u32[]{:S(2)}) collective-permute-start(bf16[128,768]{1,0:T(8,128)(2,1)S(1)} %bitcast.70), channel_id=1, source_target_pairs={{0,128},{128,256},{256,384},{384,0},{1,129},{129,257},{257,385},{3... | collective-permute-start | bytes 589832 | tf_op jit(solution)/shard_map/ppermute | solution.py:119
  41.1 13.7 %collective-permute-start.1 = (bf16[128,768]{1,0:T(8,128)(2,1)S(1)}, bf16[128,768]{1,0:T(8,128)(2,1)S(1)}, u32[]{:S(2)}, u32[]{:S(2)}) collective-permute-start(bf16[128,768]{1,0:T(8,128)(2,1)S(1)} %bitcast.66), channel_id=1, source_target_pairs={{0,384},{128,0},{256,128},{384,256},{1,385},{129,1},{257,129},{385... | collective-permute-start | bytes 589832 | tf_op jit(solution)/shard_map/ppermute | solution.py:122
  48.8 16.3 %collective-permute-start.3 = (bf16[128,768]{1,0:T(8,128)(2,1)S(1)}, bf16[128,768]{1,0:T(8,128)(2,1)S(1)}, u32[]{:S(2)}, u32[]{:S(2)}) collective-permute-start(bf16[128,768]{1,0:T(8,128)(2,1)S(1)} %collective-permute-done.2.rows_ref), channel_id=1, source_target_pairs={{0,128},{128,256},{256,384},{384,0},{1,129},{129,257},{257,385},{3... | collective-permute-start | bytes 589832 | tf_op jit(solution)/shard_map/ppermute | solution.py:119
  54.8 18.8 %collective-permute-start.4 = (bf16[128,768]{1,0:T(8,128)(2,1)S(1)}, bf16[128,768]{1,0:T(8,128)(2,1)S(1)}, u32[]{:S(2)}, u32[]{:S(2)}) collective-permute-start(bf16[128,768]{1,0:T(8,128)(2,1)S(1)} %collective-permute-done.1.grads_ref.refs_5_), channel_id=1, source_target_pairs={{0,384},{128,0},{256,128},{384,256},{1,385},{129,1},{257,129},{385... | collective-permute-start | bytes 589832 | tf_op jit(solution)/shard_map/ppermute | solution.py:122
  58.9 21.3 %collective-permute-start = (bf16[128,768]{1,0:T(8,128)(2,1)S(1)}, bf16[128,768]{1,0:T(8,128)(2,1)S(1)}, u32[]{:S(2)}, u32[]{:S(2)}) collective-permute-start(bf16[128,768]{1,0:T(8,128)(2,1)S(1)} %bitcast.71), channel_id=1, source_target_pairs={{0,384},{128,0},{256,128},{384,256},{1,385},{129,1},{257,129},{385... | collective-permute-start | bytes 589832 | tf_op jit(solution)/shard_map/ppermute | solution.py:122
  61.8 22.0 %collective-permute-start.7 = (bf16[128,768]{1,0:T(8,128)(2,1)S(1)}, bf16[128,768]{1,0:T(8,128)(2,1)S(1)}, u32[]{:S(2)}, u32[]{:S(2)}) collective-permute-start(bf16[128,768]{1,0:T(8,128)(2,1)S(1)} %bitcast.67), channel_id=1, source_target_pairs={{0,128},{128,256},{256,384},{384,0},{1,129},{129,257},{257,385},{3... | collective-permute-start | bytes 589832 | tf_op jit(solution)/shard_map/ppermute | solution.py:119
  74.9 17.2 %collective-permute-start.10 = (bf16[128,768]{1,0:T(8,128)(2,1)S(1)}, bf16[128,768]{1,0:T(8,128)(2,1)S(1)}, u32[]{:S(2)}, u32[]{:S(2)}) collective-permute-start(bf16[128,768]{1,0:T(8,128)(2,1)S(1)} %get-tuple-element.22), channel_id=1, source_target_pairs={{0,384},{128,0},{256,128},{384,256},{1,385},{129,1},{257,129},{385... | collective-permute-start | bytes 589832 | tf_op jit(solution)/shard_map/ppermute | solution.py:122
  81.4 21.8 %collective-permute-start.9 = (bf16[128,768]{1,0:T(8,128)(2,1)S(1)}, bf16[128,768]{1,0:T(8,128)(2,1)S(1)}, u32[]{:S(2)}, u32[]{:S(2)}) collective-permute-start(bf16[128,768]{1,0:T(8,128)(2,1)S(1)} %get-tuple-element.20), channel_id=1, source_target_pairs={{0,128},{128,256},{256,384},{384,0},{1,129},{129,257},{257,385},{3... | collective-permute-start | bytes 589832 | tf_op jit(solution)/shard_map/ppermute | solution.py:119
  85.2 18.2 %collective-permute-start.8 = (bf16[128,768]{1,0:T(8,128)(2,1)S(1)}, bf16[128,768]{1,0:T(8,128)(2,1)S(1)}, u32[]{:S(2)}, u32[]{:S(2)}) collective-permute-start(bf16[128,768]{1,0:T(8,128)(2,1)S(1)} %get-tuple-element.18), channel_id=1, source_target_pairs={{0,384},{128,0},{256,128},{384,256},{1,385},{129,1},{257,129},{385... | collective-permute-start | bytes 589832 | tf_op jit(solution)/shard_map/ppermute | solution.py:122
  90.1 11.2 %collective-permute-start.5 = (bf16[128,768]{1,0:T(8,128)(2,1)S(1)}, bf16[128,768]{1,0:T(8,128)(2,1)S(1)}, u32[]{:S(2)}, u32[]{:S(2)}) collective-permute-start(bf16[128,768]{1,0:T(8,128)(2,1)S(1)} %get-tuple-element.17), channel_id=1, source_target_pairs={{0,128},{128,256},{256,384},{384,0},{1,129},{129,257},{257,385},{3... | collective-permute-start | bytes 589832 | tf_op jit(solution)/shard_map/ppermute | solution.py:119
  92.1 11.2 %collective-permute-start.11 = (bf16[128,768]{1,0:T(8,128)(2,1)S(1)}, bf16[128,768]{1,0:T(8,128)(2,1)S(1)}, u32[]{:S(2)}, u32[]{:S(2)}) collective-permute-start(bf16[128,768]{1,0:T(8,128)(2,1)S(1)} %add_convert_fusion.1), channel_id=1, source_target_pairs={{0,384},{128,0},{256,128},{384,256},{1,385},{129,1},{257,129},{385... | collective-permute-start | bytes 589832 | tf_op jit(solution)/shard_map/ppermute | solution.py:122
  101.3 10.2 %collective-permute-start.6 = (bf16[128,768]{1,0:T(8,128)(2,1)S(1)}, bf16[128,768]{1,0:T(8,128)(2,1)S(1)}, u32[]{:S(2)}, u32[]{:S(2)}) collective-permute-start(bf16[128,768]{1,0:T(8,128)(2,1)S(1)} %add_convert_fusion.3), channel_id=1, source_target_pairs={{0,128},{128,256},{256,384},{384,0},{1,129},{129,257},{257,385},{3... | collective-permute-start | bytes 589832 | tf_op jit(solution)/shard_map/ppermute | solution.py:119
  171.1 16.2 %all-to-all-start.4 = ((f32[16,48,128]{2,1,0:T(8,128)}), f32[16,48,128]{2,1,0:T(8,128)S(1)}, u32[]{:S(2)}, u32[]{:S(2)}) async-start(f32[16,48,128]{2,1,0:T(8,128)} %broadcast_in_dim.10), calls=%async_computation.4 | async-start | bytes 786432 | tf_op jit(solution)/shard_map/all_to_all | solution.py:99
  178.9 2.7 %copy-start.3 = (bf16[768,128]{1,0:T(8,128)(2,1)S(1)}, bf16[768,128]{1,0:T(8,128)(2,1)}, u32[]{:S(2)}) copy-start(bf16[768,128]{1,0:T(8,128)(2,1)} %param.6) | copy-start | bytes 589828

commit v3 on v2

v3 whole, which is shorter than its diff:
```python
import math

import jax
import jax.numpy as jnp
from jax import lax
from jax.experimental import pallas as pl
from jax.experimental.pallas import tpu as pltpu
from jax.sharding import Mesh
from jax.sharding import PartitionSpec as P

GELU_SCALE = math.sqrt(2.0 / math.pi)
GELU_CUBIC = 0.044715
LOW = jnp.bfloat16
WIDE = jnp.float32
DP_SPLIT = {"gh": 2, "gl": 2}
EXPERT_SPLIT = {"yl": 2, "xh": 2, "xl": 2, "zh": 4, "zl": 2, "core": 2}
DP = tuple(DP_SPLIT)
EXPERT = tuple(EXPERT_SPLIT)
EVERY = DP + EXPERT
TEAM = ("xl", "core")
ROUTE = ("yl", "xh", "gh", "zh", "zl", "gl")
NEAR = ("yl", "xh", "xl", "zl", "core")
REST = ("gh", "gl", "zh")
VMEM_BYTES = 48 * 2**20


def wide_einsum(spec, left, right):
    return jnp.einsum(spec, left, right, preferred_element_type=WIDE)


def wide_dot(left, right, left_dim, right_dim):
    return lax.dot_general(
        left, right, (((left_dim,), (right_dim,)), ((), ())), preferred_element_type=WIDE
    )


def in_vmem(count):
    return [pl.BlockSpec(memory_space=pltpu.VMEM)] * count


def cost(flops, bytes_accessed):
    return pl.CostEstimate(flops=flops, bytes_accessed=bytes_accessed, transcendentals=0)


def expert_kernel(first_ref, second_ref, up_ref, down_ref, kept_ref, sent_ref, act_ref):
    up, down = up_ref[...], down_ref[...]
    rows = jnp.concatenate([first_ref[0], second_ref[0]])
    hidden_pre = wide_dot(rows, up, 1, 0)
    squared = hidden_pre * hidden_pre
    inner = jnp.tanh(GELU_SCALE * (hidden_pre + GELU_CUBIC * squared * hidden_pre))
    half = 0.5 * (1.0 + inner)
    activation = (hidden_pre * half).astype(LOW)
    act_ref[...] = activation
    outputs = wide_dot(activation, down, 1, 0)
    slope = half + 0.5 * hidden_pre * (1.0 - inner * inner) * (
        GELU_SCALE + 3.0 * GELU_SCALE * GELU_CUBIC * squared
    )
    grads = jnp.concatenate([first_ref[1], second_ref[1]])
    upstream = wide_dot(grads, down, 1, 1)
    hidden_grad = (upstream * slope).astype(LOW)
    input_grads = wide_dot(hidden_grad, up, 1, 1)
    count = kept_ref.shape[1]
    for route, result in enumerate((outputs, input_grads)):
        kept_ref[route] = result[:count].astype(kept_ref.dtype)
        sent_ref[route] = result[count:].astype(sent_ref.dtype)


def expert_rows(first, second, up, down):
    _, count, width = first.shape
    hidden = up.shape[1]
    return pl.pallas_call(
        expert_kernel,
        out_shape=(
            jax.ShapeDtypeStruct(first.shape, WIDE),
            jax.ShapeDtypeStruct(first.shape, LOW),
            jax.ShapeDtypeStruct((2 * count, hidden), LOW),
        ),
        in_specs=in_vmem(4),
        out_specs=tuple(in_vmem(3)),
        compiler_params=pltpu.CompilerParams(vmem_limit_bytes=VMEM_BYTES),
        cost_estimate=cost(16 * count * width * hidden, 4 * width * hidden + 28 * count * width),
    )(first, second, up, down)


def grad_kernel(near_act_ref, far_act_ref, *refs):
    *row_refs, grad_ref = refs
    grads = [ref[1] for ref in row_refs]
    total = wide_dot(near_act_ref[...], jnp.concatenate(grads[:2]), 0, 0)
    total = total + wide_dot(far_act_ref[...], jnp.concatenate(grads[2:]), 0, 0)
    grad_ref[...] = total.astype(LOW)


def outer_sum(near_act, far_act, *blocks):
    count, hidden = near_act.shape
    width = blocks[0].shape[2]
    return pl.pallas_call(
        grad_kernel,
        out_shape=jax.ShapeDtypeStruct((hidden, width), LOW),
        in_specs=in_vmem(6),
        out_specs=in_vmem(1)[0],
        compiler_params=pltpu.CompilerParams(vmem_limit_bytes=VMEM_BYTES),
        cost_estimate=cost(4 * count * width * hidden, 2 * hidden * width),
    )(near_act, far_act, *blocks)


def all_to_all(value, axes):
    return lax.all_to_all(value, axes, split_axis=0, concat_axis=0, tiled=True)


def sum_everywhere(term):
    near = lax.axis_size(NEAR)
    rest = lax.axis_size(REST)
    depth, width = term.shape
    part = jnp.sum(all_to_all(term.reshape(near, depth // near, width), NEAR), axis=0)
    part = jnp.sum(all_to_all(jnp.broadcast_to(part[None], (rest,) + part.shape), REST), axis=0)
    whole = all_to_all(jnp.broadcast_to(part[None], (near,) + part.shape), NEAR)
    return whole.reshape(depth, width)


def swap(value, axis):
    return lax.ppermute(value, axis, [(0, 1), (1, 0)])


def slab_place(slab, team):
    slabs = lax.axis_size(DP)
    return (slab % slabs) * slabs + team % slabs


def move_weights(value, way):
    slabs = lax.axis_size(DP)
    moves = []
    for slab in range(slabs):
        for team in range(slabs):
            if (team - slab) % slabs == 2:
                moves.append((slab_place(slab, team), slab_place(slab + way, slab + way)))
            elif team != slab:
                moves.append((slab_place(slab, team), slab_place(team, slab)))
    return lax.ppermute(value, DP + TEAM, moves)


def finish_move(value, once, way):
    slabs = lax.axis_size(DP)
    moves = [(slab_place(k, k), slab_place(k + way, k - way)) for k in range(slabs)]
    twice = lax.ppermute(once, DP + TEAM, moves)
    offset = (lax.axis_index(TEAM) - lax.axis_index(DP)) % slabs
    return jnp.where(offset == 0, value, jnp.where(offset == 2, twice, once))


def move_back(value):
    slabs = lax.axis_size(DP)
    swaps = [(a * slabs + b, b * slabs + a) for a in range(slabs) for b in range(slabs)]
    return lax.ppermute(value, DP + TEAM, swaps)


def shards(tokens, router, up_weight, down_weight, cotangent):
    tokens, cotangent = tokens[0], cotangent[0]
    up_once = move_weights(up_weight[0], 1)
    down_once = move_weights(down_weight[0], -1)

    logits = wide_einsum("md,ds->ms", tokens, router)
    dispatch = jax.nn.softmax(logits, axis=0)
    combine = jax.nn.softmax(logits, axis=1)
    dispatch_low = dispatch.astype(LOW)
    combine_low = combine.astype(LOW)
    slot_inputs = wide_einsum("ms,md->sd", dispatch_low, tokens).astype(LOW)
    slot_cotangent = wide_einsum("ms,md->sd", combine_low, cotangent).astype(LOW)

    sent = jnp.stack([slot_inputs, slot_cotangent], axis=1)
    own, up_once, down_once = lax.optimization_barrier((all_to_all(sent, ROUTE), up_once, down_once))
    own = jnp.swapaxes(own, 0, 1)
    beside = swap(own, "core")
    across = swap(own, "xl")
    corner = swap(across, "core")

    up = finish_move(up_weight[0], up_once, 1)
    down = finish_move(down_weight[0], down_once, -1)
    far_kept, far_sent, far_act = expert_rows(across, corner, up, down)
    far_back = swap(far_sent, "core")
    own_kept, own_sent, own_act = expert_rows(own, beside, up, down)
    own_back = swap(own_sent, "core")
    across_back = swap((far_kept + far_back.astype(WIDE)).astype(LOW), "xl")
    grad_down = move_back(outer_sum(own_act, far_act, own, beside, across, corner))
    summed = (own_kept + own_back.astype(WIDE) + across_back.astype(WIDE)).astype(LOW)

    back = all_to_all(jnp.swapaxes(summed, 0, 1), ROUTE)
    slot_outputs, input_grads = back[:, 0], back[:, 1]

    combine_grad = wide_einsum("md,sd->ms", cotangent, slot_outputs)
    dispatch_grad = wide_einsum("md,sd->ms", tokens, input_grads)
    logit_grad = combine * (combine_grad - jnp.sum(combine * combine_grad, axis=1, keepdims=True))
    logit_grad = logit_grad + dispatch * (
        dispatch_grad - jnp.sum(dispatch * dispatch_grad, axis=0, keepdims=True)
    )
    logit_low = logit_grad.astype(LOW)
    grad_router = sum_everywhere(wide_einsum("md,ms->ds", tokens, logit_low))

    grad_tokens = wide_einsum("ms,sd->md", dispatch_low, input_grads)
    grad_tokens = grad_tokens + wide_einsum("ms,ds->md", logit_low, router)
    return (grad_tokens.astype(LOW)[None], grad_router, grad_down[None])


def solution(mesh):
    sizes = tuple(DP_SPLIT.values()) + tuple(EXPERT_SPLIT.values())
    images = P(EVERY, None, None)
    return jax.shard_map(
        shards,
        mesh=Mesh(mesh.devices.reshape(sizes), EVERY),
        in_specs=(images, P(), P(EXPERT, None, DP), P(EXPERT, DP, None), images),
        out_specs=(images, P(), P(EXPERT, DP, None)),
        check_vma=False,
    )
```

time: 189 us -> 283 us (1.50)
  blocking collectives: 88.3 us -> 149 us
  starting transfers between devices: 49.6 us -> 90.2 us
  waiting for transfers between devices: 32.3 us -> 20.8 us
  other arithmetic: 0.75 us -> 5.17 us
  Pallas kernels: 7.52 us -> 4 us
    all_to_all x4 -> x3, blocking collectives: 88.3 us -> 149 us  [all_to_all(): return lax.all_to_all(value, axes, split_axis=0, concat_axis=0, tiled=True)]
    ppermute x12 -> x11, starting transfers between devices: 41.7 us -> 62.4 us  [the longest x6 48.6 us: swap(): return lax.ppermute(value, axis, [(0, 1), (1, 0)])]
    all_to_all x1 -> x2, starting transfers between devices: 7.83 us -> 27.8 us  [all_to_all(): return lax.all_to_all(value, axes, split_axis=0, concat_axis=0, tiled=True)]
    ppermute x12 -> x11, waiting for transfers between devices: 27.7 us -> 9.04 us  [the longest x6 9.03 us: swap(): return lax.ppermute(value, axis, [(0, 1), (1, 0)])]
    all_to_all x1 -> x2, waiting for transfers between devices: 4.68 us -> 11.8 us  [all_to_all(): return lax.all_to_all(value, axes, split_axis=0, concat_axis=0, tiled=True)]
    pallas_call x5 -> x3, Pallas kernels: 7.52 us -> 4 us  [the longest x2 3.2 us: expert_rows(): pl.pallas_call(expert_kernel, out_shape=(jax.ShapeDtypeStruct(first.shape...]
    select_n x0 -> x2, other arithmetic: none -> 2.92 us  [finish_move(): return jnp.where(offset == 0, value, jnp.where(offset == 2, twice, once))]
  transfers between devices with their start and end apart: 13 -> 13, of which waited for: 6 -> 3; matrix products, arithmetic and copies ran while one was open for 1% -> 4% of each run, Pallas kernels for 4% -> 1%
where the time goes in v3:
time: 283 us; the launch traced here: 282 us
  blocking collectives  149 us (53%)
  starting transfers between devices  90.2 us (32%)
  waiting for transfers between devices  20.8 us (7%)
  matrix products  6.35 us (2%)
  local copies, waits for them, and re-layouts  5.91 us (2%)
  other arithmetic  5.17 us (2%)
  Pallas kernels  4 us (1%)
    all_to_all x3, blocking collectives, all_to_all(): return lax.all_to_all(value, axes, split_axis=0, concat_axis=0, tiled=True)  149 us
    ppermute x6, starting transfers between devices, swap(): return lax.ppermute(value, axis, [(0, 1), (1, 0)])  48.6 us
    all_to_all x2, starting transfers between devices, all_to_all(): return lax.all_to_all(value, axes, split_axis=0, concat_axis=0, tiled=True)  27.8 us
    all_to_all x2, waiting for transfers between devices, all_to_all(): return lax.all_to_all(value, axes, split_axis=0, concat_axis=0, tiled=True)  11.8 us
    ppermute x6, waiting for transfers between devices, swap(): return lax.ppermute(value, axis, [(0, 1), (1, 0)])  9.03 us
    ppermute x2, starting transfers between devices, move_weights(): return lax.ppermute(value, DP + TEAM, moves)  7.67 us
    dot_general x8, matrix products, wide_einsum(): return jnp.einsum(spec, left, right, preferred_element_type=WIDE)  6.35 us
  transfers between devices with their start and end apart: 13, of which 3 were waited for; matrix products, arithmetic and copies ran while one was open for 4% of the time, Pallas kernels for 1%

profile of v3, /device:TPU:1, one launch (start us, length us, event | category | flops | bytes accessed | tf_op | source)
XLA Modules:
  0.0 282.3 jit_solution(2286175589299863922)
XLA Ops:
  0.6 0.0 copy-start
  0.7 5.7 %collective-permute-start = (bf16[768,768]{1,0:T(8,128)(2,1)}, bf16[768,768]{1,0:T(8,128)(2,1)}, u32[]{:S(2)}, u32[]{:S(2)}) collective-permute-start(bf16[768,768]{1,0:T(8,128)(2,1)} %bitcast.60), channel_id=1, source_target_pairs={{1,128},{16,129},{17,384},{128,1},{144,257},{145,272},{256,401},{2... | collective-permute-start | bytes 3538952 | tf_op jit(solution)/shard_map/ppermute | solution.py:138
  6.4 1.9 collective-permute-start.1
  8.3 1.2 fusion.23
  9.6 0.2 fusion.13
  9.8 0.0 copy-start.9
  9.8 0.2 fusion.2
  10.1 0.3 fusion.3
  10.5 0.0 copy-start.5
  10.5 0.4 copy.19
  10.9 80.1 %all_to_all.25 = bf16[128,2,768]{2,1,0:T(2,128)(2,1)S(1)} all-to-all(bf16[128,2,768]{2,1,0:T(2,128)(2,1)S(1)} %copy.19), channel_id=1, replica_groups=mesh['gh'=2,'gl'=2,'yl'=2,'xh'=2,'xl'=2,'zh'=4,'zl'=2,'core'=2] {'yl','x..., dimensions={0} | all-to-all | bytes 786432 | tf_op jit(solution)/shard_map/all_to_all | solution.py:107
  91.0 1.7 collective-permute-start.3
  92.7 1.7 collective-permute-start.4
  94.4 5.4 %collective-permute-start.6 = (bf16[2,128,768]{2,1,0:T(8,128)(2,1)S(1)}, bf16[2,128,768]{2,1,0:T(8,128)(2,1)S(1)}, u32[]{:S(2)}, u32[]{:S(2)}) collective-permute-start(bf16[2,128,768]{2,1,0:T(8,128)(2,1)S(1)} %bitcast.55), channel_id=1, source_target_pairs={{0,16},{16,0},{1,17},{17,1},{2,18},{18,2},{3,19},{19,3},{4,20},{20... | collective-permute-start | bytes 1179656 | tf_op jit(solution)/shard_map/ppermute | solution.py:121
  99.8 13.5 %collective-permute-start.2 = (bf16[2,128,768]{2,1,0:T(8,128)(2,1)S(1)}, bf16[2,128,768]{2,1,0:T(8,128)(2,1)S(1)}, u32[]{:S(2)}, u32[]{:S(2)}) collective-permute-start(bf16[2,128,768]{2,1,0:T(8,128)(2,1)S(1)} %bitcast.56), channel_id=1, source_target_pairs={{0,1},{1,0},{2,3},{3,2},{4,5},{5,4},{6,7},{7,6},{8,9},{9,8},{10,11... | collective-permute-start | bytes 1179656 | tf_op jit(solution)/shard_map/ppermute | solution.py:121
  113.3 7.5 %collective-permute-start.7 = (bf16[2,128,768]{2,1,0:T(8,128)(2,1)S(1)}, bf16[2,128,768]{2,1,0:T(8,128)(2,1)S(1)}, u32[]{:S(2)}, u32[]{:S(2)}) collective-permute-start(bf16[2,128,768]{2,1,0:T(8,128)(2,1)S(1)} %collective-permute-done.6.first_ref.refs_2_), channel_id=1, source_target_pairs={{0,1},{1,0},{2,3},{3,2},{4,5},{5,4},{6,7},{7,6},{8,9},{9,8},{10,11... | collective-permute-start | bytes 1179656 | tf_op jit(solution)/shard_map/ppermute | solution.py:121
  120.9 1.5 select_select_fusion.1.up_ref
  122.4 1.5 select_select_fusion.down_ref
  123.9 1.6 shard_map.77
  125.5 14.4 %collective-permute-start.8 = (bf16[2,128,768]{2,1,0:T(8,128)(2,1)S(1)}, bf16[2,128,768]{2,1,0:T(8,128)(2,1)S(1)}, u32[]{:S(2)}, u32[]{:S(2)}) collective-permute-start(bf16[2,128,768]{2,1,0:T(8,128)(2,1)S(1)} %get-tuple-element.18), channel_id=1, source_target_pairs={{0,1},{1,0},{2,3},{3,2},{4,5},{5,4},{6,7},{7,6},{8,9},{9,8},{10,11... | collective-permute-start | bytes 1179656 | tf_op jit(solution)/shard_map/ppermute | solution.py:121
  139.9 1.6 shard_map.76
  141.5 1.9 collective-permute-start.5
  143.4 0.1 add_convert_fusion.1
  143.5 5.9 %collective-permute-start.9 = (bf16[2,128,768]{2,1,0:T(8,128)(2,1)S(1)}, bf16[2,128,768]{2,1,0:T(8,128)(2,1)S(1)}, u32[]{:S(2)}, u32[]{:S(2)}) collective-permute-start(bf16[2,128,768]{2,1,0:T(8,128)(2,1)S(1)} %add_convert_fusion.1), channel_id=1, source_target_pairs={{0,16},{16,0},{1,17},{17,1},{2,18},{18,2},{3,19},{19,3},{4,20},{20... | collective-permute-start | bytes 1179656 | tf_op jit(solution)/shard_map/ppermute | solution.py:121
  149.4 9.0 %collective-permute-done.9 = bf16[2,128,768]{2,1,0:T(8,128)(2,1)S(1)} collective-permute-done((bf16[2,128,768]{2,1,0:T(8,128)(2,1)S(1)}, bf16[2,128,768]{2,1,0:T(8,128)(2,1)S(1)}, u32[]{:S(2)}, u32[]{:S(2)}) %collective-permute-start.9) | collective-permute-done | bytes 393248 | tf_op jit(solution)/shard_map/ppermute | solution.py:121
  158.4 0.1 fusion.4
  158.6 0.4 copy.21
  159.0 26.0 %all_to_all.26 = bf16[128,2,768]{2,1,0:T(2,128)(2,1)S(1)} all-to-all(bf16[128,2,768]{2,1,0:T(2,128)(2,1)S(1)} %copy.21), channel_id=1, replica_groups=mesh['gh'=2,'gl'=2,'yl'=2,'xh'=2,'xl'=2,'zh'=4,'zl'=2,'core'=2] {'yl','x..., dimensions={0} | all-to-all | bytes 786432 | tf_op jit(solution)/shard_map/all_to_all | solution.py:107
  184.9 0.5 fusion.24
  185.5 0.2 convolution_bitcast_fusion.1
  185.8 0.3 multiply_reduce_fusion.1
  186.1 0.8 add_convert_fusion.2
  186.9 1.0 convolution_bitcast_fusion
  187.9 0.9 copy.24
  188.9 8.2 %all-to-all-start.2 = ((f32[32,24,128]{2,1,0:T(8,128)}), f32[32,24,128]{2,1,0:T(8,128)}, u32[]{:S(2)}, u32[]{:S(2)}) async-start(f32[32,24,128]{2,1,0:T(8,128)} %bitcast.14), calls=%async_computation.2 | async-start | bytes 786432 | tf_op jit(solution)/shard_map/all_to_all | solution.py:107
  197.1 1.0 copy-done.2
  198.1 0.8 shard_map.78
  198.9 2.7 collective-permute-start.10
  201.6 5.1 %all-to-all-done.2 = f32[32,24,128]{2,1,0:T(8,128)} async-done(((f32[32,24,128]{2,1,0:T(8,128)}), f32[32,24,128]{2,1,0:T(8,128)}, u32[]{:S(2)}, u32[]{:S(2)}) %all-to-all-start.2) | async-done | bytes 393248 | tf_op jit(solution)/shard_map/all_to_all | solution.py:107
  206.7 1.0 reduce_sum.58
  207.8 42.7 %all_to_all.27 = f32[16,24,128]{2,1,0:T(8,128)S(1)} all-to-all(f32[16,24,128]{2,1,0:T(8,128)S(1)} %broadcast_in_dim.9), channel_id=1, replica_groups=mesh['gh'=2,'gl'=2,'yl'=2,'xh'=2,'xl'=2,'zh'=4,'zl'=2,'core'=2] {'gh','g..., dimensions={0} | all-to-all | bytes 393216 | tf_op jit(solution)/shard_map/all_to_all | solution.py:107
  250.6 0.8 broadcast_in_dim.10
  251.3 19.6 %all-to-all-start.4 = ((f32[32,24,128]{2,1,0:T(8,128)}), f32[32,24,128]{2,1,0:T(8,128)S(1)}, u32[]{:S(2)}, u32[]{:S(2)}) async-start(f32[32,24,128]{2,1,0:T(8,128)} %broadcast_in_dim.10), calls=%async_computation.4 | async-start | bytes 786432 | tf_op jit(solution)/shard_map/all_to_all | solution.py:107
  270.9 0.9 fusion.16
  271.8 2.0 fusion.1
  273.8 6.7 %all-to-all-done.4 = f32[32,24,128]{2,1,0:T(8,128)S(1)} async-done(((f32[32,24,128]{2,1,0:T(8,128)}), f32[32,24,128]{2,1,0:T(8,128)S(1)}, u32[]{:S(2)}, u32[]{:S(2)}) %all-to-all-start.4) | async-done | bytes 393248 | tf_op jit(solution)/shard_map/all_to_all | solution.py:107
  280.5 0.7 copy.38
  281.3 1.0 copy.39
  (30 shorter events, 0.2 us)
Async XLA Ops:
  0.6 7.7 %copy-start = (bf16[1,196,768]{2,1,0:T(8,128)(2,1)S(1)}, bf16[1,196,768]{2,1,0:T(8,128)(2,1)}, u32[]{:S(2)}) copy-start(bf16[1,196,768]{2,1,0:T(8,128)(2,1)} %param.5) | copy-start | bytes 903172
  0.6 9.4 %copy-start.7 = (bf16[1,196,768]{2,1,0:T(8,128)(2,1)S(1)}, bf16[1,196,768]{2,1,0:T(8,128)(2,1)}, u32[]{:S(2)}) copy-start(bf16[1,196,768]{2,1,0:T(8,128)(2,1)} %param.9) | copy-start | bytes 903172
  0.7 90.3 %collective-permute-start = (bf16[768,768]{1,0:T(8,128)(2,1)}, bf16[768,768]{1,0:T(8,128)(2,1)}, u32[]{:S(2)}, u32[]{:S(2)}) collective-permute-start(bf16[768,768]{1,0:T(8,128)(2,1)} %bitcast.60), channel_id=1, source_target_pairs={{1,128},{16,129},{17,384},{128,1},{144,257},{145,272},{256,401},{2... | collective-permute-start | bytes 3538952 | tf_op jit(solution)/shard_map/ppermute | solution.py:138
  6.4 84.6 %collective-permute-start.1 = (bf16[768,768]{1,0:T(8,128)(2,1)}, bf16[768,768]{1,0:T(8,128)(2,1)}, u32[]{:S(2)}, u32[]{:S(2)}) collective-permute-start(bf16[768,768]{1,0:T(8,128)(2,1)} %bitcast.61), channel_id=1, source_target_pairs={{1,128},{16,401},{17,384},{128,1},{144,257},{145,0},{256,129},{257... | collective-permute-start | bytes 3538952 | tf_op jit(solution)/shard_map/ppermute | solution.py:138
  9.6 176.5 %copy-start.8 = (f32[128]{0:T(128)}, f32[128]{0:T(128)S(1)}, u32[]{:S(2)}) copy-start(f32[128]{0:T(128)S(1)} %get-tuple-element.25) | copy-start | bytes 1540
  9.8 176.3 %copy-start.9 = (f32[128]{0:T(128)}, f32[128]{0:T(128)S(1)}, u32[]{:S(2)}) copy-start(f32[128]{0:T(128)S(1)} %get-tuple-element.23) | copy-start | bytes 1540
  10.5 110.4 %copy-start.5 = (bf16[1,768,768]{2,1,0:T(8,128)(2,1)S(1)}, bf16[1,768,768]{2,1,0:T(8,128)(2,1)}, u32[]{:S(2)}) copy-start(bf16[1,768,768]{2,1,0:T(8,128)(2,1)} %param.7) | copy-start | bytes 3538948
  91.0 29.9 %collective-permute-start.3 = (bf16[768,768]{1,0:T(8,128)(2,1)}, bf16[768,768]{1,0:T(8,128)(2,1)}, u32[]{:S(2)}, u32[]{:S(2)}) collective-permute-start(bf16[768,768]{1,0:T(8,128)(2,1)} %collective-permute-done), channel_id=1, source_target_pairs={{0,145},{129,256},{272,385},{401,16},{2,147},{131,258},{274,387},{... | collective-permute-start | bytes 3538952 | tf_op jit(solution)/shard_map/ppermute | solution.py:144
  92.7 29.7 %collective-permute-start.4 = (bf16[768,768]{1,0:T(8,128)(2,1)}, bf16[768,768]{1,0:T(8,128)(2,1)}, u32[]{:S(2)}, u32[]{:S(2)}) collective-permute-start(bf16[768,768]{1,0:T(8,128)(2,1)} %collective-permute-done.1), channel_id=1, source_target_pairs={{0,385},{129,16},{272,145},{401,256},{2,387},{131,18},{274,147},{4... | collective-permute-start | bytes 3538952 | tf_op jit(solution)/shard_map/ppermute | solution.py:144
  94.4 18.9 %collective-permute-start.6 = (bf16[2,128,768]{2,1,0:T(8,128)(2,1)S(1)}, bf16[2,128,768]{2,1,0:T(8,128)(2,1)S(1)}, u32[]{:S(2)}, u32[]{:S(2)}) collective-permute-start(bf16[2,128,768]{2,1,0:T(8,128)(2,1)S(1)} %bitcast.55), channel_id=1, source_target_pairs={{0,16},{16,0},{1,17},{17,1},{2,18},{18,2},{3,19},{19,3},{4,20},{20... | collective-permute-start | bytes 1179656 | tf_op jit(solution)/shard_map/ppermute | solution.py:121
  99.8 22.6 %copy-start.6 = (bf16[1,768,768]{2,1,0:T(8,128)(2,1)S(1)}, bf16[1,768,768]{2,1,0:T(8,128)(2,1)}, u32[]{:S(2)}) copy-start(bf16[1,768,768]{2,1,0:T(8,128)(2,1)} %param.8) | copy-start | bytes 3538948
  99.8 40.1 %collective-permute-start.2 = (bf16[2,128,768]{2,1,0:T(8,128)(2,1)S(1)}, bf16[2,128,768]{2,1,0:T(8,128)(2,1)S(1)}, u32[]{:S(2)}, u32[]{:S(2)}) collective-permute-start(bf16[2,128,768]{2,1,0:T(8,128)(2,1)S(1)} %bitcast.56), channel_id=1, source_target_pairs={{0,1},{1,0},{2,3},{3,2},{4,5},{5,4},{6,7},{7,6},{8,9},{9,8},{10,11... | collective-permute-start | bytes 1179656 | tf_op jit(solution)/shard_map/ppermute | solution.py:121
  113.3 10.5 %collective-permute-start.7 = (bf16[2,128,768]{2,1,0:T(8,128)(2,1)S(1)}, bf16[2,128,768]{2,1,0:T(8,128)(2,1)S(1)}, u32[]{:S(2)}, u32[]{:S(2)}) collective-permute-start(bf16[2,128,768]{2,1,0:T(8,128)(2,1)S(1)} %collective-permute-done.6.first_ref.refs_2_), channel_id=1, source_target_pairs={{0,1},{1,0},{2,3},{3,2},{4,5},{5,4},{6,7},{7,6},{8,9},{9,8},{10,11... | collective-permute-start | bytes 1179656 | tf_op jit(solution)/shard_map/ppermute | solution.py:121
  125.5 18.0 %collective-permute-start.8 = (bf16[2,128,768]{2,1,0:T(8,128)(2,1)S(1)}, bf16[2,128,768]{2,1,0:T(8,128)(2,1)S(1)}, u32[]{:S(2)}, u32[]{:S(2)}) collective-permute-start(bf16[2,128,768]{2,1,0:T(8,128)(2,1)S(1)} %get-tuple-element.18), channel_id=1, source_target_pairs={{0,1},{1,0},{2,3},{3,2},{4,5},{5,4},{6,7},{7,6},{8,9},{9,8},{10,11... | collective-permute-start | bytes 1179656 | tf_op jit(solution)/shard_map/ppermute | solution.py:121
  141.5 17.1 %copy-start.1 = (bf16[256,768]{1,0:T(8,128)(2,1)}, bf16[256,768]{1,0:T(8,128)(2,1)S(1)}, u32[]{:S(2)}) copy-start(bf16[256,768]{1,0:T(8,128)(2,1)S(1)} %get-tuple-element.19.near_act_ref) | copy-start | bytes 1179652
  141.5 7.9 %collective-permute-start.5 = (bf16[2,128,768]{2,1,0:T(8,128)(2,1)S(1)}, bf16[2,128,768]{2,1,0:T(8,128)(2,1)S(1)}, u32[]{:S(2)}, u32[]{:S(2)}) collective-permute-start(bf16[2,128,768]{2,1,0:T(8,128)(2,1)S(1)} %get-tuple-element.16), channel_id=1, source_target_pairs={{0,1},{1,0},{2,3},{3,2},{4,5},{5,4},{6,7},{7,6},{8,9},{9,8},{10,11... | collective-permute-start | bytes 1179656 | tf_op jit(solution)/shard_map/ppermute | solution.py:121
  143.5 14.9 %collective-permute-start.9 = (bf16[2,128,768]{2,1,0:T(8,128)(2,1)S(1)}, bf16[2,128,768]{2,1,0:T(8,128)(2,1)S(1)}, u32[]{:S(2)}, u32[]{:S(2)}) collective-permute-start(bf16[2,128,768]{2,1,0:T(8,128)(2,1)S(1)} %add_convert_fusion.1), channel_id=1, source_target_pairs={{0,16},{16,0},{1,17},{17,1},{2,18},{18,2},{3,19},{19,3},{4,20},{20... | collective-permute-start | bytes 1179656 | tf_op jit(solution)/shard_map/ppermute | solution.py:121
  185.5 1.4 copy-start.3
  188.9 17.9 %all-to-all-start.2 = ((f32[32,24,128]{2,1,0:T(8,128)}), f32[32,24,128]{2,1,0:T(8,128)}, u32[]{:S(2)}, u32[]{:S(2)}) async-start(f32[32,24,128]{2,1,0:T(8,128)} %bitcast.14), calls=%async_computation.2 | async-start | bytes 786432 | tf_op jit(solution)/shard_map/all_to_all | solution.py:107
  197.1 1.0 copy-start.2
  198.9 72.0 %copy-start.4 = (bf16[128,1,768]{2,1,0:T(2,128)(2,1)S(1)}, bf16[128,1,768]{2,1,0:T(2,128)(2,1)}, u32[]{:S(2)}) copy-start(bf16[128,1,768]{2,1,0:T(2,128)(2,1)} %copy-done.3) | copy-start | bytes 589828
  198.9 72.0 %collective-permute-start.10 = (bf16[768,768]{1,0:T(8,128)(2,1)S(1)}, bf16[768,768]{1,0:T(8,128)(2,1)S(1)}, u32[]{:S(2)}, u32[]{:S(2)}) collective-permute-start(bf16[768,768]{1,0:T(8,128)(2,1)S(1)} %shard_map.78), channel_id=1, source_target_pairs={{0,0},{1,128},{16,256},{17,384},{128,1},{129,129},{144,257},{145,3... | collective-permute-start | bytes 3538952 | tf_op jit(solution)/shard_map/ppermute | solution.py:152
  251.3 29.2 %all-to-all-start.4 = ((f32[32,24,128]{2,1,0:T(8,128)}), f32[32,24,128]{2,1,0:T(8,128)S(1)}, u32[]{:S(2)}, u32[]{:S(2)}) async-start(f32[32,24,128]{2,1,0:T(8,128)} %broadcast_in_dim.10), calls=%async_computation.4 | async-start | bytes 786432 | tf_op jit(solution)/shard_map/all_to_all | solution.py:107

commit v4 on v3

v4 whole, which is shorter than its diff:
```python
import functools
import math

import jax
import jax.numpy as jnp
from jax import lax
from jax.experimental import pallas as pl
from jax.experimental.pallas import tpu as pltpu
from jax.sharding import Mesh
from jax.sharding import PartitionSpec as P

GELU_SCALE = math.sqrt(2.0 / math.pi)
GELU_CUBIC = 0.044715
LOW = jnp.bfloat16
WIDE = jnp.float32
DP_SPLIT = {"gh": 2, "gl": 2}
EXPERT_SPLIT = {"yl": 2, "x": 4, "zh": 4, "zl": 2, "core": 2}
DP = tuple(DP_SPLIT)
EXPERT = tuple(EXPERT_SPLIT)
EVERY = DP + EXPERT
TEAM = ("yl", "core")
ROUTE = ("gl", "x", "zh", "zl", "gh")
NEAR = ("yl", "x", "zl", "core")
REST = ("gh", "gl", "zh")
VMEM_BYTES = 48 * 2**20


def wide_einsum(spec, left, right):
    return jnp.einsum(spec, left, right, preferred_element_type=WIDE)


def wide_dot(left, right, left_dim, right_dim):
    return lax.dot_general(
        left, right, (((left_dim,), (right_dim,)), ((), ())), preferred_element_type=WIDE
    )


def in_vmem(count):
    return [pl.BlockSpec(memory_space=pltpu.VMEM)] * count


def cost(flops, bytes_accessed):
    return pl.CostEstimate(flops=flops, bytes_accessed=bytes_accessed, transcendentals=0)


def hidden_kernel(*refs):
    *row_refs, up_ref, act_ref, slope_ref, grad_ref = refs
    hidden_pre = wide_dot(jnp.concatenate([ref[0] for ref in row_refs]), up_ref[...], 1, 0)
    squared = hidden_pre * hidden_pre
    inner = jnp.tanh(GELU_SCALE * (hidden_pre + GELU_CUBIC * squared * hidden_pre))
    half = 0.5 * (1.0 + inner)
    activation = (hidden_pre * half).astype(LOW)
    act_ref[...] = activation
    slope_ref[...] = half + 0.5 * hidden_pre * (1.0 - inner * inner) * (
        GELU_SCALE + 3.0 * GELU_SCALE * GELU_CUBIC * squared
    )
    grads = jnp.concatenate([ref[1] for ref in row_refs])
    grad_ref[...] = wide_dot(activation, grads, 0, 0).astype(LOW)


def hidden_rows(blocks, up):
    _, count, width = blocks[0].shape
    count *= len(blocks)
    hidden = up.shape[1]
    return pl.pallas_call(
        hidden_kernel,
        out_shape=(
            jax.ShapeDtypeStruct((count, hidden), LOW),
            jax.ShapeDtypeStruct((count, hidden), WIDE),
            jax.ShapeDtypeStruct((hidden, width), LOW),
        ),
        in_specs=in_vmem(len(blocks) + 1),
        out_specs=tuple(in_vmem(3)),
        compiler_params=pltpu.CompilerParams(vmem_limit_bytes=VMEM_BYTES),
        cost_estimate=cost(4 * count * width * hidden, 4 * width * hidden + 10 * count * width),
    )(*blocks, up)


def result_kernel(half, first_ref, second_ref, act_ref, slope_ref, up_ref, down_ref, kept_ref, sent_ref):
    count = kept_ref.shape[1]
    here = pl.ds(half * 2 * count, 2 * count)
    down = down_ref[...]
    upstream = wide_dot(jnp.concatenate([first_ref[1], second_ref[1]]), down, 1, 1)
    hidden_grad = (upstream * slope_ref[here, :]).astype(LOW)
    outputs = wide_dot(act_ref[here, :], down, 1, 0)
    input_grads = wide_dot(hidden_grad, up_ref[...], 1, 1)
    for route, result in enumerate((outputs, input_grads)):
        kept_ref[route] = result[:count].astype(kept_ref.dtype)
        sent_ref[route] = result[count:].astype(sent_ref.dtype)


def result_rows(half, first, second, act, slope, up, down):
    _, count, width = first.shape
    hidden = up.shape[1]
    return pl.pallas_call(
        functools.partial(result_kernel, half),
        out_shape=(
            jax.ShapeDtypeStruct(first.shape, WIDE),
            jax.ShapeDtypeStruct(first.shape, LOW),
        ),
        in_specs=in_vmem(6),
        out_specs=tuple(in_vmem(2)),
        compiler_params=pltpu.CompilerParams(vmem_limit_bytes=VMEM_BYTES),
        cost_estimate=cost(12 * count * width * hidden, 4 * width * hidden + 28 * count * width),
    )(first, second, act, slope, up, down)


def all_to_all(value, axes):
    return lax.all_to_all(value, axes, split_axis=0, concat_axis=0, tiled=True)


def sum_everywhere(term):
    near = lax.axis_size(NEAR)
    rest = lax.axis_size(REST)
    depth, width = term.shape
    part = jnp.sum(all_to_all(term.reshape(near, depth // near, width), NEAR), axis=0)
    part = jnp.sum(all_to_all(jnp.broadcast_to(part[None], (rest,) + part.shape), REST), axis=0)
    whole = all_to_all(jnp.broadcast_to(part[None], (near,) + part.shape), NEAR)
    return whole.reshape(depth, width)


def swap(value, axis):
    return lax.ppermute(value, axis, [(0, 1), (1, 0)])


def team_moves():
    moves = []
    for slab in range(4):
        low, odd = slab // 2, slab % 2
        others = ((slab - 1, 0), (slab + 1, 1))
        placed = {slab: (odd, low)}
        for quarter, yl in others + ((slab + 2, 1 - odd),):
            taken = set(placed.values())
            core = low if (yl, low) not in taken else 1 - low
            placed[quarter % 4] = (yl, core)
        for quarter, (yl, core) in placed.items():
            moves.append(((quarter * 2 + odd) * 2 + low, (slab * 2 + yl) * 2 + core))
    return moves


def move(value, moves):
    return lax.ppermute(value, DP + TEAM, moves)


def shards(tokens, router, up_weight, down_weight, cotangent):
    tokens, cotangent = tokens[0], cotangent[0]
    moves = team_moves()
    up = move(up_weight[0], moves)

    logits = wide_einsum("md,ds->ms", tokens, router)
    dispatch = jax.nn.softmax(logits, axis=0)
    combine = jax.nn.softmax(logits, axis=1)
    dispatch_low = dispatch.astype(LOW)
    combine_low = combine.astype(LOW)
    slot_inputs = wide_einsum("ms,md->sd", dispatch_low, tokens).astype(LOW)
    slot_cotangent = wide_einsum("ms,md->sd", combine_low, cotangent).astype(LOW)

    sent = jnp.stack([slot_inputs, slot_cotangent], axis=1)
    own, down = lax.optimization_barrier((all_to_all(sent, ROUTE), down_weight[0]))
    own = jnp.swapaxes(own, 0, 1)
    beside = swap(own, "core")
    across = swap(own, "yl")
    down = move(down, moves)
    corner = swap(across, "core")

    act, slope, grad_down = hidden_rows((across, corner, own, beside), up)
    far_kept, far_sent = result_rows(0, across, corner, act, slope, up, down)
    far_back = swap(far_sent, "core")
    own_kept, own_sent = result_rows(1, own, beside, act, slope, up, down)
    own_back = swap(own_sent, "core")
    across_back = swap((far_kept + far_back.astype(WIDE)).astype(LOW), "yl")
    grad_down, _ = lax.optimization_barrier((grad_down, own_sent))
    grad_down = move(grad_down, [(there, here) for here, there in moves])
    summed = (own_kept + own_back.astype(WIDE) + across_back.astype(WIDE)).astype(LOW)

    back = all_to_all(jnp.swapaxes(summed, 0, 1), ROUTE)
    slot_outputs, input_grads = back[:, 0], back[:, 1]

    combine_grad = wide_einsum("md,sd->ms", cotangent, slot_outputs)
    dispatch_grad = wide_einsum("md,sd->ms", tokens, input_grads)
    logit_grad = combine * (combine_grad - jnp.sum(combine * combine_grad, axis=1, keepdims=True))
    logit_grad = logit_grad + dispatch * (
        dispatch_grad - jnp.sum(dispatch * dispatch_grad, axis=0, keepdims=True)
    )
    logit_low = logit_grad.astype(LOW)
    grad_router = sum_everywhere(wide_einsum("md,ms->ds", tokens, logit_low))

    grad_tokens = wide_einsum("ms,sd->md", dispatch_low, input_grads)
    grad_tokens = grad_tokens + wide_einsum("ms,ds->md", logit_low, router)
    return (grad_tokens.astype(LOW)[None], grad_router, grad_down[None])


def solution(mesh):
    sizes = tuple(DP_SPLIT.values()) + tuple(EXPERT_SPLIT.values())
    images = P(EVERY, None, None)
    return jax.shard_map(
        shards,
        mesh=Mesh(mesh.devices.reshape(sizes), EVERY),
        in_specs=(images, P(), P(EXPERT, None, DP), P(EXPERT, DP, None), images),
        out_specs=(images, P(), P(EXPERT, DP, None)),
        check_vma=False,
    )
```

time: 283 us -> 218 us (0.77)
  blocking collectives: 149 us -> 52.8 us
  waiting for transfers between devices: 20.8 us -> 50.9 us
  other arithmetic: 5.17 us -> 0.66 us
  Pallas kernels: 4 us -> 7.67 us
    all_to_all x3 -> x2, blocking collectives: 149 us -> 52.8 us  [all_to_all(): return lax.all_to_all(value, axes, split_axis=0, concat_axis=0, tiled=True)]
    ppermute x6, starting transfers between devices: 48.6 us -> 13.9 us  [swap(): return lax.ppermute(value, axis, [(0, 1), (1, 0)])]
    ppermute x5 -> x3, starting transfers between devices: 13.8 us -> 39.8 us  [move(): return lax.ppermute(value, DP + TEAM, moves)]
    ppermute x6, waiting for transfers between devices: 9.03 us -> 25.3 us  [swap(): return lax.ppermute(value, axis, [(0, 1), (1, 0)])]
    all_to_all x2 -> x3, waiting for transfers between devices: 11.8 us -> 25.6 us  [all_to_all(): return lax.all_to_all(value, axes, split_axis=0, concat_axis=0, tiled=True)]
    all_to_all x2 -> x3, starting transfers between devices: 27.8 us -> 39.2 us  [all_to_all(): return lax.all_to_all(value, axes, split_axis=0, concat_axis=0, tiled=True)]
    pallas_call x3, Pallas kernels: 4 us -> 7.67 us  [the longest x2 5.09 us: result_rows(): pl.pallas_call(functools.partial(result_kernel, half), out_shape=(jax.Sha...]
    select_n x2 -> x0, other arithmetic: 2.92 us -> none  [finish_move(): return jnp.where(offset == 0, value, jnp.where(offset == 2, twice, once))]
  transfers between devices with their start and end apart: 13 -> 12, of which waited for: 3 -> 6; matrix products, arithmetic and copies ran while one was open for 4% -> 1% of each run, Pallas kernels for 1% -> 2%
where the time goes in v4:
time: 218 us
  starting transfers between devices  92.9 us (43%)
  blocking collectives  52.8 us (24%)
  waiting for transfers between devices  50.9 us (23%)
  local copies, waits for them, and re-layouts  7.92 us (4%)
  Pallas kernels  7.67 us (4%)
  matrix products  3.91 us (2%)
    all_to_all x2, blocking collectives, all_to_all(): return lax.all_to_all(value, axes, split_axis=0, concat_axis=0, tiled=True)  52.8 us
    ppermute x3, starting transfers between devices, move(): return lax.ppermute(value, DP + TEAM, moves)  39.8 us
    all_to_all x3, starting transfers between devices, all_to_all(): return lax.all_to_all(value, axes, split_axis=0, concat_axis=0, tiled=True)  39.2 us
    all_to_all x3, waiting for transfers between devices, all_to_all(): return lax.all_to_all(value, axes, split_axis=0, concat_axis=0, tiled=True)  25.6 us
    ppermute x6, waiting for transfers between devices, swap(): return lax.ppermute(value, axis, [(0, 1), (1, 0)])  25.3 us
    ppermute x6, starting transfers between devices, swap(): return lax.ppermute(value, axis, [(0, 1), (1, 0)])  13.9 us
    pallas_call x2, Pallas kernels, result_rows(): pl.pallas_call(functools.partial(result_kernel, half), out_shape=(jax.Sha...  5.09 us
  transfers between devices with their start and end apart: 12, of which 6 were waited for; matrix products, arithmetic and copies ran while one was open for 1% of the time, Pallas kernels for 2%

profile of v4, /device:TPU:1, one launch (start us, length us, event | category | flops | bytes accessed | tf_op | source)
XLA Modules:
  0.0 217.7 jit_solution(5149902783202458301)
XLA Ops:
  0.6 0.0 copy-start
  0.7 0.9 copy-done
  1.6 1.2 fusion.23
  2.9 0.2 fusion.13
  3.1 0.2 fusion.2
  3.3 0.3 fusion.3
  3.7 1.2 copy.19
  4.9 20.8 %all-to-all-start = ((bf16[128,2,768]{2,1,0:T(2,128)(2,1)}), bf16[128,2,768]{2,1,0:T(2,128)(2,1)S(1)}, u32[]{:S(2)}, u32[]{:S(2)}) async-start(bf16[128,2,768]{2,1,0:T(2,128)(2,1)} %copy.19), calls=%async_computation | async-start | bytes 786432 | tf_op jit(solution)/shard_map/all_to_all | solution.py:109
  25.7 6.7 %collective-permute-start.3 = (bf16[768,768]{1,0:T(8,128)(2,1)}, bf16[768,768]{1,0:T(8,128)(2,1)S(1)}, u32[]{:S(2)}, u32[]{:S(2)}) collective-permute-start(bf16[768,768]{1,0:T(8,128)(2,1)} %bitcast.58), channel_id=1, source_target_pairs={{0,0},{384,1},{128,64},{256,65},{192,192},{64,128},{320,193},{448,... | collective-permute-start | bytes 3538952 | tf_op jit(solution)/shard_map/ppermute | solution.py:142
  32.4 9.7 %all-to-all-done = bf16[128,2,768]{2,1,0:T(2,128)(2,1)S(1)} async-done(((bf16[128,2,768]{2,1,0:T(2,128)(2,1)}), bf16[128,2,768]{2,1,0:T(2,128)(2,1)S(1)}, u32[]{:S(2)}, u32[]{:S(2)}) %all-to-all-start) | async-done | bytes 393248 | tf_op jit(solution)/shard_map/all_to_all | solution.py:109
  42.2 30.3 %collective-permute-start.4 = (bf16[768,768]{1,0:T(8,128)(2,1)}, bf16[768,768]{1,0:T(8,128)(2,1)S(1)}, u32[]{:S(2)}, u32[]{:S(2)}) collective-permute-start(bf16[768,768]{1,0:T(8,128)(2,1)} %bitcast.59), channel_id=1, source_target_pairs={{0,0},{384,1},{128,64},{256,65},{192,192},{64,128},{320,193},{448,... | collective-permute-start | bytes 3538952 | tf_op jit(solution)/shard_map/ppermute | solution.py:142
  72.5 1.9 collective-permute-start.1
  74.5 1.9 collective-permute-start
  76.4 14.3 %collective-permute-done.1.refs_0_.first_ref = bf16[2,128,768]{2,1,0:T(8,128)(2,1)S(1)} collective-permute-done((bf16[2,128,768]{2,1,0:T(8,128)(2,1)S(1)}, bf16[2,128,768]{2,1,0:T(8,128)(2,1)S(1)}, u32[]{:S(2)}, u32[]{:S(2)}) %collective-permute-start.1) | collective-permute-done | bytes 393248 | tf_op jit(solution)/shard_map/ppermute | solution.py:123
  90.7 1.9 collective-permute-start.2
  92.6 0.0 collective-permute-done.refs_3_.second_ref
  92.6 0.0 collective-permute-done.3.refs_4_.up_ref
  92.6 1.7 collective-permute-done.2.refs_1_.second_ref
  94.3 2.6 %shard_map.76 = (bf16[512,768]{1,0:T(8,128)(2,1)S(1)}, f32[512,768]{1,0:T(8,128)}, bf16[768,768]{1,0:T(8,128)(2,1)S(1)}) custom-call(bf16[2,128,768]{2,1,0:T(8,128)(2,1)S(1)} %collective-permute-done.1.refs_0_.first_ref, bf16[2,128,768]{2,1,0:T(8,128)(2,1)S(1)} %collective-permute-done.2.refs_1_.second_ref, bf16[2,128,768]{2,1,0:T(8,128)(2,1)S(1)} %bitcast.55, ...), custom_call_target="tpu_custom_call" | custom-call | flops 1207959552 | bytes 6291456 | tf_op jit(solution)/shard_map/pallas_call | solution.py:65
  96.9 0.0 collective-permute-done.4.down_ref
  96.9 2.5 %shard_map.78 = (f32[2,128,768]{2,1,0:T(8,128)S(1)}, bf16[2,128,768]{2,1,0:T(8,128)(2,1)S(1)}) custom-call(bf16[2,128,768]{2,1,0:T(8,128)(2,1)S(1)} %collective-permute-done.1.refs_0_.first_ref, bf16[2,128,768]{2,1,0:T(8,128)(2,1)S(1)} %collective-permute-done.2.refs_1_.second_ref, bf16[512,768]{1,0:T(8,128)(2,1)S(1)} %get-tuple-element.14.act_ref, ...), custom_call_target="tpu_custom_call" | custom-call | flops 905969664 | bytes 5111808 | tf_op jit(solution)/shard_map/pallas_call | solution.py:95
  99.4 2.0 collective-permute-start.6
  101.5 2.5 %shard_map.77 = (f32[2,128,768]{2,1,0:T(8,128)S(1)}, bf16[2,128,768]{2,1,0:T(8,128)(2,1)S(1)}) custom-call(bf16[2,128,768]{2,1,0:T(8,128)(2,1)S(1)} %bitcast.56, bf16[2,128,768]{2,1,0:T(8,128)(2,1)S(1)} %collective-permute-done.refs_3_.second_ref, bf16[512,768]{1,0:T(8,128)(2,1)S(1)} %get-tuple-element.14.act_ref, f32[512,768]{1,0:T(8,128)} %get-tuple-element.15.slope_ref, ...), custom_call_target="tpu_custom_call" | custom-call | flops 905969664 | bytes 5111808 | tf_op jit(solution)/shard_map/pallas_call | solution.py:95
  104.0 2.3 %collective-permute-start.5 = (bf16[2,128,768]{2,1,0:T(8,128)(2,1)S(1)}, bf16[2,128,768]{2,1,0:T(8,128)(2,1)S(1)}, u32[]{:S(2)}, u32[]{:S(2)}) collective-permute-start(bf16[2,128,768]{2,1,0:T(8,128)(2,1)S(1)} %get-tuple-element.18), channel_id=1, source_target_pairs={{0,1},{1,0},{2,3},{3,2},{4,5},{5,4},{6,7},{7,6},{8,9},{9,8},{10,11... | collective-permute-start | bytes 1179656 | tf_op jit(solution)/shard_map/ppermute | solution.py:123
  106.3 0.0 collective-permute-done.6
  106.3 0.1 add_convert_fusion.1
  106.4 3.8 %collective-permute-start.7 = (bf16[2,128,768]{2,1,0:T(8,128)(2,1)S(1)}, bf16[2,128,768]{2,1,0:T(8,128)(2,1)S(1)}, u32[]{:S(2)}, u32[]{:S(2)}) collective-permute-start(bf16[2,128,768]{2,1,0:T(8,128)(2,1)S(1)} %add_convert_fusion.1), channel_id=1, source_target_pairs={{0,64},{64,0},{1,65},{65,1},{2,66},{66,2},{3,67},{67,3},{4,68},{68... | collective-permute-start | bytes 1179656 | tf_op jit(solution)/shard_map/ppermute | solution.py:123
  110.2 9.3 %collective-permute-done.7 = bf16[2,128,768]{2,1,0:T(8,128)(2,1)S(1)} collective-permute-done((bf16[2,128,768]{2,1,0:T(8,128)(2,1)S(1)}, bf16[2,128,768]{2,1,0:T(8,128)(2,1)S(1)}, u32[]{:S(2)}, u32[]{:S(2)}) %collective-permute-start.7) | collective-permute-done | bytes 393248 | tf_op jit(solution)/shard_map/ppermute | solution.py:123
  119.6 0.1 fusion.4
  119.7 0.4 copy.21
  120.1 27.2 %all_to_all.25 = bf16[128,2,768]{2,1,0:T(2,128)(2,1)S(1)} all-to-all(bf16[128,2,768]{2,1,0:T(2,128)(2,1)S(1)} %copy.21), channel_id=1, replica_groups=mesh['gh'=2,'gl'=2,'yl'=2,'x'=4,'zh'=4,'zl'=2,'core'=2] {'gl','x','zh','..., dimensions={0} | all-to-all | bytes 786432 | tf_op jit(solution)/shard_map/all_to_all | solution.py:109
  147.4 0.5 fusion.24
  147.9 0.2 convolution_bitcast_fusion.1
  148.2 0.3 multiply_reduce_fusion.1
  148.5 0.2 add_convert_fusion.2
  148.7 0.2 convolution_bitcast_fusion
  148.9 0.9 copy.24
  149.8 10.0 %all-to-all-start.2 = ((f32[32,24,128]{2,1,0:T(8,128)}), f32[32,24,128]{2,1,0:T(8,128)S(1)}, u32[]{:S(2)}, u32[]{:S(2)}) async-start(f32[32,24,128]{2,1,0:T(8,128)} %bitcast.14), calls=%async_computation.2 | async-start | bytes 786432 | tf_op jit(solution)/shard_map/all_to_all | solution.py:109
  159.9 2.7 %collective-permute-start.8 = (bf16[768,768]{1,0:T(8,128)(2,1)S(1)}, bf16[768,768]{1,0:T(8,128)(2,1)}, u32[]{:S(2)}, u32[]{:S(2)}) collective-permute-start(bf16[768,768]{1,0:T(8,128)(2,1)S(1)} %get-tuple-element.22), channel_id=1, source_target_pairs={{0,0},{1,384},{64,128},{65,256},{192,192},{128,64},{193,320},{129,... | collective-permute-start | bytes 3538952 | tf_op jit(solution)/shard_map/ppermute | solution.py:142
  162.6 7.5 %all-to-all-done.2 = f32[32,24,128]{2,1,0:T(8,128)S(1)} async-done(((f32[32,24,128]{2,1,0:T(8,128)}), f32[32,24,128]{2,1,0:T(8,128)S(1)}, u32[]{:S(2)}, u32[]{:S(2)}) %all-to-all-start.2) | async-done | bytes 393248 | tf_op jit(solution)/shard_map/all_to_all | solution.py:109
  170.2 25.6 %all_to_all.26 = f32[16,24,128]{2,1,0:T(8,128)S(1)} all-to-all(f32[16,24,128]{2,1,0:T(8,128)S(1)} %broadcast_in_dim.9), channel_id=1, replica_groups=mesh['gh'=2,'gl'=2,'yl'=2,'x'=4,'zh'=4,'zl'=2,'core'=2] {'gh','gl','zh'}, dimensions={0} | all-to-all | bytes 393216 | tf_op jit(solution)/shard_map/all_to_all | solution.py:109
  195.8 0.8 broadcast_in_dim.10
  196.6 8.4 %all-to-all-start.4 = ((f32[32,24,128]{2,1,0:T(8,128)}), f32[32,24,128]{2,1,0:T(8,128)S(1)}, u32[]{:S(2)}, u32[]{:S(2)}) async-start(f32[32,24,128]{2,1,0:T(8,128)} %broadcast_in_dim.10), calls=%async_computation.4 | async-start | bytes 786432 | tf_op jit(solution)/shard_map/all_to_all | solution.py:109
  204.9 0.2 fusion.16
  205.2 1.0 fusion.1
  206.2 8.3 %all-to-all-done.4 = f32[32,24,128]{2,1,0:T(8,128)S(1)} async-done(((f32[32,24,128]{2,1,0:T(8,128)}), f32[32,24,128]{2,1,0:T(8,128)S(1)}, u32[]{:S(2)}, u32[]{:S(2)}) %all-to-all-start.4) | async-done | bytes 393248 | tf_op jit(solution)/shard_map/all_to_all | solution.py:109
  214.5 0.7 copy.38
  215.3 2.4 %copy.39 = bf16[1,768,768]{2,1,0:T(8,128)(2,1)} copy(bf16[1,768,768]{2,1,0:T(8,128)(2,1)} %bitcast.16) | data formatting | bytes 2359296
  (11 shorter events, 0.2 us)
Async XLA Ops:
  0.6 1.0 copy-start
  0.6 2.7 %copy-start.2 = (bf16[1,196,768]{2,1,0:T(8,128)(2,1)S(1)}, bf16[1,196,768]{2,1,0:T(8,128)(2,1)}, u32[]{:S(2)}) copy-start(bf16[1,196,768]{2,1,0:T(8,128)(2,1)} %param.9) | copy-start | bytes 903172
  4.9 37.3 %all-to-all-start = ((bf16[128,2,768]{2,1,0:T(2,128)(2,1)}), bf16[128,2,768]{2,1,0:T(2,128)(2,1)S(1)}, u32[]{:S(2)}, u32[]{:S(2)}) async-start(bf16[128,2,768]{2,1,0:T(2,128)(2,1)} %copy.19), calls=%async_computation | async-start | bytes 786432 | tf_op jit(solution)/shard_map/all_to_all | solution.py:109
  25.7 66.9 %collective-permute-start.3 = (bf16[768,768]{1,0:T(8,128)(2,1)}, bf16[768,768]{1,0:T(8,128)(2,1)S(1)}, u32[]{:S(2)}, u32[]{:S(2)}) collective-permute-start(bf16[768,768]{1,0:T(8,128)(2,1)} %bitcast.58), channel_id=1, source_target_pairs={{0,0},{384,1},{128,64},{256,65},{192,192},{64,128},{320,193},{448,... | collective-permute-start | bytes 3538952 | tf_op jit(solution)/shard_map/ppermute | solution.py:142
  42.2 54.7 %collective-permute-start.4 = (bf16[768,768]{1,0:T(8,128)(2,1)}, bf16[768,768]{1,0:T(8,128)(2,1)S(1)}, u32[]{:S(2)}, u32[]{:S(2)}) collective-permute-start(bf16[768,768]{1,0:T(8,128)(2,1)} %bitcast.59), channel_id=1, source_target_pairs={{0,0},{384,1},{128,64},{256,65},{192,192},{64,128},{320,193},{448,... | collective-permute-start | bytes 3538952 | tf_op jit(solution)/shard_map/ppermute | solution.py:142
  72.5 18.2 %collective-permute-start.1 = (bf16[2,128,768]{2,1,0:T(8,128)(2,1)S(1)}, bf16[2,128,768]{2,1,0:T(8,128)(2,1)S(1)}, u32[]{:S(2)}, u32[]{:S(2)}) collective-permute-start(bf16[2,128,768]{2,1,0:T(8,128)(2,1)S(1)} %bitcast.53), channel_id=1, source_target_pairs={{0,64},{64,0},{1,65},{65,1},{2,66},{66,2},{3,67},{67,3},{4,68},{68... | collective-permute-start | bytes 1179656 | tf_op jit(solution)/shard_map/ppermute | solution.py:123
  74.5 18.1 %collective-permute-start = (bf16[2,128,768]{2,1,0:T(8,128)(2,1)S(1)}, bf16[2,128,768]{2,1,0:T(8,128)(2,1)S(1)}, u32[]{:S(2)}, u32[]{:S(2)}) collective-permute-start(bf16[2,128,768]{2,1,0:T(8,128)(2,1)S(1)} %bitcast.54), channel_id=1, source_target_pairs={{0,1},{1,0},{2,3},{3,2},{4,5},{5,4},{6,7},{7,6},{8,9},{9,8},{10,11... | collective-permute-start | bytes 1179656 | tf_op jit(solution)/shard_map/ppermute | solution.py:123
  90.7 3.6 %collective-permute-start.2 = (bf16[2,128,768]{2,1,0:T(8,128)(2,1)S(1)}, bf16[2,128,768]{2,1,0:T(8,128)(2,1)S(1)}, u32[]{:S(2)}, u32[]{:S(2)}) collective-permute-start(bf16[2,128,768]{2,1,0:T(8,128)(2,1)S(1)} %collective-permute-done.1.refs_0_.first_ref), channel_id=1, source_target_pairs={{0,1},{1,0},{2,3},{3,2},{4,5},{5,4},{6,7},{7,6},{8,9},{9,8},{10,11... | collective-permute-start | bytes 1179656 | tf_op jit(solution)/shard_map/ppermute | solution.py:123
  99.4 6.9 %collective-permute-start.6 = (bf16[2,128,768]{2,1,0:T(8,128)(2,1)S(1)}, bf16[2,128,768]{2,1,0:T(8,128)(2,1)S(1)}, u32[]{:S(2)}, u32[]{:S(2)}) collective-permute-start(bf16[2,128,768]{2,1,0:T(8,128)(2,1)S(1)} %get-tuple-element.20), channel_id=1, source_target_pairs={{0,1},{1,0},{2,3},{3,2},{4,5},{5,4},{6,7},{7,6},{8,9},{9,8},{10,11... | collective-permute-start | bytes 1179656 | tf_op jit(solution)/shard_map/ppermute | solution.py:123
  104.0 6.2 %collective-permute-start.5 = (bf16[2,128,768]{2,1,0:T(8,128)(2,1)S(1)}, bf16[2,128,768]{2,1,0:T(8,128)(2,1)S(1)}, u32[]{:S(2)}, u32[]{:S(2)}) collective-permute-start(bf16[2,128,768]{2,1,0:T(8,128)(2,1)S(1)} %get-tuple-element.18), channel_id=1, source_target_pairs={{0,1},{1,0},{2,3},{3,2},{4,5},{5,4},{6,7},{7,6},{8,9},{9,8},{10,11... | collective-permute-start | bytes 1179656 | tf_op jit(solution)/shard_map/ppermute | solution.py:123
  106.4 13.2 %collective-permute-start.7 = (bf16[2,128,768]{2,1,0:T(8,128)(2,1)S(1)}, bf16[2,128,768]{2,1,0:T(8,128)(2,1)S(1)}, u32[]{:S(2)}, u32[]{:S(2)}) collective-permute-start(bf16[2,128,768]{2,1,0:T(8,128)(2,1)S(1)} %add_convert_fusion.1), channel_id=1, source_target_pairs={{0,64},{64,0},{1,65},{65,1},{2,66},{66,2},{3,67},{67,3},{4,68},{68... | collective-permute-start | bytes 1179656 | tf_op jit(solution)/shard_map/ppermute | solution.py:123
  149.8 20.3 %all-to-all-start.2 = ((f32[32,24,128]{2,1,0:T(8,128)}), f32[32,24,128]{2,1,0:T(8,128)S(1)}, u32[]{:S(2)}, u32[]{:S(2)}) async-start(f32[32,24,128]{2,1,0:T(8,128)} %bitcast.14), calls=%async_computation.2 | async-start | bytes 786432 | tf_op jit(solution)/shard_map/all_to_all | solution.py:109
  159.9 45.1 %collective-permute-start.8 = (bf16[768,768]{1,0:T(8,128)(2,1)S(1)}, bf16[768,768]{1,0:T(8,128)(2,1)}, u32[]{:S(2)}, u32[]{:S(2)}) collective-permute-start(bf16[768,768]{1,0:T(8,128)(2,1)S(1)} %get-tuple-element.22), channel_id=1, source_target_pairs={{0,0},{1,384},{64,128},{65,256},{192,192},{128,64},{193,320},{129,... | collective-permute-start | bytes 3538952 | tf_op jit(solution)/shard_map/ppermute | solution.py:142
  195.8 9.4 %copy-start.1 = (bf16[768,128]{1,0:T(8,128)(2,1)S(1)}, bf16[768,128]{1,0:T(8,128)(2,1)}, u32[]{:S(2)}) copy-start(bf16[768,128]{1,0:T(8,128)(2,1)} %param.6) | copy-start | bytes 589828
  196.6 18.0 %all-to-all-start.4 = ((f32[32,24,128]{2,1,0:T(8,128)}), f32[32,24,128]{2,1,0:T(8,128)S(1)}, u32[]{:S(2)}, u32[]{:S(2)}) async-start(f32[32,24,128]{2,1,0:T(8,128)} %broadcast_in_dim.10), calls=%async_computation.4 | async-start | bytes 786432 | tf_op jit(solution)/shard_map/all_to_all | solution.py:109

commit v5 on v2

v5 whole, which is shorter than its diff:
```python
import math

import jax
import jax.numpy as jnp
from jax import lax
from jax.experimental import pallas as pl
from jax.experimental.pallas import tpu as pltpu
from jax.sharding import Mesh
from jax.sharding import PartitionSpec as P

GELU_SCALE = math.sqrt(2.0 / math.pi)
GELU_CUBIC = 0.044715
LOW = jnp.bfloat16
WIDE = jnp.float32
EXPERT_SPLIT = {"yl": 2, "x": 4, "zh": 4, "zl": 2, "core": 2}
EXPERT = tuple(EXPERT_SPLIT)
EVERY = ("dp",) + EXPERT
NEAR = ("yl", "x", "zl", "core")
REST = ("dp", "zh")
VMEM_BYTES = 48 * 2**20


def wide_einsum(spec, left, right):
    return jnp.einsum(spec, left, right, preferred_element_type=WIDE)


def wide_dot(left, right, left_dim, right_dim):
    return lax.dot_general(
        left, right, (((left_dim,), (right_dim,)), ((), ())), preferred_element_type=WIDE
    )


def in_vmem(count):
    return [pl.BlockSpec(memory_space=pltpu.VMEM)] * count


def cost(flops, bytes_accessed):
    return pl.CostEstimate(flops=flops, bytes_accessed=bytes_accessed, transcendentals=0)


def expert_kernel(rows_ref, up_ref, down_ref, share_ref, act_ref):
    up, down = up_ref[...], down_ref[...]
    hidden_pre = wide_dot(rows_ref[0], up, 1, 0)
    squared = hidden_pre * hidden_pre
    inner = jnp.tanh(GELU_SCALE * (hidden_pre + GELU_CUBIC * squared * hidden_pre))
    half = 0.5 * (1.0 + inner)
    activation = (hidden_pre * half).astype(LOW)
    act_ref[...] = activation
    share_ref[0] = wide_dot(activation, down, 1, 0).astype(LOW)
    slope = half + 0.5 * hidden_pre * (1.0 - inner * inner) * (
        GELU_SCALE + 3.0 * GELU_SCALE * GELU_CUBIC * squared
    )
    upstream = wide_dot(rows_ref[1], down, 1, 1)
    hidden_grad = (upstream * slope).astype(LOW)
    share_ref[1] = wide_dot(hidden_grad, up, 1, 1).astype(LOW)


def expert_rows(rows, up, down):
    _, count, width = rows.shape
    hidden = up.shape[1]
    return pl.pallas_call(
        expert_kernel,
        out_shape=(
            jax.ShapeDtypeStruct(rows.shape, LOW),
            jax.ShapeDtypeStruct((count, hidden), LOW),
        ),
        in_specs=in_vmem(3),
        out_specs=tuple(in_vmem(2)),
        compiler_params=pltpu.CompilerParams(vmem_limit_bytes=VMEM_BYTES),
        cost_estimate=cost(8 * count * width * hidden, 4 * width * hidden + 10 * count * width),
    )(rows, up, down)


def outer_kernel(act_ref, rows_ref, grad_ref):
    grad_ref[...] = wide_dot(act_ref[...], rows_ref[1], 0, 0).astype(LOW)


def outer_sum(act, rows):
    count, hidden = act.shape
    width = rows.shape[2]
    return pl.pallas_call(
        outer_kernel,
        out_shape=jax.ShapeDtypeStruct((hidden, width), LOW),
        in_specs=in_vmem(2),
        out_specs=in_vmem(1)[0],
        compiler_params=pltpu.CompilerParams(vmem_limit_bytes=VMEM_BYTES),
        cost_estimate=cost(2 * count * width * hidden, 2 * hidden * width),
    )(act, rows)


def all_to_all(value, axes):
    return lax.all_to_all(value, axes, split_axis=0, concat_axis=0, tiled=True)


def sum_everywhere(term):
    near = lax.axis_size(NEAR)
    rest = lax.axis_size(REST)
    depth, width = term.shape
    part = jnp.sum(all_to_all(term.reshape(near, depth // near, width), NEAR), axis=0)
    part = jnp.sum(all_to_all(jnp.broadcast_to(part[None], (rest,) + part.shape), REST), axis=0)
    whole = all_to_all(jnp.broadcast_to(part[None], (near,) + part.shape), NEAR)
    return whole.reshape(depth, width)


def shards(tokens, router, up_weight, down_weight, cotangent):
    tokens, cotangent = tokens[0], cotangent[0]
    up, down = up_weight[0], down_weight[0]
    slabs = lax.axis_size("dp")

    logits = wide_einsum("md,ds->ms", tokens, router)
    dispatch = jax.nn.softmax(logits, axis=0)
    combine = jax.nn.softmax(logits, axis=1)
    dispatch_low = dispatch.astype(LOW)
    combine_low = combine.astype(LOW)
    slot_inputs = wide_einsum("ms,md->sd", dispatch_low, tokens).astype(LOW)
    slot_cotangent = wide_einsum("ms,md->sd", combine_low, cotangent).astype(LOW)

    sent = jnp.stack([slot_inputs, slot_cotangent], axis=1)
    copies = jnp.broadcast_to(sent[None], (slabs,) + sent.shape).reshape((-1,) + sent.shape[1:])
    rows = jnp.swapaxes(all_to_all(copies, EVERY), 0, 1)
    shares, act = expert_rows(rows, up, down)
    grad_down = outer_sum(act, rows)
    back = all_to_all(jnp.swapaxes(shares, 0, 1), EVERY).reshape((slabs,) + sent.shape)
    back = jnp.sum(back.astype(WIDE), axis=0).astype(LOW)
    slot_outputs, input_grads = back[:, 0], back[:, 1]

    combine_grad = wide_einsum("md,sd->ms", cotangent, slot_outputs)
    dispatch_grad = wide_einsum("md,sd->ms", tokens, input_grads)
    logit_grad = combine * (combine_grad - jnp.sum(combine * combine_grad, axis=1, keepdims=True))
    logit_grad = logit_grad + dispatch * (
        dispatch_grad - jnp.sum(dispatch * dispatch_grad, axis=0, keepdims=True)
    )
    logit_low = logit_grad.astype(LOW)
    grad_router = sum_everywhere(wide_einsum("md,ms->ds", tokens, logit_low))

    grad_tokens = wide_einsum("ms,sd->md", dispatch_low, input_grads)
    grad_tokens = grad_tokens + wide_einsum("ms,ds->md", logit_low, router)
    return (grad_tokens.astype(LOW)[None], grad_router, grad_down[None])


def solution(mesh):
    sizes = (-1,) + tuple(EXPERT_SPLIT.values())
    images = P(EVERY, None, None)
    return jax.shard_map(
        shards,
        mesh=Mesh(mesh.devices.reshape(sizes), EVERY),
        in_specs=(images, P(), P(EXPERT, None, "dp"), P(EXPERT, "dp", None), images),
        out_specs=(images, P(), P(EXPERT, "dp", None)),
        check_vma=False,
    )
```

time: 189 us -> 184 us (0.974)
  blocking collectives: 88.3 us -> 148 us
  starting transfers between devices: 49.6 us -> 5.6 us
  waiting for transfers between devices: 32.3 us -> 6.42 us
  local copies, waits for them, and re-layouts: 4.66 us -> 8.64 us
  other arithmetic: 0.75 us -> 2.8 us
    all_to_all x4, blocking collectives: 88.3 us -> 148 us  [all_to_all(): return lax.all_to_all(value, axes, split_axis=0, concat_axis=0, tiled=True)]
    ppermute x12 -> x0, starting transfers between devices: 41.7 us -> none  [the longest x6 24.5 us: left(): return lax.ppermute(value, 'dp', [(i, (i - 1) % dp) for i in range(dp)])]
    ppermute x12 -> x0, waiting for transfers between devices: 27.7 us -> none  [the longest x6 16.4 us: right(): return lax.ppermute(value, 'dp', [(i, (i + 1) % dp) for i in range(dp)])]
    reduce_sum x1 -> x2, other arithmetic: 0.07 us -> 2.38 us  [the longest x1 2.36 us: shards(): back = jnp.sum(back.astype(WIDE), axis=0).astype(LOW)]
    all_to_all x1, starting transfers between devices: 7.83 us -> 5.6 us  [all_to_all(): return lax.all_to_all(value, axes, split_axis=0, concat_axis=0, tiled=True)]
    pallas_call x5 -> x2, Pallas kernels: 7.52 us -> 6.18 us  [the longest x1 4.34 us: expert_rows(): pl.pallas_call(expert_kernel, out_shape=(jax.ShapeDtypeStruct(rows.shape,...]
  transfers between devices with their start and end apart: 13 -> 1, of which waited for: 6 -> 1; matrix products, arithmetic and copies ran while one was open for 1% -> 1% of each run, Pallas kernels for 4% -> 1%
where the time goes in v5:
time: 184 us
  blocking collectives  148 us (80%)
  local copies, waits for them, and re-layouts  8.64 us (5%)
  waiting for transfers between devices  6.42 us (3%)
  Pallas kernels  6.18 us (3%)
  starting transfers between devices  5.6 us (3%)
  matrix products  4.86 us (3%)
  other arithmetic  2.8 us (2%)
    all_to_all x4, blocking collectives, all_to_all(): return lax.all_to_all(value, axes, split_axis=0, concat_axis=0, tiled=True)  148 us
    all_to_all x1, waiting for transfers between devices, all_to_all(): return lax.all_to_all(value, axes, split_axis=0, concat_axis=0, tiled=True)  6.42 us
    all_to_all x1, starting transfers between devices, all_to_all(): return lax.all_to_all(value, axes, split_axis=0, concat_axis=0, tiled=True)  5.6 us
    dot_general x8, matrix products, wide_einsum(): return jnp.einsum(spec, left, right, preferred_element_type=WIDE)  4.86 us
    pallas_call x1, Pallas kernels, expert_rows(): pl.pallas_call(expert_kernel, out_shape=(jax.ShapeDtypeStruct(rows.shape,...  4.34 us
  transfers between devices with their start and end apart: 1, of which 1 were waited for; matrix products, arithmetic and copies ran while one was open for 1% of the time, Pallas kernels for 1%

profile of v5, /device:TPU:1, one launch (start us, length us, event | category | flops | bytes accessed | tf_op | source)
XLA Modules:
  0.0 183.9 jit_solution(13956501623143881642)
XLA Ops:
  0.6 0.0 copy-start
  0.6 1.0 copy-done
  1.6 1.2 fusion.28
  2.9 0.0 copy-start.10
  2.9 0.2 fusion.17
  3.1 0.0 copy-start.12
  3.1 0.2 fusion.2
  3.3 1.3 fusion.3
  4.7 0.4 copy.17
  5.1 0.8 broadcast_in_dim.10
  5.9 66.4 %all_to_all.25 = bf16[512,2,768]{2,1,0:T(2,128)(2,1)S(1)} all-to-all(bf16[512,2,768]{2,1,0:T(2,128)(2,1)S(1)} %bitcast.61), channel_id=1, replica_groups=mesh['dp'=4,'yl'=2,'x'=4,'zh'=4,'zl'=2,'core'=2] {'dp','yl','x','zh','zl..., dimensions={0} | all-to-all | bytes 3145728 | tf_op jit(solution)/shard_map/all_to_all | solution.py:92
  72.3 1.3 copy.38
  73.6 0.3 copy-done.2
  73.9 0.6 copy-done.3
  74.5 4.3 %shard_map.76 = (bf16[2,512,768]{2,1,0:T(8,128)(2,1)S(1)}, bf16[512,768]{1,0:T(8,128)(2,1)S(1)}) custom-call(bf16[2,512,768]{2,1,0:T(8,128)(2,1)} %bitcast.55, bf16[768,768]{1,0:T(8,128)(2,1)S(1)} %bitcast.58, bf16[768,768]{1,0:T(8,128)(2,1)S(1)} %bitcast.59), custom_call_target="tpu_custom_call" | custom-call | flops 2415919104 | bytes 6291456 | tf_op jit(solution)/shard_map/pallas_call | solution.py:61
  78.8 1.6 copy.19
  80.4 52.7 %all_to_all.26 = bf16[512,2,768]{2,1,0:T(2,128)(2,1)S(1)} all-to-all(bf16[512,2,768]{2,1,0:T(2,128)(2,1)S(1)} %copy.19), channel_id=1, replica_groups=mesh['dp'=4,'yl'=2,'x'=4,'zh'=4,'zl'=2,'core'=2] {'dp','yl','x','zh','zl..., dimensions={0} | all-to-all | bytes 3145728 | tf_op jit(solution)/shard_map/all_to_all | solution.py:92
  133.2 2.4 %reduce_sum.68 = bf16[128,2,768]{2,1,0:T(2,128)(2,1)S(1)} reduce(bf16[4,128,2,768]{3,2,1,0:T(2,128)(2,1)S(1)} %bitcast.60, bf16[]{:T(256)} %constant.2.clone.1), dimensions={0}, to_apply=%region_4.0 | reduce | flops 589824 | bytes 1966082 | tf_op jit(solution)/shard_map/reduce_sum | solution.py:124
  135.6 0.0 copy-start.9
  135.6 0.5 fusion.29
  136.1 0.0 copy-start.4
  136.1 0.2 convolution_bitcast_fusion.1
  136.4 0.1 copy-done.9
  136.5 0.3 multiply_reduce_fusion.1
  136.9 0.0 copy-done.10
  136.9 0.0 copy-done.12
  136.9 0.0 copy-done.4
  136.9 0.2 add_convert_fusion
  137.1 0.0 copy-start.7
  137.1 0.2 convolution_bitcast_fusion
  137.3 0.2 copy.20
  137.5 0.2 copy-done.7
  137.7 13.6 %all_to_all.27 = f32[32,24,128]{2,1,0:T(8,128)S(1)} all-to-all(f32[32,24,128]{2,1,0:T(8,128)S(1)} %bitcast.63), channel_id=1, replica_groups=mesh['dp'=4,'yl'=2,'x'=4,'zh'=4,'zl'=2,'core'=2] {'yl','x','zl','core'}, dimensions={0} | all-to-all | bytes 786432 | tf_op jit(solution)/shard_map/all_to_all | solution.py:92
  151.4 15.7 %all_to_all.28 = f32[16,24,128]{2,1,0:T(8,128)S(1)} all-to-all(f32[16,24,128]{2,1,0:T(8,128)S(1)} %broadcast_in_dim.12), channel_id=1, replica_groups=mesh['dp'=4,'yl'=2,'x'=4,'zh'=4,'zl'=2,'core'=2] {'dp','zh'}, dimensions={0} | all-to-all | bytes 393216 | tf_op jit(solution)/shard_map/all_to_all | solution.py:92
  167.1 0.8 broadcast_in_dim.13
  167.9 5.6 %all-to-all-start.4 = ((f32[32,24,128]{2,1,0:T(8,128)}), f32[32,24,128]{2,1,0:T(8,128)S(1)}, u32[]{:S(2)}, u32[]{:S(2)}) async-start(f32[32,24,128]{2,1,0:T(8,128)} %broadcast_in_dim.13), calls=%async_computation.4 | async-start | bytes 786432 | tf_op jit(solution)/shard_map/all_to_all | solution.py:92
  173.5 0.0 copy-done.1
  173.5 0.0 copy-start.5
  173.5 0.0 copy-start.6
  173.6 0.0 copy-start.8
  173.6 1.8 %shard_map.77 = bf16[768,768]{1,0:T(8,128)(2,1)} custom-call(bf16[512,768]{1,0:T(8,128)(2,1)S(1)} %get-tuple-element.6.act_ref, bf16[2,512,768]{2,1,0:T(8,128)(2,1)S(1)} %bitcast.56), custom_call_target="tpu_custom_call" | custom-call | flops 603979776 | bytes 1179648 | tf_op jit(solution)/shard_map/pallas_call | solution.py:81
  175.4 0.0 copy-done.13
  175.4 0.2 fusion.14
  175.6 0.0 copy-done.6
  175.7 0.0 copy-done.8
  175.7 1.0 fusion.1
  176.7 6.4 %all-to-all-done.4 = f32[32,24,128]{2,1,0:T(8,128)S(1)} async-done(((f32[32,24,128]{2,1,0:T(8,128)}), f32[32,24,128]{2,1,0:T(8,128)S(1)}, u32[]{:S(2)}, u32[]{:S(2)}) %all-to-all-start.4) | async-done | bytes 393248 | tf_op jit(solution)/shard_map/all_to_all | solution.py:92
  183.1 0.7 copy.40
  (11 shorter events, 0.1 us)
Async XLA Ops:
  0.6 1.0 copy-start
  2.9 134.0 %copy-start.10 = (f32[128]{0:T(128)}, f32[128]{0:T(128)S(1)}, u32[]{:S(2)}) copy-start(f32[128]{0:T(128)S(1)} %get-tuple-element.11) | copy-start | bytes 1540
  3.1 133.8 %copy-start.12 = (f32[128]{0:T(128)}, f32[128]{0:T(128)S(1)}, u32[]{:S(2)}) copy-start(f32[128]{0:T(128)S(1)} %get-tuple-element.9) | copy-start | bytes 1540
  72.3 1.6 copy-start.2
  72.3 2.2 %copy-start.3 = (bf16[1,768,768]{2,1,0:T(8,128)(2,1)S(1)}, bf16[1,768,768]{2,1,0:T(8,128)(2,1)}, u32[]{:S(2)}) copy-start(bf16[1,768,768]{2,1,0:T(8,128)(2,1)} %param.8) | copy-start | bytes 3538948
  135.6 1.0 copy-start.9
  136.1 0.8 copy-start.4
  137.1 0.6 copy-start.7
  137.7 35.8 %copy-start.1 = (bf16[512,2,768]{2,0,1:T(8,128)(2,1)S(1)}, bf16[512,2,768]{2,0,1:T(8,128)(2,1)}, u32[]{:S(2)}) copy-start(bf16[512,2,768]{2,0,1:T(8,128)(2,1)} %copy.38) | copy-start | bytes 4718596
  167.9 15.2 %all-to-all-start.4 = ((f32[32,24,128]{2,1,0:T(8,128)}), f32[32,24,128]{2,1,0:T(8,128)S(1)}, u32[]{:S(2)}, u32[]{:S(2)}) async-start(f32[32,24,128]{2,1,0:T(8,128)} %broadcast_in_dim.13), calls=%async_computation.4 | async-start | bytes 786432 | tf_op jit(solution)/shard_map/all_to_all | solution.py:92
  173.5 1.9 %copy-start.5 = (bf16[128,1,768]{2,1,0:T(2,128)(2,1)S(1)}, bf16[128,1,768]{2,1,0:T(2,128)(2,1)}, u32[]{:S(2)}) copy-start(bf16[128,1,768]{2,1,0:T(2,128)(2,1)} %copy-done.4) | copy-start | bytes 589828
  173.5 1.9 %copy-start.11 = (f32[128]{0:T(128)S(1)}, f32[128]{0:T(128)}, u32[]{:S(2)}) copy-start(f32[128]{0:T(128)} %copy-done.10) | copy-start | bytes 1540
  173.5 1.9 %copy-start.13 = (f32[128]{0:T(128)S(1)}, f32[128]{0:T(128)}, u32[]{:S(2)}) copy-start(f32[128]{0:T(128)} %copy-done.12) | copy-start | bytes 1540
  173.5 2.1 %copy-start.6 = (bf16[768,128]{1,0:T(8,128)(2,1)S(1)}, bf16[768,128]{1,0:T(8,128)(2,1)}, u32[]{:S(2)}) copy-start(bf16[768,128]{1,0:T(8,128)(2,1)} %param.6) | copy-start | bytes 589828
  173.6 2.1 %copy-start.8 = (bf16[196,128]{1,0:T(8,128)(2,1)S(1)}, bf16[196,128]{1,0:T(8,128)(2,1)}, u32[]{:S(2)}) copy-start(bf16[196,128]{1,0:T(8,128)(2,1)} %copy-done.7) | copy-start | bytes 150532

commit v6 on v5

--- a/solution.py
+++ b/solution.py
@@ -1,3 +1,4 @@
+import functools
 import math
 
 import jax
@@ -20,10 +21,6 @@
 VMEM_BYTES = 48 * 2**20
 
 
-def wide_einsum(spec, left, right):
-    return jnp.einsum(spec, left, right, preferred_element_type=WIDE)
-
-
 def wide_dot(left, right, left_dim, right_dim):
     return lax.dot_general(
         left, right, (((left_dim,), (right_dim,)), ((), ())), preferred_element_type=WIDE
@@ -36,6 +33,34 @@
 
 def cost(flops, bytes_accessed):
     return pl.CostEstimate(flops=flops, bytes_accessed=bytes_accessed, transcendentals=0)
+
+
+def routing_kernel(tokens_ref, router_ref, cotangent_ref, dispatch_ref, combine_ref, inputs_ref, grads_ref):
+    tokens = tokens_ref[...]
+    logits = wide_dot(tokens, router_ref[...], 1, 0)
+    powers = jnp.exp(logits - jnp.max(logits, axis=0, keepdims=True))
+    dispatch = powers / jnp.sum(powers, axis=0, keepdims=True)
+    dispatch_ref[...] = dispatch
+    inputs_ref[...] = wide_dot(dispatch.astype(LOW), tokens, 0, 0).astype(LOW)
+    powers = jnp.exp(logits - jnp.max(logits, axis=1, keepdims=True))
+    combine = powers / jnp.sum(powers, axis=1, keepdims=True)
+    combine_ref[...] = combine
+    grads_ref[...] = wide_dot(combine.astype(LOW), cotangent_ref[...], 0, 0).astype(LOW)
+
+
+def routing(tokens, router, cotangent):
+    patches, width = tokens.shape
+    slots = router.shape[1]
+    weights = jax.ShapeDtypeStruct((patches, slots), WIDE)
+    rows = jax.ShapeDtypeStruct((slots, width), LOW)
+    return pl.pallas_call(
+        routing_kernel,
+        out_shape=(weights, weights, rows, rows),
+        in_specs=in_vmem(3),
+        out_specs=tuple(in_vmem(4)),
+        compiler_params=pltpu.CompilerParams(vmem_limit_bytes=VMEM_BYTES),
+        cost_estimate=cost(6 * patches * width * slots, 4 * patches * width),
+    )(tokens, router, cotangent)
 
 
 def expert_kernel(rows_ref, up_ref, down_ref, share_ref, act_ref):
@@ -88,18 +113,86 @@
     )(act, rows)
 
 
+def logit_kernel(shares_ref, tokens_ref, cotangent_ref, dispatch_ref, combine_ref, inputs_ref, logit_ref, term_ref):
+    slabs = shares_ref.shape[1]
+
+    def total(route):
+        terms = [shares_ref[route, k].astype(WIDE) for k in range(slabs)]
+        return functools.reduce(jnp.add, terms).astype(LOW)
+
+    tokens = tokens_ref[...]
+    dispatch, combine = dispatch_ref[...], combine_ref[...]
+    input_grads = total(1)
+    inputs_ref[...] = input_grads
+    grad = wide_dot(cotangent_ref[...], total(0), 1, 1)
+    logit_grad = combine * (grad - jnp.sum(combine * grad, axis=1, keepdims=True))
+    grad = wide_dot(tokens, input_grads, 1, 1)
+    logit_grad = logit_grad + dispatch * (grad - jnp.sum(dispatch * grad, axis=0, keepdims=True))
+    logit_low = logit_grad.astype(LOW)
+    logit_ref[...] = logit_low
+    term_ref[...] = wide_dot(tokens, logit_low, 0, 0).astype(LOW)
+
+
+def logit_grads(shares, tokens, cotangent, dispatch, combine):
+    patches, width = tokens.shape
+    slots = dispatch.shape[1]
+    return pl.pallas_call(
+        logit_kernel,
+        out_shape=(
+            jax.ShapeDtypeStruct((slots, width), LOW),
+            jax.ShapeDtypeStruct((patches, slots), LOW),
+            jax.ShapeDtypeStruct((width, slots), LOW),
+        ),
+        in_specs=in_vmem(5),
+        out_specs=tuple(in_vmem(3)),
+        compiler_params=pltpu.CompilerParams(vmem_limit_bytes=VMEM_BYTES),
+        cost_estimate=cost(6 * patches * width * slots, 4 * patches * width),
+    )(shares, tokens, cotangent, dispatch, combine)
+
+
+def token_kernel(dispatch_ref, inputs_ref, logit_ref, router_ref, grad_ref):
+    grad = wide_dot(dispatch_ref[...].astype(LOW), inputs_ref[...], 1, 0)
+    grad_ref[...] = (grad + wide_dot(logit_ref[...], router_ref[...], 1, 1)).astype(LOW)
+
+
+def token_grads(dispatch, input_grads, logit_low, router):
+    patches, slots = dispatch.shape
+    width = router.shape[0]
+    return pl.pallas_call(
+        token_kernel,
+        out_shape=jax.ShapeDtypeStruct((patches, width), LOW),
+        in_specs=in_vmem(4),
+        out_specs=in_vmem(1)[0],
+        compiler_params=pltpu.CompilerParams(vmem_limit_bytes=VMEM_BYTES),
+        cost_estimate=cost(4 * patches * width * slots, 4 * patches * width),
+    )(dispatch, input_grads, logit_low, router)
+
+
+def total_kernel(parts_ref, copies_ref):
+    total = jnp.sum(parts_ref[...].astype(WIDE), axis=0).astype(LOW)
+    copies_ref[...] = jnp.broadcast_to(total[None], copies_ref.shape)
+
+
+def total_copies(parts, copies):
+    return pl.pallas_call(
+        total_kernel,
+        out_shape=jax.ShapeDtypeStruct((copies,) + parts.shape[1:], LOW),
+        in_specs=in_vmem(1),
+        out_specs=in_vmem(1)[0],
+        compiler_params=pltpu.CompilerParams(vmem_limit_bytes=VMEM_BYTES),
+    )(parts)
+
+
 def all_to_all(value, axes):
     return lax.all_to_all(value, axes, split_axis=0, concat_axis=0, tiled=True)
 
 
 def sum_everywhere(term):
     near = lax.axis_size(NEAR)
-    rest = lax.axis_size(REST)
     depth, width = term.shape
-    part = jnp.sum(all_to_all(term.reshape(near, depth // near, width), NEAR), axis=0)
-    part = jnp.sum(all_to_all(jnp.broadcast_to(part[None], (rest,) + part.shape), REST), axis=0)
-    whole = all_to_all(jnp.broadcast_to(part[None], (near,) + part.shape), NEAR)
-    return whole.reshape(depth, width)
+    parts = all_to_all(term.reshape(near, depth // near, width), NEAR)
+    parts = all_to_all(total_copies(parts, lax.axis_size(REST)), REST)
+    return all_to_all(total_copies(parts, near), NEAR).reshape(depth, width).astype(WIDE)
 
 
 def shards(tokens, router, up_weight, down_weight, cotangent):
@@ -107,35 +200,18 @@
     up, down = up_weight[0], down_weight[0]
     slabs = lax.axis_size("dp")
 
-    logits = wide_einsum("md,ds->ms", tokens, router)
-    dispatch = jax.nn.softmax(logits, axis=0)
-    combine = jax.nn.softmax(logits, axis=1)
-    dispatch_low = dispatch.astype(LOW)
-    combine_low = combine.astype(LOW)
-    slot_inputs = wide_einsum("ms,md->sd", dispatch_low, tokens).astype(LOW)
-    slot_cotangent = wide_einsum("ms,md->sd", combine_low, cotangent).astype(LOW)
-
+    dispatch, combine, slot_inputs, slot_cotangent = routing(tokens, router, cotangent)
     sent = jnp.stack([slot_inputs, slot_cotangent], axis=1)
     copies = jnp.broadcast_to(sent[None], (slabs,) + sent.shape).reshape((-1,) + sent.shape[1:])
     rows = jnp.swapaxes(all_to_all(copies, EVERY), 0, 1)
     shares, act = expert_rows(rows, up, down)
     grad_down = outer_sum(act, rows)
-    back = all_to_all(jnp.swapaxes(shares, 0, 1), EVERY).reshape((slabs,) + sent.shape)
-    back = jnp.sum(back.astype(WIDE), axis=0).astype(LOW)
-    slot_outputs, input_grads = back[:, 0], back[:, 1]
-
-    combine_grad = wide_einsum("md,sd->ms", cotangent, slot_outputs)
-    dispatch_grad = wide_einsum("md,sd->ms", tokens, input_grads)
-    logit_grad = combine * (combine_grad - jnp.sum(combine * combine_grad, axis=1, keepdims=True))
-    logit_grad = logit_grad + dispatch * (
-        dispatch_grad - jnp.sum(dispatch * dispatch_grad, axis=0, keepdims=True)
-    )
-    logit_low = logit_grad.astype(LOW)
-    grad_router = sum_everywhere(wide_einsum("md,ms->ds", tokens, logit_low))
-
-    grad_tokens = wide_einsum("ms,sd->md", dispatch_low, input_grads)
-    grad_tokens = grad_tokens + wide_einsum("ms,ds->md", logit_low, router)
-    return (grad_tokens.astype(LOW)[None], grad_router, grad_down[None])
+    back = jnp.swapaxes(all_to_all(jnp.swapaxes(shares, 0, 1), EVERY), 0, 1)
+    back = back.reshape((2, slabs) + slot_inputs.shape)
+    input_grads, logit_low, term = logit_grads(back, tokens, cotangent, dispatch, combine)
+    grad_router = sum_everywhere(term)
+    grad_tokens = token_grads(dispatch, input_grads, logit_low, router)
+    return (grad_tokens[None], grad_router, grad_down[None])
 
 
 def solution(mesh):

time: 184 us -> 176 us (0.957)
  matrix products: 4.86 us -> 0 us
  Pallas kernels: 6.18 us -> 9.43 us
  blocking collectives: 148 us -> 146 us
  other arithmetic: 2.8 us -> 0.82 us
    dot_general x8 -> x0, matrix products: 4.86 us -> none  [wide_einsum(): return jnp.einsum(spec, left, right, preferred_element_type=WIDE)]
    pallas_call x0 -> x5, Pallas kernels: none -> 3.25 us  [the longest x1 1.05 us: token_grads(): pl.pallas_call(token_kernel, out_shape=jax.ShapeDtypeStruct((patches, wid...]
    all_to_all x4, blocking collectives: 148 us -> 146 us  [all_to_all(): return lax.all_to_all(value, axes, split_axis=0, concat_axis=0, tiled=True)]
    reduce_sum x4 -> x0, other arithmetic: 2.61 us -> none  [the longest x1 2.36 us: shards(): back = jnp.sum(back.astype(WIDE), axis=0).astype(LOW)]
    unnamed x29 -> x18, local copies, waits for them, and re-layouts: 2.96 us -> 4.56 us
  transfers between devices with their start and end apart: 1 -> 1, of which waited for: 1 -> 1; matrix products, arithmetic and copies ran while one was open for 1% -> 0% of each run, Pallas kernels for 1% -> 2%
where the time goes in v6:
time: 176 us
  blocking collectives  146 us (83%)
  Pallas kernels  9.43 us (5%)
  local copies, waits for them, and re-layouts  8.95 us (5%)
  starting transfers between devices  5.25 us (3%)
  waiting for transfers between devices  4.77 us (3%)
    all_to_all x4, blocking collectives, all_to_all(): return lax.all_to_all(value, axes, split_axis=0, concat_axis=0, tiled=True)  146 us
    all_to_all x1, starting transfers between devices, all_to_all(): return lax.all_to_all(value, axes, split_axis=0, concat_axis=0, tiled=True)  5.25 us
    all_to_all x1, waiting for transfers between devices, all_to_all(): return lax.all_to_all(value, axes, split_axis=0, concat_axis=0, tiled=True)  4.77 us
    unnamed x18, local copies, waits for them, and re-layouts  4.56 us
    pallas_call x1, Pallas kernels, expert_rows(): pl.pallas_call(expert_kernel, out_shape=(jax.ShapeDtypeStruct(rows.shape,...  4.34 us
  transfers between devices with their start and end apart: 1, of which 1 were waited for; matrix products, arithmetic and copies ran while one was open for 0% of the time, Pallas kernels for 2%

profile of v6, /device:TPU:1, one launch (start us, length us, event | category | flops | bytes accessed | tf_op | source)
XLA Modules:
  0.0 175.8 jit_solution(861839899235761558)
XLA Ops:
  0.6 0.0 copy-start.1
  0.6 1.0 copy-done.1
  1.6 0.0 copy-start.3
  1.6 1.0 copy-done.3
  2.6 0.0 copy-start.5
  2.6 0.9 copy-done.5
  3.5 0.7 shard_map.76
  4.3 0.4 copy.8
  4.7 0.8 broadcast_in_dim.12
  5.5 66.4 %all_to_all.25 = bf16[512,2,768]{2,1,0:T(2,128)(2,1)S(1)} all-to-all(bf16[512,2,768]{2,1,0:T(2,128)(2,1)S(1)} %bitcast.33), channel_id=1, replica_groups=mesh['dp'=4,'yl'=2,'x'=4,'zh'=4,'zl'=2,'core'=2] {'dp','yl','x','zh','zl..., dimensions={0} | all-to-all | bytes 3145728 | tf_op jit(solution)/shard_map/all_to_all | solution.py:187
  71.9 0.0 copy-start.7
  71.9 0.0 copy-start.8
  71.9 1.4 copy.13
  73.2 0.3 copy-done.7
  73.5 0.6 copy-done.8
  74.1 4.3 %shard_map.77 = (bf16[2,512,768]{2,1,0:T(8,128)(2,1)S(1)}, bf16[512,768]{1,0:T(8,128)(2,1)S(1)}) custom-call(bf16[2,512,768]{2,1,0:T(8,128)(2,1)} %bitcast.19, bf16[768,768]{1,0:T(8,128)(2,1)S(1)} %bitcast.30, bf16[768,768]{1,0:T(8,128)(2,1)S(1)} %bitcast.31), custom_call_target="tpu_custom_call" | custom-call | flops 2415919104 | bytes 6291456 | tf_op jit(solution)/shard_map/pallas_call | solution.py:86
  78.4 1.6 copy.10
  80.0 52.7 %all_to_all.26 = bf16[512,2,768]{2,1,0:T(2,128)(2,1)S(1)} all-to-all(bf16[512,2,768]{2,1,0:T(2,128)(2,1)S(1)} %copy.10), channel_id=1, replica_groups=mesh['dp'=4,'yl'=2,'x'=4,'zh'=4,'zl'=2,'core'=2] {'dp','yl','x','zh','zl..., dimensions={0} | all-to-all | bytes 3145728 | tf_op jit(solution)/shard_map/all_to_all | solution.py:187
  132.8 0.0 copy-start.2
  132.8 0.0 copy-start.4
  132.8 0.2 copy.11
  133.0 0.8 copy-done.2
  133.7 0.1 copy-done.4
  133.8 0.0 copy-start
  133.8 0.7 shard_map.78
  134.6 11.5 %all_to_all.27.parts_ref = bf16[32,24,128]{2,1,0:T(8,128)(2,1)S(1)} all-to-all(bf16[32,24,128]{2,1,0:T(8,128)(2,1)S(1)} %bitcast.27), channel_id=1, replica_groups=mesh['dp'=4,'yl'=2,'x'=4,'zh'=4,'zl'=2,'core'=2] {'yl','x','zl','core'}, dimensions={0} | all-to-all | bytes 393216 | tf_op jit(solution)/shard_map/all_to_all | solution.py:187
  146.1 15.2 %all_to_all.28.parts_ref = bf16[16,24,128]{2,1,0:T(8,128)(2,1)S(1)} all-to-all(bf16[16,24,128]{2,1,0:T(8,128)(2,1)S(1)} %shard_map.80), channel_id=1, replica_groups=mesh['dp'=4,'yl'=2,'x'=4,'zh'=4,'zl'=2,'core'=2] {'dp','zh'}, dimensions={0} | all-to-all | bytes 196608 | tf_op jit(solution)/shard_map/all_to_all | solution.py:187
  161.4 0.7 shard_map.81
  162.1 5.2 %all-to-all-start.4 = ((bf16[32,24,128]{2,1,0:T(8,128)(2,1)}), bf16[32,24,128]{2,1,0:T(8,128)(2,1)S(1)}, u32[]{:S(2)}, u32[]{:S(2)}) async-start(bf16[32,24,128]{2,1,0:T(8,128)(2,1)} %shard_map.81), calls=%async_computation.4 | async-start | bytes 393216 | tf_op jit(solution)/shard_map/all_to_all | solution.py:187
  167.3 0.0 copy-done
  167.3 0.0 copy-start.6
  167.3 1.8 %shard_map.82 = bf16[768,768]{1,0:T(8,128)(2,1)} custom-call(bf16[512,768]{1,0:T(8,128)(2,1)S(1)} %get-tuple-element.20.act_ref, bf16[2,512,768]{2,1,0:T(8,128)(2,1)S(1)} %bitcast.20), custom_call_target="tpu_custom_call" | custom-call | flops 603979776 | bytes 1179648 | tf_op jit(solution)/shard_map/pallas_call | solution.py:106
  169.2 0.0 copy-done.6
  169.2 1.0 shard_map.79
  170.2 4.8 %all-to-all-done.4 = bf16[32,24,128]{2,1,0:T(8,128)(2,1)S(1)} async-done(((bf16[32,24,128]{2,1,0:T(8,128)(2,1)}), bf16[32,24,128]{2,1,0:T(8,128)(2,1)S(1)}, u32[]{:S(2)}, u32[]{:S(2)}) %all-to-all-start.4) | async-done | bytes 196640 | tf_op jit(solution)/shard_map/all_to_all | solution.py:187
  175.0 0.8 bitcast_convert_fusion
  (2 shorter events, 0.1 us)
Async XLA Ops:
  0.6 1.0 copy-start.1
  1.6 1.0 copy-start.3
  2.6 0.9 copy-start.5
  71.9 1.6 copy-start.7
  71.9 2.2 %copy-start.8 = (bf16[1,768,768]{2,1,0:T(8,128)(2,1)S(1)}, bf16[1,768,768]{2,1,0:T(8,128)(2,1)}, u32[]{:S(2)}) copy-start(bf16[1,768,768]{2,1,0:T(8,128)(2,1)} %param.8) | copy-start | bytes 3538948
  132.8 1.0 copy-start.2
  132.8 1.1 copy-start.4
  133.8 33.5 %copy-start = (bf16[512,2,768]{2,0,1:T(8,128)(2,1)S(1)}, bf16[512,2,768]{2,0,1:T(8,128)(2,1)}, u32[]{:S(2)}) copy-start(bf16[512,2,768]{2,0,1:T(8,128)(2,1)} %copy.13) | copy-start | bytes 4718596
  162.1 12.9 %all-to-all-start.4 = ((bf16[32,24,128]{2,1,0:T(8,128)(2,1)}), bf16[32,24,128]{2,1,0:T(8,128)(2,1)S(1)}, u32[]{:S(2)}, u32[]{:S(2)}) async-start(bf16[32,24,128]{2,1,0:T(8,128)(2,1)} %shard_map.81), calls=%async_computation.4 | async-start | bytes 393216 | tf_op jit(solution)/shard_map/all_to_all | solution.py:187
  167.3 1.9 %copy-start.6 = (bf16[768,128]{1,0:T(8,128)(2,1)S(1)}, bf16[768,128]{1,0:T(8,128)(2,1)}, u32[]{:S(2)}) copy-start(bf16[768,128]{1,0:T(8,128)(2,1)} %router_ref.3) | copy-start | bytes 589828

commit v7 on v6

--- a/solution.py
+++ b/solution.py
@@ -18,7 +18,7 @@
 EVERY = ("dp",) + EXPERT
 NEAR = ("yl", "x", "zl", "core")
 REST = ("dp", "zh")
-VMEM_BYTES = 48 * 2**20
+VMEM_BYTES = 20 * 2**20
 
 
 def wide_dot(left, right, left_dim, right_dim):
@@ -31,11 +31,34 @@
     return [pl.BlockSpec(memory_space=pltpu.VMEM)] * count
 
 
+def in_hbm(count):
+    return [pl.BlockSpec(memory_space=pltpu.HBM)] * count
+
+
+def fetch(sources, buffers, sems):
+    copies = [pltpu.make_async_copy(*pair, sems.at[k]) for k, pair in enumerate(zip(sources, buffers))]
+    for copy in copies:
+        copy.start()
+    return copies
+
+
+def buffers_for(*arrays):
+    return [pltpu.VMEM(a.shape, a.dtype) for a in arrays] + [pltpu.SemaphoreType.DMA((len(arrays),))]
+
+
 def cost(flops, bytes_accessed):
     return pl.CostEstimate(flops=flops, bytes_accessed=bytes_accessed, transcendentals=0)
 
 
-def routing_kernel(tokens_ref, router_ref, cotangent_ref, dispatch_ref, combine_ref, inputs_ref, grads_ref):
+def routing_kernel(
+    tokens_hbm, router_hbm, cotangent_hbm, dispatch_ref, combine_ref, inputs_ref, grads_ref,
+    tokens_ref, router_ref, cotangent_ref, sems,
+):
+    copies = fetch(
+        (tokens_hbm, router_hbm, cotangent_hbm), (tokens_ref, router_ref, cotangent_ref), sems
+    )
+    copies[0].wait()
+    copies[1].wait()
     tokens = tokens_ref[...]
     logits = wide_dot(tokens, router_ref[...], 1, 0)
     powers = jnp.exp(logits - jnp.max(logits, axis=0, keepdims=True))
@@ -45,6 +68,7 @@
     powers = jnp.exp(logits - jnp.max(logits, axis=1, keepdims=True))
     combine = powers / jnp.sum(powers, axis=1, keepdims=True)
     combine_ref[...] = combine
+    copies[2].wait()
     grads_ref[...] = wide_dot(combine.astype(LOW), cotangent_ref[...], 0, 0).astype(LOW)
 
 
@@ -56,21 +80,26 @@
     return pl.pallas_call(
         routing_kernel,
         out_shape=(weights, weights, rows, rows),
-        in_specs=in_vmem(3),
+        in_specs=in_hbm(3),
         out_specs=tuple(in_vmem(4)),
-        compiler_params=pltpu.CompilerParams(vmem_limit_bytes=VMEM_BYTES),
+        scratch_shapes=buffers_for(tokens, router, cotangent),
+        compiler_params=pltpu.CompilerParams(vmem_limit_bytes=61 * 2**20),
         cost_estimate=cost(6 * patches * width * slots, 4 * patches * width),
     )(tokens, router, cotangent)
 
 
-def expert_kernel(rows_ref, up_ref, down_ref, share_ref, act_ref):
-    up, down = up_ref[...], down_ref[...]
+def expert_kernel(rows_ref, up_hbm, down_hbm, share_ref, act_ref, up_ref, down_ref, sems):
+    copies = fetch((up_hbm, down_hbm), (up_ref, down_ref), sems)
+    copies[0].wait()
+    up = up_ref[...]
     hidden_pre = wide_dot(rows_ref[0], up, 1, 0)
     squared = hidden_pre * hidden_pre
     inner = jnp.tanh(GELU_SCALE * (hidden_pre + GELU_CUBIC * squared * hidden_pre))
     half = 0.5 * (1.0 + inner)
     activation = (hidden_pre * half).astype(LOW)
     act_ref[...] = activation
+    copies[1].wait()
+    down = down_ref[...]
     share_ref[0] = wide_dot(activation, down, 1, 0).astype(LOW)
     slope = half + 0.5 * hidden_pre * (1.0 - inner * inner) * (
         GELU_SCALE + 3.0 * GELU_SCALE * GELU_CUBIC * squared
@@ -89,8 +118,9 @@
             jax.ShapeDtypeStruct(rows.shape, LOW),
             jax.ShapeDtypeStruct((count, hidden), LOW),
         ),
-        in_specs=in_vmem(3),
+        in_specs=in_vmem(1) + in_hbm(2),
         out_specs=tuple(in_vmem(2)),
+        scratch_shapes=buffers_for(up, down),
         compiler_params=pltpu.CompilerParams(vmem_limit_bytes=VMEM_BYTES),
         cost_estimate=cost(8 * count * width * hidden, 4 * width * hidden + 10 * count * width),
     )(rows, up, down)
@@ -113,18 +143,25 @@
     )(act, rows)
 
 
-def logit_kernel(shares_ref, tokens_ref, cotangent_ref, dispatch_ref, combine_ref, inputs_ref, logit_ref, term_ref):
+def logit_kernel(
+    shares_ref, tokens_hbm, cotangent_hbm, dispatch_ref, combine_ref, inputs_ref, logit_ref, term_ref,
+    tokens_ref, cotangent_ref, sems,
+):
+    copies = fetch((tokens_hbm, cotangent_hbm), (tokens_ref, cotangent_ref), sems)
     slabs = shares_ref.shape[1]
 
     def total(route):
         terms = [shares_ref[route, k].astype(WIDE) for k in range(slabs)]
         return functools.reduce(jnp.add, terms).astype(LOW)
 
-    tokens = tokens_ref[...]
     dispatch, combine = dispatch_ref[...], combine_ref[...]
     input_grads = total(1)
     inputs_ref[...] = input_grads
-    grad = wide_dot(cotangent_ref[...], total(0), 1, 1)
+    slot_outputs = total(0)
+    copies[0].wait()
+    copies[1].wait()
+    tokens = tokens_ref[...]
+    grad = wide_dot(cotangent_ref[...], slot_outputs, 1, 1)
     logit_grad = combine * (grad - jnp.sum(combine * grad, axis=1, keepdims=True))
     grad = wide_dot(tokens, input_grads, 1, 1)
     logit_grad = logit_grad + dispatch * (grad - jnp.sum(dispatch * grad, axis=0, keepdims=True))
@@ -143,8 +180,9 @@
             jax.ShapeDtypeStruct((patches, slots), LOW),
             jax.ShapeDtypeStruct((width, slots), LOW),
         ),
-        in_specs=in_vmem(5),
+        in_specs=in_vmem(1) + in_hbm(2) + in_vmem(2),
         out_specs=tuple(in_vmem(3)),
+        scratch_shapes=buffers_for(tokens, cotangent),
         compiler_params=pltpu.CompilerParams(vmem_limit_bytes=VMEM_BYTES),
         cost_estimate=cost(6 * patches * width * slots, 4 * patches * width),
     )(shares, tokens, cotangent, dispatch, combine)

time: 176 us -> 175 us (level)
  local copies, waits for them, and re-layouts: 8.95 us -> 5.56 us
    unnamed x18 -> x14, local copies, waits for them, and re-layouts: 4.56 us -> 2.33 us
    pallas_call x1, Pallas kernels: 0.72 us -> 2.54 us  [routing(): pl.pallas_call(routing_kernel, out_shape=(weights, weights, rows, rows),...]
where the time goes in v7:
time: 175 us
  blocking collectives  146 us (83%)
  Pallas kernels  11 us (6%)
  local copies, waits for them, and re-layouts  5.56 us (3%)
  starting transfers between devices  5.25 us (3%)
  waiting for transfers between devices  4.77 us (3%)
  other arithmetic  1.85 us (1%)
    all_to_all x4, blocking collectives, all_to_all(): return lax.all_to_all(value, axes, split_axis=0, concat_axis=0, tiled=True)  146 us
    all_to_all x1, starting transfers between devices, all_to_all(): return lax.all_to_all(value, axes, split_axis=0, concat_axis=0, tiled=True)  5.25 us
    all_to_all x1, waiting for transfers between devices, all_to_all(): return lax.all_to_all(value, axes, split_axis=0, concat_axis=0, tiled=True)  4.77 us
    pallas_call x1, Pallas kernels, expert_rows(): pl.pallas_call(expert_kernel, out_shape=(jax.ShapeDtypeStruct(rows.shape,...  3.82 us
  transfers between devices with their start and end apart: 1, of which 1 were waited for; matrix products, arithmetic and copies ran while one was open for 0% of the time, Pallas kernels for 2%

profile of v7, /device:TPU:1, one launch (start us, length us, event | category | flops | bytes accessed | tf_op | source)
XLA Modules:
  0.0 175.0 jit_solution(12388056671240475696)
XLA Ops:
  0.6 2.5 %shard_map.76 = (f32[196,128]{1,0:T(8,128)}, f32[196,128]{1,0:T(8,128)}, bf16[128,768]{1,0:T(8,128)(2,1)}, bf16[128,768]{1,0:T(8,128)(2,1)}) custom-call(bf16[196,768]{1,0:T(8,128)(2,1)} %bitcast.23, bf16[768,128]{1,0:T(8,128)(2,1)} %router_ref.1, bf16[196,768]{1,0:T(8,128)(2,1)} %bitcast.25), custom_call_target="tpu_custom_call" | custom-call | flops 115605504 | bytes 602112 | tf_op jit(solution)/shard_map/pallas_call | solution.py:80
  3.2 1.1 pad_maximum_fusion
  4.2 0.4 copy.8
  4.7 0.8 broadcast_in_dim.12
  5.5 66.4 %all_to_all.25 = bf16[512,2,768]{2,1,0:T(2,128)(2,1)S(1)} all-to-all(bf16[512,2,768]{2,1,0:T(2,128)(2,1)S(1)} %bitcast.31), channel_id=1, replica_groups=mesh['dp'=4,'yl'=2,'x'=4,'zh'=4,'zl'=2,'core'=2] {'dp','yl','x','zh','zl..., dimensions={0} | all-to-all | bytes 3145728 | tf_op jit(solution)/shard_map/all_to_all | solution.py:225
  71.8 0.0 copy-start.5
  71.8 0.0 copy-start.6
  71.8 0.2 copy.13
  72.0 1.1 copy-done.5
  73.1 0.4 copy-done.6
  73.5 3.8 %shard_map.77 = (bf16[2,512,768]{2,1,0:T(8,128)(2,1)S(1)}, bf16[512,768]{1,0:T(8,128)(2,1)S(1)}) custom-call(bf16[2,512,768]{2,1,0:T(8,128)(2,1)S(1)} %bitcast.19, bf16[768,768]{1,0:T(8,128)(2,1)S(1)} %bitcast.28, bf16[768,768]{1,0:T(8,128)(2,1)S(1)} %bitcast.29), custom_call_target="tpu_custom_call" | custom-call | flops 2415919104 | bytes 6291456 | tf_op jit(solution)/shard_map/pallas_call | solution.py:115
  77.3 1.6 copy.10
  78.9 52.7 %all_to_all.26 = bf16[512,2,768]{2,1,0:T(2,128)(2,1)S(1)} all-to-all(bf16[512,2,768]{2,1,0:T(2,128)(2,1)S(1)} %copy.10), channel_id=1, replica_groups=mesh['dp'=4,'yl'=2,'x'=4,'zh'=4,'zl'=2,'core'=2] {'dp','yl','x','zh','zl..., dimensions={0} | all-to-all | bytes 3145728 | tf_op jit(solution)/shard_map/all_to_all | solution.py:225
  131.7 0.0 copy-start
  131.7 0.0 copy-start.1
  131.7 0.0 copy-start.3
  131.7 0.0 copy-start.4
  131.7 0.2 copy.11
  131.9 0.8 copy-done
  132.6 0.1 copy-done.1
  132.7 0.0 copy-done.3
  132.7 0.0 copy-done.4
  132.8 1.0 shard_map.78
  133.8 11.5 %all_to_all.27.parts_ref = bf16[32,24,128]{2,1,0:T(8,128)(2,1)S(1)} all-to-all(bf16[32,24,128]{2,1,0:T(8,128)(2,1)S(1)} %bitcast.27), channel_id=1, replica_groups=mesh['dp'=4,'yl'=2,'x'=4,'zh'=4,'zl'=2,'core'=2] {'yl','x','zl','core'}, dimensions={0} | all-to-all | bytes 393216 | tf_op jit(solution)/shard_map/all_to_all | solution.py:225
  145.4 15.2 %all_to_all.28.parts_ref = bf16[16,24,128]{2,1,0:T(8,128)(2,1)S(1)} all-to-all(bf16[16,24,128]{2,1,0:T(8,128)(2,1)S(1)} %shard_map.80), channel_id=1, replica_groups=mesh['dp'=4,'yl'=2,'x'=4,'zh'=4,'zl'=2,'core'=2] {'dp','zh'}, dimensions={0} | all-to-all | bytes 196608 | tf_op jit(solution)/shard_map/all_to_all | solution.py:225
  160.6 0.7 shard_map.81
  161.3 5.2 %all-to-all-start.4 = ((bf16[32,24,128]{2,1,0:T(8,128)(2,1)}), bf16[32,24,128]{2,1,0:T(8,128)(2,1)S(1)}, u32[]{:S(2)}, u32[]{:S(2)}) async-start(bf16[32,24,128]{2,1,0:T(8,128)(2,1)} %shard_map.81), calls=%async_computation.4 | async-start | bytes 393216 | tf_op jit(solution)/shard_map/all_to_all | solution.py:225
  166.6 0.0 copy-start.2
  166.6 1.8 %shard_map.82 = bf16[768,768]{1,0:T(8,128)(2,1)} custom-call(bf16[512,768]{1,0:T(8,128)(2,1)S(1)} %get-tuple-element.20.act_ref, bf16[2,512,768]{2,1,0:T(8,128)(2,1)S(1)} %bitcast.20), custom_call_target="tpu_custom_call" | custom-call | flops 603979776 | bytes 1179648 | tf_op jit(solution)/shard_map/pallas_call | solution.py:136
  168.4 0.0 copy-done.2
  168.4 1.0 shard_map.79
  169.5 4.8 %all-to-all-done.4 = bf16[32,24,128]{2,1,0:T(8,128)(2,1)S(1)} async-done(((bf16[32,24,128]{2,1,0:T(8,128)(2,1)}), bf16[32,24,128]{2,1,0:T(8,128)(2,1)S(1)}, u32[]{:S(2)}, u32[]{:S(2)}) %all-to-all-start.4) | async-done | bytes 196640 | tf_op jit(solution)/shard_map/all_to_all | solution.py:225
  174.2 0.8 bitcast_convert_fusion
  (1 shorter events, 0.0 us)
Async XLA Ops:
  71.8 1.3 copy-start.5
  71.8 1.6 copy-start.6
  131.7 1.0 copy-start
  131.7 1.1 copy-start.1
  131.7 1.1 copy-start.3
  131.7 1.1 copy-start.4
  161.3 12.9 %all-to-all-start.4 = ((bf16[32,24,128]{2,1,0:T(8,128)(2,1)}), bf16[32,24,128]{2,1,0:T(8,128)(2,1)S(1)}, u32[]{:S(2)}, u32[]{:S(2)}) async-start(bf16[32,24,128]{2,1,0:T(8,128)(2,1)} %shard_map.81), calls=%async_computation.4 | async-start | bytes 393216 | tf_op jit(solution)/shard_map/all_to_all | solution.py:225
  166.6 1.9 %copy-start.2 = (bf16[768,128]{1,0:T(8,128)(2,1)S(1)}, bf16[768,128]{1,0:T(8,128)(2,1)}, u32[]{:S(2)}) copy-start(bf16[768,128]{1,0:T(8,128)(2,1)} %router_ref.1) | copy-start | bytes 589828

commit v8 on v7

--- a/solution.py
+++ b/solution.py
@@ -19,6 +19,7 @@
 NEAR = ("yl", "x", "zl", "core")
 REST = ("dp", "zh")
 VMEM_BYTES = 20 * 2**20
+WHOLE_BYTES = 61 * 2**20
 
 
 def wide_dot(left, right, left_dim, right_dim):
@@ -51,7 +52,7 @@
 
 
 def routing_kernel(
-    tokens_hbm, router_hbm, cotangent_hbm, dispatch_ref, combine_ref, inputs_ref, grads_ref,
+    tokens_hbm, router_hbm, cotangent_hbm, dispatch_ref, combine_ref, rows_ref,
     tokens_ref, router_ref, cotangent_ref, sems,
 ):
     copies = fetch(
@@ -64,42 +65,38 @@
     powers = jnp.exp(logits - jnp.max(logits, axis=0, keepdims=True))
     dispatch = powers / jnp.sum(powers, axis=0, keepdims=True)
     dispatch_ref[...] = dispatch
-    inputs_ref[...] = wide_dot(dispatch.astype(LOW), tokens, 0, 0).astype(LOW)
+    rows_ref[0] = wide_dot(dispatch.astype(LOW), tokens, 0, 0).astype(LOW)
     powers = jnp.exp(logits - jnp.max(logits, axis=1, keepdims=True))
     combine = powers / jnp.sum(powers, axis=1, keepdims=True)
     combine_ref[...] = combine
     copies[2].wait()
-    grads_ref[...] = wide_dot(combine.astype(LOW), cotangent_ref[...], 0, 0).astype(LOW)
+    rows_ref[1] = wide_dot(combine.astype(LOW), cotangent_ref[...], 0, 0).astype(LOW)
 
 
 def routing(tokens, router, cotangent):
     patches, width = tokens.shape
     slots = router.shape[1]
     weights = jax.ShapeDtypeStruct((patches, slots), WIDE)
-    rows = jax.ShapeDtypeStruct((slots, width), LOW)
+    rows = jax.ShapeDtypeStruct((2, slots, width), LOW)
     return pl.pallas_call(
         routing_kernel,
-        out_shape=(weights, weights, rows, rows),
+        out_shape=(weights, weights, rows),
         in_specs=in_hbm(3),
-        out_specs=tuple(in_vmem(4)),
+        out_specs=tuple(in_vmem(3)),
         scratch_shapes=buffers_for(tokens, router, cotangent),
-        compiler_params=pltpu.CompilerParams(vmem_limit_bytes=61 * 2**20),
+        compiler_params=pltpu.CompilerParams(vmem_limit_bytes=WHOLE_BYTES),
         cost_estimate=cost(6 * patches * width * slots, 4 * patches * width),
     )(tokens, router, cotangent)
 
 
-def expert_kernel(rows_ref, up_hbm, down_hbm, share_ref, act_ref, up_ref, down_ref, sems):
-    copies = fetch((up_hbm, down_hbm), (up_ref, down_ref), sems)
-    copies[0].wait()
-    up = up_ref[...]
+def expert_kernel(rows_ref, up_ref, down_ref, share_ref, act_ref):
+    up, down = up_ref[...], down_ref[...]
     hidden_pre = wide_dot(rows_ref[0], up, 1, 0)
     squared = hidden_pre * hidden_pre
     inner = jnp.tanh(GELU_SCALE * (hidden_pre + GELU_CUBIC * squared * hidden_pre))
     half = 0.5 * (1.0 + inner)
     activation = (hidden_pre * half).astype(LOW)
     act_ref[...] = activation
-    copies[1].wait()
-    down = down_ref[...]
     share_ref[0] = wide_dot(activation, down, 1, 0).astype(LOW)
     slope = half + 0.5 * hidden_pre * (1.0 - inner * inner) * (
         GELU_SCALE + 3.0 * GELU_SCALE * GELU_CUBIC * squared
@@ -118,9 +115,8 @@
             jax.ShapeDtypeStruct(rows.shape, LOW),
             jax.ShapeDtypeStruct((count, hidden), LOW),
         ),
-        in_specs=in_vmem(1) + in_hbm(2),
+        in_specs=in_vmem(3),
         out_specs=tuple(in_vmem(2)),
-        scratch_shapes=buffers_for(up, down),
         compiler_params=pltpu.CompilerParams(vmem_limit_bytes=VMEM_BYTES),
         cost_estimate=cost(8 * count * width * hidden, 4 * width * hidden + 10 * count * width),
     )(rows, up, down)
@@ -144,10 +140,8 @@
 
 
 def logit_kernel(
-    shares_ref, tokens_hbm, cotangent_hbm, dispatch_ref, combine_ref, inputs_ref, logit_ref, term_ref,
-    tokens_ref, cotangent_ref, sems,
+    shares_ref, tokens_ref, cotangent_ref, dispatch_ref, combine_ref, inputs_ref, logit_ref, term_ref
 ):
-    copies = fetch((tokens_hbm, cotangent_hbm), (tokens_ref, cotangent_ref), sems)
     slabs = shares_ref.shape[1]
 
     def total(route):
@@ -157,11 +151,8 @@
     dispatch, combine = dispatch_ref[...], combine_ref[...]
     input_grads = total(1)
     inputs_ref[...] = input_grads
-    slot_outputs = total(0)
-    copies[0].wait()
-    copies[1].wait()
     tokens = tokens_ref[...]
-    grad = wide_dot(cotangent_ref[...], slot_outputs, 1, 1)
+    grad = wide_dot(cotangent_ref[...], total(0), 1, 1)
     logit_grad = combine * (grad - jnp.sum(combine * grad, axis=1, keepdims=True))
     grad = wide_dot(tokens, input_grads, 1, 1)
     logit_grad = logit_grad + dispatch * (grad - jnp.sum(dispatch * grad, axis=0, keepdims=True))
@@ -180,9 +171,8 @@
             jax.ShapeDtypeStruct((patches, slots), LOW),
             jax.ShapeDtypeStruct((width, slots), LOW),
         ),
-        in_specs=in_vmem(1) + in_hbm(2) + in_vmem(2),
+        in_specs=in_vmem(5),
         out_specs=tuple(in_vmem(3)),
-        scratch_shapes=buffers_for(tokens, cotangent),
         compiler_params=pltpu.CompilerParams(vmem_limit_bytes=VMEM_BYTES),
         cost_estimate=cost(6 * patches * width * slots, 4 * patches * width),
     )(shares, tokens, cotangent, dispatch, combine)
@@ -238,14 +228,15 @@
     up, down = up_weight[0], down_weight[0]
     slabs = lax.axis_size("dp")
 
-    dispatch, combine, slot_inputs, slot_cotangent = routing(tokens, router, cotangent)
-    sent = jnp.stack([slot_inputs, slot_cotangent], axis=1)
+    dispatch, combine, slot_rows = routing(tokens, router, cotangent)
+
+    sent = jnp.swapaxes(slot_rows, 0, 1)
     copies = jnp.broadcast_to(sent[None], (slabs,) + sent.shape).reshape((-1,) + sent.shape[1:])
     rows = jnp.swapaxes(all_to_all(copies, EVERY), 0, 1)
     shares, act = expert_rows(rows, up, down)
     grad_down = outer_sum(act, rows)
     back = jnp.swapaxes(all_to_all(jnp.swapaxes(shares, 0, 1), EVERY), 0, 1)
-    back = back.reshape((2, slabs) + slot_inputs.shape)
+    back = back.reshape((2, slabs) + slot_rows.shape[1:])
     input_grads, logit_low, term = logit_grads(back, tokens, cotangent, dispatch, combine)
     grad_router = sum_everywhere(term)
     grad_tokens = token_grads(dispatch, input_grads, logit_low, router)

time: 175 us -> 174 us (level)
  no operation moved by 1% of the time
where the time goes in v8:
time: 174 us
  blocking collectives  146 us (84%)
  Pallas kernels  9.91 us (6%)
  local copies, waits for them, and re-layouts  6.56 us (4%)
  starting transfers between devices  5.25 us (3%)
  waiting for transfers between devices  4.78 us (3%)
    all_to_all x4, blocking collectives, all_to_all(): return lax.all_to_all(value, axes, split_axis=0, concat_axis=0, tiled=True)  146 us
    all_to_all x1, starting transfers between devices, all_to_all(): return lax.all_to_all(value, axes, split_axis=0, concat_axis=0, tiled=True)  5.25 us
    all_to_all x1, waiting for transfers between devices, all_to_all(): return lax.all_to_all(value, axes, split_axis=0, concat_axis=0, tiled=True)  4.78 us
  transfers between devices with their start and end apart: 1, of which 1 were waited for; matrix products, arithmetic and copies ran while one was open for 0% of the time, Pallas kernels for 2%

profile of v8, /device:TPU:1, one launch (start us, length us, event | category | flops | bytes accessed | tf_op | source)
XLA Modules:
  0.0 173.8 jit_solution(2568232002390641408)
XLA Ops:
  0.6 2.6 %shard_map.76 = (f32[196,128]{1,0:T(8,128)}, f32[196,128]{1,0:T(8,128)}, bf16[2,128,768]{2,1,0:T(8,128)(2,1)}) custom-call(bf16[196,768]{1,0:T(8,128)(2,1)} %bitcast.22, bf16[768,128]{1,0:T(8,128)(2,1)} %router_ref.1, bf16[196,768]{1,0:T(8,128)(2,1)} %bitcast.24), custom_call_target="tpu_custom_call" | custom-call | flops 115605504 | bytes 602112 | tf_op jit(solution)/shard_map/pallas_call | solution.py:81
  3.2 1.4 copy.8
  4.7 0.8 broadcast_in_dim.12
  5.5 66.4 %all_to_all.25 = bf16[512,2,768]{2,1,0:T(2,128)(2,1)S(1)} all-to-all(bf16[512,2,768]{2,1,0:T(2,128)(2,1)S(1)} %bitcast.30), channel_id=1, replica_groups=mesh['dp'=4,'yl'=2,'x'=4,'zh'=4,'zl'=2,'core'=2] {'dp','yl','x','zh','zl..., dimensions={0} | all-to-all | bytes 3145728 | tf_op jit(solution)/shard_map/all_to_all | solution.py:215
  71.8 0.0 copy-start.5
  71.8 0.0 copy-start.6
  71.8 0.2 copy.13
  72.0 1.1 copy-done.5
  73.1 0.4 copy-done.6
  73.5 2.9 %shard_map.77 = (bf16[2,512,768]{2,1,0:T(8,128)(2,1)S(1)}, bf16[512,768]{1,0:T(8,128)(2,1)S(1)}) custom-call(bf16[2,512,768]{2,1,0:T(8,128)(2,1)S(1)} %bitcast.18, bf16[768,768]{1,0:T(8,128)(2,1)S(1)} %bitcast.27, bf16[768,768]{1,0:T(8,128)(2,1)S(1)} %bitcast.28), custom_call_target="tpu_custom_call" | custom-call | flops 2415919104 | bytes 6291456 | tf_op jit(solution)/shard_map/pallas_call | solution.py:112
  76.4 1.6 copy.10
  78.0 52.7 %all_to_all.26 = bf16[512,2,768]{2,1,0:T(2,128)(2,1)S(1)} all-to-all(bf16[512,2,768]{2,1,0:T(2,128)(2,1)S(1)} %copy.10), channel_id=1, replica_groups=mesh['dp'=4,'yl'=2,'x'=4,'zh'=4,'zl'=2,'core'=2] {'dp','yl','x','zh','zl..., dimensions={0} | all-to-all | bytes 3145728 | tf_op jit(solution)/shard_map/all_to_all | solution.py:215
  130.8 0.0 copy-start
  130.8 0.0 copy-start.1
  130.8 0.0 copy-start.3
  130.8 0.0 copy-start.4
  130.8 0.2 copy.11
  131.0 0.8 copy-done
  131.7 0.1 copy-done.1
  131.8 0.0 copy-done.3
  131.8 0.0 copy-done.4
  131.9 0.7 shard_map.78
  132.6 11.5 %all_to_all.27.parts_ref = bf16[32,24,128]{2,1,0:T(8,128)(2,1)S(1)} all-to-all(bf16[32,24,128]{2,1,0:T(8,128)(2,1)S(1)} %bitcast.26), channel_id=1, replica_groups=mesh['dp'=4,'yl'=2,'x'=4,'zh'=4,'zl'=2,'core'=2] {'yl','x','zl','core'}, dimensions={0} | all-to-all | bytes 393216 | tf_op jit(solution)/shard_map/all_to_all | solution.py:215
  144.1 15.2 %all_to_all.28.parts_ref = bf16[16,24,128]{2,1,0:T(8,128)(2,1)S(1)} all-to-all(bf16[16,24,128]{2,1,0:T(8,128)(2,1)S(1)} %shard_map.80), channel_id=1, replica_groups=mesh['dp'=4,'yl'=2,'x'=4,'zh'=4,'zl'=2,'core'=2] {'dp','zh'}, dimensions={0} | all-to-all | bytes 196608 | tf_op jit(solution)/shard_map/all_to_all | solution.py:215
  159.4 0.7 shard_map.81
  160.1 5.2 %all-to-all-start.4 = ((bf16[32,24,128]{2,1,0:T(8,128)(2,1)}), bf16[32,24,128]{2,1,0:T(8,128)(2,1)S(1)}, u32[]{:S(2)}, u32[]{:S(2)}) async-start(bf16[32,24,128]{2,1,0:T(8,128)(2,1)} %shard_map.81), calls=%async_computation.4 | async-start | bytes 393216 | tf_op jit(solution)/shard_map/all_to_all | solution.py:215
  165.3 0.0 copy-start.2
  165.4 1.8 %shard_map.82 = bf16[768,768]{1,0:T(8,128)(2,1)} custom-call(bf16[512,768]{1,0:T(8,128)(2,1)S(1)} %get-tuple-element.18.act_ref, bf16[2,512,768]{2,1,0:T(8,128)(2,1)S(1)} %bitcast.19), custom_call_target="tpu_custom_call" | custom-call | flops 603979776 | bytes 1179648 | tf_op jit(solution)/shard_map/pallas_call | solution.py:132
  167.2 0.0 copy-done.2
  167.2 1.0 shard_map.79
  168.2 4.8 %all-to-all-done.4 = bf16[32,24,128]{2,1,0:T(8,128)(2,1)S(1)} async-done(((bf16[32,24,128]{2,1,0:T(8,128)(2,1)}), bf16[32,24,128]{2,1,0:T(8,128)(2,1)S(1)}, u32[]{:S(2)}, u32[]{:S(2)}) %all-to-all-start.4) | async-done | bytes 196640 | tf_op jit(solution)/shard_map/all_to_all | solution.py:215
  173.0 0.8 bitcast_convert_fusion
  (1 shorter events, 0.0 us)
Async XLA Ops:
  71.8 1.3 copy-start.5
  71.8 1.6 copy-start.6
  130.8 1.0 copy-start
  130.8 1.1 copy-start.1
  130.8 1.1 copy-start.3
  130.8 1.1 copy-start.4
  160.1 12.9 %all-to-all-start.4 = ((bf16[32,24,128]{2,1,0:T(8,128)(2,1)}), bf16[32,24,128]{2,1,0:T(8,128)(2,1)S(1)}, u32[]{:S(2)}, u32[]{:S(2)}) async-start(bf16[32,24,128]{2,1,0:T(8,128)(2,1)} %shard_map.81), calls=%async_computation.4 | async-start | bytes 393216 | tf_op jit(solution)/shard_map/all_to_all | solution.py:215
  165.3 1.9 %copy-start.2 = (bf16[768,128]{1,0:T(8,128)(2,1)S(1)}, bf16[768,128]{1,0:T(8,128)(2,1)}, u32[]{:S(2)}) copy-start(bf16[768,128]{1,0:T(8,128)(2,1)} %router_ref.1) | copy-start | bytes 589828

commit v9 on v8

--- a/solution.py
+++ b/solution.py
@@ -197,14 +197,14 @@
 
 
 def total_kernel(parts_ref, copies_ref):
-    total = jnp.sum(parts_ref[...].astype(WIDE), axis=0).astype(LOW)
+    total = jnp.sum(parts_ref[...].astype(WIDE), axis=0).astype(copies_ref.dtype)
     copies_ref[...] = jnp.broadcast_to(total[None], copies_ref.shape)
 
 
-def total_copies(parts, copies):
+def total_copies(parts, copies, kind):
     return pl.pallas_call(
         total_kernel,
-        out_shape=jax.ShapeDtypeStruct((copies,) + parts.shape[1:], LOW),
+        out_shape=jax.ShapeDtypeStruct((copies,) + parts.shape[1:], kind),
         in_specs=in_vmem(1),
         out_specs=in_vmem(1)[0],
         compiler_params=pltpu.CompilerParams(vmem_limit_bytes=VMEM_BYTES),
@@ -219,8 +219,8 @@
     near = lax.axis_size(NEAR)
     depth, width = term.shape
     parts = all_to_all(term.reshape(near, depth // near, width), NEAR)
-    parts = all_to_all(total_copies(parts, lax.axis_size(REST)), REST)
-    return all_to_all(total_copies(parts, near), NEAR).reshape(depth, width).astype(WIDE)
+    parts = all_to_all(total_copies(parts, lax.axis_size(REST), WIDE), REST)
+    return all_to_all(total_copies(parts, near, LOW), NEAR).reshape(depth, width).astype(WIDE)
 
 
 def shards(tokens, router, up_weight, down_weight, cotangent):

time: 174 us -> 175 us (level)
  no operation moved by 1% of the time
where the time goes in v9:
time: 175 us; the launch traced here: 174 us
  blocking collectives  146 us (83%)
  Pallas kernels  9.91 us (6%)
  local copies, waits for them, and re-layouts  6.56 us (4%)
  starting transfers between devices  5.74 us (3%)
  waiting for transfers between devices  4.66 us (3%)
    all_to_all x4, blocking collectives, all_to_all(): return lax.all_to_all(value, axes, split_axis=0, concat_axis=0, tiled=True)  146 us
    all_to_all x1, starting transfers between devices, all_to_all(): return lax.all_to_all(value, axes, split_axis=0, concat_axis=0, tiled=True)  5.74 us
    all_to_all x1, waiting for transfers between devices, all_to_all(): return lax.all_to_all(value, axes, split_axis=0, concat_axis=0, tiled=True)  4.66 us
  transfers between devices with their start and end apart: 1, of which 1 were waited for; matrix products, arithmetic and copies ran while one was open for 0% of the time, Pallas kernels for 2%

profile of v9, /device:TPU:1, one launch (start us, length us, event | category | flops | bytes accessed | tf_op | source)
XLA Modules:
  0.0 174.5 jit_solution(6330511818083023301)
XLA Ops:
  0.6 2.6 %shard_map.76 = (f32[196,128]{1,0:T(8,128)}, f32[196,128]{1,0:T(8,128)}, bf16[2,128,768]{2,1,0:T(8,128)(2,1)}) custom-call(bf16[196,768]{1,0:T(8,128)(2,1)} %bitcast.22, bf16[768,128]{1,0:T(8,128)(2,1)} %router_ref.1, bf16[196,768]{1,0:T(8,128)(2,1)} %bitcast.24), custom_call_target="tpu_custom_call" | custom-call | flops 115605504 | bytes 602112 | tf_op jit(solution)/shard_map/pallas_call | solution.py:81
  3.2 1.4 copy.8
  4.7 0.8 broadcast_in_dim.12
  5.5 66.4 %all_to_all.25 = bf16[512,2,768]{2,1,0:T(2,128)(2,1)S(1)} all-to-all(bf16[512,2,768]{2,1,0:T(2,128)(2,1)S(1)} %bitcast.30), channel_id=1, replica_groups=mesh['dp'=4,'yl'=2,'x'=4,'zh'=4,'zl'=2,'core'=2] {'dp','yl','x','zh','zl..., dimensions={0} | all-to-all | bytes 3145728 | tf_op jit(solution)/shard_map/all_to_all | solution.py:215
  71.8 0.0 copy-start.5
  71.8 0.0 copy-start.6
  71.8 0.2 copy.13
  72.0 1.1 copy-done.5
  73.1 0.4 copy-done.6
  73.5 2.9 %shard_map.77 = (bf16[2,512,768]{2,1,0:T(8,128)(2,1)S(1)}, bf16[512,768]{1,0:T(8,128)(2,1)S(1)}) custom-call(bf16[2,512,768]{2,1,0:T(8,128)(2,1)S(1)} %bitcast.18, bf16[768,768]{1,0:T(8,128)(2,1)S(1)} %bitcast.27, bf16[768,768]{1,0:T(8,128)(2,1)S(1)} %bitcast.28), custom_call_target="tpu_custom_call" | custom-call | flops 2415919104 | bytes 6291456 | tf_op jit(solution)/shard_map/pallas_call | solution.py:112
  76.4 1.6 copy.10
  78.0 52.7 %all_to_all.26 = bf16[512,2,768]{2,1,0:T(2,128)(2,1)S(1)} all-to-all(bf16[512,2,768]{2,1,0:T(2,128)(2,1)S(1)} %copy.10), channel_id=1, replica_groups=mesh['dp'=4,'yl'=2,'x'=4,'zh'=4,'zl'=2,'core'=2] {'dp','yl','x','zh','zl..., dimensions={0} | all-to-all | bytes 3145728 | tf_op jit(solution)/shard_map/all_to_all | solution.py:215
  130.8 0.0 copy-start
  130.8 0.0 copy-start.1
  130.8 0.0 copy-start.3
  130.8 0.0 copy-start.4
  130.8 0.2 copy.11
  131.0 0.8 copy-done
  131.7 0.1 copy-done.1
  131.8 0.0 copy-done.3
  131.8 0.0 copy-done.4
  131.9 0.7 shard_map.78
  132.6 11.5 %all_to_all.27.parts_ref = bf16[32,24,128]{2,1,0:T(8,128)(2,1)S(1)} all-to-all(bf16[32,24,128]{2,1,0:T(8,128)(2,1)S(1)} %bitcast.26), channel_id=1, replica_groups=mesh['dp'=4,'yl'=2,'x'=4,'zh'=4,'zl'=2,'core'=2] {'yl','x','zl','core'}, dimensions={0} | all-to-all | bytes 393216 | tf_op jit(solution)/shard_map/all_to_all | solution.py:215
  144.1 15.5 %all_to_all.28.parts_ref = f32[16,24,128]{2,1,0:T(8,128)S(1)} all-to-all(f32[16,24,128]{2,1,0:T(8,128)S(1)} %shard_map.80), channel_id=1, replica_groups=mesh['dp'=4,'yl'=2,'x'=4,'zh'=4,'zl'=2,'core'=2] {'dp','zh'}, dimensions={0} | all-to-all | bytes 393216 | tf_op jit(solution)/shard_map/all_to_all | solution.py:215
  159.7 0.7 shard_map.81
  160.4 5.7 %all-to-all-start.4 = ((bf16[32,24,128]{2,1,0:T(8,128)(2,1)}), bf16[32,24,128]{2,1,0:T(8,128)(2,1)S(1)}, u32[]{:S(2)}, u32[]{:S(2)}) async-start(bf16[32,24,128]{2,1,0:T(8,128)(2,1)} %shard_map.81), calls=%async_computation.4 | async-start | bytes 393216 | tf_op jit(solution)/shard_map/all_to_all | solution.py:215
  166.1 0.0 copy-start.2
  166.1 1.8 %shard_map.82 = bf16[768,768]{1,0:T(8,128)(2,1)} custom-call(bf16[512,768]{1,0:T(8,128)(2,1)S(1)} %get-tuple-element.18.act_ref, bf16[2,512,768]{2,1,0:T(8,128)(2,1)S(1)} %bitcast.19), custom_call_target="tpu_custom_call" | custom-call | flops 603979776 | bytes 1179648 | tf_op jit(solution)/shard_map/pallas_call | solution.py:132
  168.0 0.0 copy-done.2
  168.0 1.0 shard_map.79
  169.0 4.7 %all-to-all-done.4 = bf16[32,24,128]{2,1,0:T(8,128)(2,1)S(1)} async-done(((bf16[32,24,128]{2,1,0:T(8,128)(2,1)}), bf16[32,24,128]{2,1,0:T(8,128)(2,1)S(1)}, u32[]{:S(2)}, u32[]{:S(2)}) %all-to-all-start.4) | async-done | bytes 196640 | tf_op jit(solution)/shard_map/all_to_all | solution.py:215
  173.7 0.8 bitcast_convert_fusion
  (1 shorter events, 0.0 us)
Async XLA Ops:
  71.8 1.3 copy-start.5
  71.8 1.6 copy-start.6
  130.8 1.0 copy-start
  130.8 1.1 copy-start.1
  130.8 1.1 copy-start.3
  130.8 1.1 copy-start.4
  160.4 13.3 %all-to-all-start.4 = ((bf16[32,24,128]{2,1,0:T(8,128)(2,1)}), bf16[32,24,128]{2,1,0:T(8,128)(2,1)S(1)}, u32[]{:S(2)}, u32[]{:S(2)}) async-start(bf16[32,24,128]{2,1,0:T(8,128)(2,1)} %shard_map.81), calls=%async_computation.4 | async-start | bytes 393216 | tf_op jit(solution)/shard_map/all_to_all | solution.py:215
  166.1 1.9 %copy-start.2 = (bf16[768,128]{1,0:T(8,128)(2,1)S(1)}, bf16[768,128]{1,0:T(8,128)(2,1)}, u32[]{:S(2)}) copy-start(bf16[768,128]{1,0:T(8,128)(2,1)} %router_ref.1) | copy-start | bytes 589828

commit v10 on v9

--- a/solution.py
+++ b/solution.py
@@ -18,6 +18,8 @@
 EVERY = ("dp",) + EXPERT
 NEAR = ("yl", "x", "zl", "core")
 REST = ("dp", "zh")
+COLUMN = ("dp", "yl", "core")
+HOSTS = ("dp", "yl", "x", "zh", "zl")
 VMEM_BYTES = 20 * 2**20
 WHOLE_BYTES = 61 * 2**20
 
@@ -97,22 +99,22 @@
     half = 0.5 * (1.0 + inner)
     activation = (hidden_pre * half).astype(LOW)
     act_ref[...] = activation
-    share_ref[0] = wide_dot(activation, down, 1, 0).astype(LOW)
+    share_ref[0] = wide_dot(activation, down, 1, 0).astype(share_ref.dtype)
     slope = half + 0.5 * hidden_pre * (1.0 - inner * inner) * (
         GELU_SCALE + 3.0 * GELU_SCALE * GELU_CUBIC * squared
     )
     upstream = wide_dot(rows_ref[1], down, 1, 1)
     hidden_grad = (upstream * slope).astype(LOW)
-    share_ref[1] = wide_dot(hidden_grad, up, 1, 1).astype(LOW)
-
-
-def expert_rows(rows, up, down):
+    share_ref[1] = wide_dot(hidden_grad, up, 1, 1).astype(share_ref.dtype)
+
+
+def expert_rows(rows, up, down, kind):
     _, count, width = rows.shape
     hidden = up.shape[1]
     return pl.pallas_call(
         expert_kernel,
         out_shape=(
-            jax.ShapeDtypeStruct(rows.shape, LOW),
+            jax.ShapeDtypeStruct(rows.shape, kind),
             jax.ShapeDtypeStruct((count, hidden), LOW),
         ),
         in_specs=in_vmem(3),
@@ -122,21 +124,22 @@
     )(rows, up, down)
 
 
-def outer_kernel(act_ref, rows_ref, grad_ref):
-    grad_ref[...] = wide_dot(act_ref[...], rows_ref[1], 0, 0).astype(LOW)
-
-
-def outer_sum(act, rows):
+def outer_kernel(act_ref, rows_ref, other_act_ref, other_rows_ref, grad_ref):
+    total = wide_dot(act_ref[...], rows_ref[1], 0, 0)
+    grad_ref[...] = (total + wide_dot(other_act_ref[...], other_rows_ref[1], 0, 0)).astype(LOW)
+
+
+def outer_sum(act, rows, other_act, other_rows):
     count, hidden = act.shape
     width = rows.shape[2]
     return pl.pallas_call(
         outer_kernel,
         out_shape=jax.ShapeDtypeStruct((hidden, width), LOW),
-        in_specs=in_vmem(2),
+        in_specs=in_vmem(4),
         out_specs=in_vmem(1)[0],
         compiler_params=pltpu.CompilerParams(vmem_limit_bytes=VMEM_BYTES),
-        cost_estimate=cost(2 * count * width * hidden, 2 * hidden * width),
-    )(act, rows)
+        cost_estimate=cost(4 * count * width * hidden, 2 * hidden * width),
+    )(act, rows, other_act, other_rows)
 
 
 def logit_kernel(
@@ -223,20 +226,61 @@
     return all_to_all(total_copies(parts, near, LOW), NEAR).reshape(depth, width).astype(WIDE)
 
 
+def host_moves():
+    moves = []
+    for slab in range(4):
+        for yl in range(2):
+            for core in range(2):
+                place = 2 * slab + yl
+                onward = (slab + core) % 2 == 0
+                host = (place + (1 if onward else -1)) % 8
+                moves.append((2 * place + core, 2 * host + (0 if onward else 1)))
+    return moves
+
+
+def move(value, moves):
+    return lax.ppermute(value, COLUMN, moves)
+
+
+def swap_cores(value):
+    return lax.ppermute(value, "core", [(0, 1), (1, 0)])
+
+
+def to_hosts(rows):
+    _, routes, width = rows.shape
+    placed = rows.reshape(2, -1, 2, routes, width)
+    even = jnp.stack([placed[1, :, 1], placed[0, :, 0]])
+    odd = jnp.stack([placed[1, :, 0], placed[0, :, 1]])
+    return jnp.stack([even, odd, even, odd]).reshape(-1, routes, width)
+
+
+def from_hosts(rows):
+    _, routes, width = rows.shape
+    hosted = rows.reshape(2, 2, 2, -1, routes, width)
+    shares = jnp.stack([hosted[:, :, 1], hosted[:, ::-1, 0]], axis=1)
+    return shares.transpose(4, 0, 1, 3, 2, 5).reshape(routes, 2, -1, width)
+
+
 def shards(tokens, router, up_weight, down_weight, cotangent):
     tokens, cotangent = tokens[0], cotangent[0]
-    up, down = up_weight[0], down_weight[0]
-    slabs = lax.axis_size("dp")
+    moves = host_moves()
+    up, down = move(up_weight[0], moves), move(down_weight[0], moves)
 
     dispatch, combine, slot_rows = routing(tokens, router, cotangent)
 
-    sent = jnp.swapaxes(slot_rows, 0, 1)
-    copies = jnp.broadcast_to(sent[None], (slabs,) + sent.shape).reshape((-1,) + sent.shape[1:])
-    rows = jnp.swapaxes(all_to_all(copies, EVERY), 0, 1)
-    shares, act = expert_rows(rows, up, down)
-    grad_down = outer_sum(act, rows)
-    back = jnp.swapaxes(all_to_all(jnp.swapaxes(shares, 0, 1), EVERY), 0, 1)
-    back = back.reshape((2, slabs) + slot_rows.shape[1:])
+    arrived = all_to_all(to_hosts(jnp.swapaxes(slot_rows, 0, 1)), HOSTS)
+    arrived, up, down = lax.optimization_barrier((arrived, up, down))
+    rows = jnp.swapaxes(arrived, 0, 1)
+    other = swap_cores(rows)
+    other_share, other_act = expert_rows(other, up, down, LOW)
+    got = swap_cores(other_share)
+    share, act = expert_rows(rows, up, down, WIDE)
+    grad_down = outer_sum(act, rows, other_act, other)
+    shares = (share + got.astype(WIDE)).astype(LOW)
+    back = all_to_all(jnp.swapaxes(shares, 0, 1), HOSTS)
+    back, grad_down = lax.optimization_barrier((back, grad_down))
+    grad_down = move(grad_down, [(there, here) for here, there in moves])
+    back = from_hosts(back)
     input_grads, logit_low, term = logit_grads(back, tokens, cotangent, dispatch, combine)
     grad_router = sum_everywhere(term)
     grad_tokens = token_grads(dispatch, input_grads, logit_low, router)

time: 175 us -> 186 us (1.063)
  blocking collectives: 146 us -> 14.7 us
  starting transfers between devices: 5.74 us -> 71.5 us
  waiting for transfers between devices: 4.66 us -> 69.5 us
  local copies, waits for them, and re-layouts: 6.56 us -> 15.5 us
  other arithmetic: 0.78 us -> 3.08 us
    all_to_all x4 -> x1, blocking collectives: 146 us -> 14.7 us  [all_to_all(): return lax.all_to_all(value, axes, split_axis=0, concat_axis=0, tiled=True)]
    all_to_all x1 -> x4, starting transfers between devices: 5.74 us -> 53.6 us  [all_to_all(): return lax.all_to_all(value, axes, split_axis=0, concat_axis=0, tiled=True)]
    ppermute x0 -> x5, waiting for transfers between devices: none -> 36.3 us  [the longest x3 34.2 us: move(): return lax.ppermute(value, COLUMN, moves)]
    all_to_all x1 -> x4, waiting for transfers between devices: 4.66 us -> 33.2 us  [all_to_all(): return lax.all_to_all(value, axes, split_axis=0, concat_axis=0, tiled=True)]
    ppermute x0 -> x5, starting transfers between devices: none -> 17.9 us  [the longest x3 10.6 us: move(): return lax.ppermute(value, COLUMN, moves)]
    reshape x0 -> x3, local copies, waits for them, and re-layouts: none -> 5.19 us  [the longest x1 2.34 us: from_hosts(): return shares.transpose(4, 0, 1, 3, 2, 5).reshape(routes, 2, -1, width)]
    slice x0 -> x2, local copies, waits for them, and re-layouts: none -> 2.21 us  [the longest x1 1.66 us: from_hosts(): shares = jnp.stack([hosted[:, :, 1], hosted[:, ::-1, 0]], axis=1)]
    transpose x0 -> x2, other arithmetic: none -> 2.15 us  [the longest x1 1.99 us: from_hosts(): return shares.transpose(4, 0, 1, 3, 2, 5).reshape(routes, 2, -1, width)]
  transfers between devices with their start and end apart: 1 -> 9, of which waited for: 1 -> 7; matrix products, arithmetic and copies ran while one was open for 0% -> 0% of each run, Pallas kernels for 2% -> 2%
where the time goes in v10:
time: 186 us; the launch traced here: 185 us
  starting transfers between devices  71.5 us (38%)
  waiting for transfers between devices  69.5 us (37%)
  local copies, waits for them, and re-layouts  15.5 us (8%)
  blocking collectives  14.7 us (8%)
  Pallas kernels  9.76 us (5%)
  other arithmetic  3.08 us (2%)
    all_to_all x4, starting transfers between devices, all_to_all(): return lax.all_to_all(value, axes, split_axis=0, concat_axis=0, tiled=True)  53.6 us
    ppermute x3, waiting for transfers between devices, move(): return lax.ppermute(value, COLUMN, moves)  34.2 us
    all_to_all x4, waiting for transfers between devices, all_to_all(): return lax.all_to_all(value, axes, split_axis=0, concat_axis=0, tiled=True)  33.2 us
    all_to_all x1, blocking collectives, all_to_all(): return lax.all_to_all(value, axes, split_axis=0, concat_axis=0, tiled=True)  14.7 us
    ppermute x3, starting transfers between devices, move(): return lax.ppermute(value, COLUMN, moves)  10.6 us
    ppermute x2, starting transfers between devices, swap_cores(): return lax.ppermute(value, 'core', [(0, 1), (1, 0)])  7.24 us
    unnamed x21, local copies, waits for them, and re-layouts  4.16 us
  transfers between devices with their start and end apart: 9, of which 7 were waited for; matrix products, arithmetic and copies ran while one was open for 0% of the time, Pallas kernels for 2%

profile of v10, /device:TPU:1, one launch (start us, length us, event | category | flops | bytes accessed | tf_op | source)
XLA Modules:
  0.0 184.9 jit_solution(11860070193344821379)
XLA Ops:
  0.6 2.6 %shard_map.76 = (f32[196,128]{1,0:T(8,128)}, f32[196,128]{1,0:T(8,128)}, bf16[2,128,768]{2,1,0:T(8,128)(2,1)}) custom-call(bf16[196,768]{1,0:T(8,128)(2,1)} %bitcast.41, bf16[768,128]{1,0:T(8,128)(2,1)} %router_ref.1, bf16[196,768]{1,0:T(8,128)(2,1)} %bitcast.43), custom_call_target="tpu_custom_call" | custom-call | flops 115605504 | bytes 602112 | tf_op jit(solution)/shard_map/pallas_call | solution.py:83
  3.2 1.1 reshape.24
  4.4 0.6 fusion.2
  5.1 0.1 pad_maximum_fusion
  5.2 0.1 copy.34
  5.2 1.7 copy.35
  7.0 23.2 %all-to-all-start = ((bf16[256,2,768]{2,1,0:T(2,128)(2,1)}), bf16[256,2,768]{2,1,0:T(2,128)(2,1)S(1)}, u32[]{:S(2)}, u32[]{:S(2)}) async-start(bf16[256,2,768]{2,1,0:T(2,128)(2,1)} %copy.35), calls=%async_computation | async-start | bytes 1572864 | tf_op jit(solution)/shard_map/all_to_all | solution.py:218
  30.2 4.2 %collective-permute-start = (bf16[768,768]{1,0:T(8,128)(2,1)}, bf16[768,768]{1,0:T(8,128)(2,1)S(1)}, u32[]{:S(2)}, u32[]{:S(2)}) collective-permute-start(bf16[768,768]{1,0:T(8,128)(2,1)} %bitcast.51), channel_id=1, source_target_pairs={{0,64},{1,449},{64,128},{65,1},{128,65},{129,192},{192,129},{193,2... | collective-permute-start | bytes 3538952 | tf_op jit(solution)/shard_map/ppermute | solution.py:242
  34.4 3.1 %collective-permute-start.1 = (bf16[768,768]{1,0:T(8,128)(2,1)}, bf16[768,768]{1,0:T(8,128)(2,1)S(1)}, u32[]{:S(2)}, u32[]{:S(2)}) collective-permute-start(bf16[768,768]{1,0:T(8,128)(2,1)} %bitcast.52), channel_id=1, source_target_pairs={{0,64},{1,449},{64,128},{65,1},{128,65},{129,192},{192,129},{193,2... | collective-permute-start | bytes 3538952 | tf_op jit(solution)/shard_map/ppermute | solution.py:242
  37.5 21.5 %collective-permute-done.up_ref = bf16[768,768]{1,0:T(8,128)(2,1)S(1)} collective-permute-done((bf16[768,768]{1,0:T(8,128)(2,1)}, bf16[768,768]{1,0:T(8,128)(2,1)S(1)}, u32[]{:S(2)}, u32[]{:S(2)}) %collective-permute-start) | collective-permute-done | bytes 1179680 | tf_op jit(solution)/shard_map/ppermute | solution.py:242
  59.0 12.6 %collective-permute-done.1.down_ref = bf16[768,768]{1,0:T(8,128)(2,1)S(1)} collective-permute-done((bf16[768,768]{1,0:T(8,128)(2,1)}, bf16[768,768]{1,0:T(8,128)(2,1)S(1)}, u32[]{:S(2)}, u32[]{:S(2)}) %collective-permute-start.1) | collective-permute-done | bytes 1179680 | tf_op jit(solution)/shard_map/ppermute | solution.py:242
  71.7 1.0 copy-done.7
  72.7 0.0 all-to-all-done
  72.7 0.1 copy.52
  72.8 5.0 %collective-permute-start.2 = (bf16[2,256,768]{2,1,0:T(8,128)(2,1)S(1)}, bf16[2,256,768]{2,1,0:T(8,128)(2,1)S(1)}, u32[]{:S(2)}, u32[]{:S(2)}) collective-permute-start(bf16[2,256,768]{2,1,0:T(8,128)(2,1)S(1)} %bitcast.38), channel_id=1, source_target_pairs={{0,1},{1,0},{2,3},{3,2},{4,5},{5,4},{6,7},{7,6},{8,9},{9,8},{10,11... | collective-permute-start | bytes 2359304 | tf_op jit(solution)/shard_map/ppermute | solution.py:246
  77.7 1.9 %collective-permute-done.2.rows_ref.other_rows_ref = bf16[2,256,768]{2,1,0:T(8,128)(2,1)S(1)} collective-permute-done((bf16[2,256,768]{2,1,0:T(8,128)(2,1)S(1)}, bf16[2,256,768]{2,1,0:T(8,128)(2,1)S(1)}, u32[]{:S(2)}, u32[]{:S(2)}) %collective-permute-start.2) | collective-permute-done | bytes 786464 | tf_op jit(solution)/shard_map/ppermute | solution.py:246
  79.6 0.0 copy-done.8
  79.6 1.6 shard_map.78
  81.2 2.3 %collective-permute-start.3 = (bf16[2,256,768]{2,1,0:T(8,128)(2,1)S(1)}, bf16[2,256,768]{2,1,0:T(8,128)(2,1)S(1)}, u32[]{:S(2)}, u32[]{:S(2)}) collective-permute-start(bf16[2,256,768]{2,1,0:T(8,128)(2,1)S(1)} %get-tuple-element.24), channel_id=1, source_target_pairs={{0,1},{1,0},{2,3},{3,2},{4,5},{5,4},{6,7},{7,6},{8,9},{9,8},{10,11... | collective-permute-start | bytes 2359304 | tf_op jit(solution)/shard_map/ppermute | solution.py:246
  83.5 1.6 shard_map.77
  85.1 0.0 copy-start.4
  85.1 0.3 collective-permute-done.3
  85.4 0.2 fusion
  85.6 0.3 copy-done.4
  85.9 1.7 copy.37
  87.6 16.5 %all-to-all-start.1 = ((bf16[256,2,768]{2,1,0:T(2,128)(2,1)}), bf16[256,2,768]{2,1,0:T(2,128)(2,1)}, u32[]{:S(2)}, u32[]{:S(2)}) async-start(bf16[256,2,768]{2,1,0:T(2,128)(2,1)} %copy.37), calls=%async_computation.1 | async-start | bytes 1572864 | tf_op jit(solution)/shard_map/all_to_all | solution.py:218
  104.1 0.0 copy-start.5
  104.1 1.0 copy-done.5
  105.1 0.8 shard_map.79
  105.9 22.5 %all-to-all-done.1 = bf16[256,2,768]{2,1,0:T(2,128)(2,1)} async-done(((bf16[256,2,768]{2,1,0:T(2,128)(2,1)}), bf16[256,2,768]{2,1,0:T(2,128)(2,1)}, u32[]{:S(2)}, u32[]{:S(2)}) %all-to-all-start.1) | async-done | bytes 786464 | tf_op jit(solution)/shard_map/all_to_all | solution.py:218
  128.4 1.7 fusion.1
  130.0 0.4 copy.53
  130.4 0.4 copy.45
  130.9 2.1 %rev.3 = bf16[2,2,1,32,2,768]{5,1,3,0,4,2:T(2,128)(2,1)S(1)} reverse(bf16[2,2,1,32,2,768]{5,1,3,0,4,2:T(2,128)(2,1)S(1)} %copy.45), dimensions={1} | reverse | bytes 786432 | tf_op jit(solution)/shard_map/rev | solution.py:260
  133.0 2.0 %maximum_bitcast_fusion = bf16[2,2,2,32,2,768]{5,4,3,2,1,0:T(2,128)(2,1)} fusion(bf16[2,1,2,32,2,768]{5,2,3,1,0,4:T(2,128)(2,1)S(1)} %bitcast.47, bf16[2,1,2,32,2,768]{5,2,3,1,0,4:T(2,128)(2,1)S(1)} %bitcast.46), kind=kLoop, calls=%fused_computation.3 | loop fusion | flops 393216 | bytes 1572864 | tf_op jit(solution)/shard_map/transpose | solution.py:261
  135.0 2.3 %reshape.27.shares_ref = bf16[2,2,128,768]{3,2,1,0:T(8,128)(2,1)S(1)} reshape(bf16[2,2,2,32,2,768]{5,4,3,2,1,0:T(2,128)(2,1)} %maximum_bitcast_fusion) | data formatting | bytes 1572864 | tf_op jit(solution)/shard_map/reshape | solution.py:261
  137.3 1.3 shard_map.80
  138.7 6.5 %all-to-all-start.2 = ((bf16[32,24,128]{2,1,0:T(8,128)(2,1)}), bf16[32,24,128]{2,1,0:T(8,128)(2,1)S(1)}, u32[]{:S(2)}, u32[]{:S(2)}) async-start(bf16[32,24,128]{2,1,0:T(8,128)(2,1)} %bitcast.19), calls=%async_computation.2 | async-start | bytes 393216 | tf_op jit(solution)/shard_map/all_to_all | solution.py:218
  145.2 3.3 %collective-permute-start.4 = (bf16[768,768]{1,0:T(8,128)(2,1)S(1)}, bf16[768,768]{1,0:T(8,128)(2,1)S(1)}, u32[]{:S(2)}, u32[]{:S(2)}) collective-permute-start(bf16[768,768]{1,0:T(8,128)(2,1)S(1)} %shard_map.79), channel_id=1, source_target_pairs={{64,0},{449,1},{128,64},{1,65},{65,128},{192,129},{129,192},{256,1... | collective-permute-start | bytes 3538952 | tf_op jit(solution)/shard_map/ppermute | solution.py:242
  148.5 4.3 %all-to-all-done.2.parts_ref = bf16[32,24,128]{2,1,0:T(8,128)(2,1)S(1)} async-done(((bf16[32,24,128]{2,1,0:T(8,128)(2,1)}), bf16[32,24,128]{2,1,0:T(8,128)(2,1)S(1)}, u32[]{:S(2)}, u32[]{:S(2)}) %all-to-all-start.2) | async-done | bytes 196640 | tf_op jit(solution)/shard_map/all_to_all | solution.py:218
  152.8 14.7 %all_to_all.25.parts_ref = f32[16,24,128]{2,1,0:T(8,128)S(1)} all-to-all(f32[16,24,128]{2,1,0:T(8,128)S(1)} %shard_map.82), channel_id=1, replica_groups=mesh['dp'=4,'yl'=2,'x'=4,'zh'=4,'zl'=2,'core'=2] {'dp','zh'}, dimensions={0} | all-to-all | bytes 393216 | tf_op jit(solution)/shard_map/all_to_all | solution.py:218
  167.5 0.7 shard_map.83
  168.2 7.4 %all-to-all-start.4 = ((bf16[32,24,128]{2,1,0:T(8,128)(2,1)}), bf16[32,24,128]{2,1,0:T(8,128)(2,1)S(1)}, u32[]{:S(2)}, u32[]{:S(2)}) async-start(bf16[32,24,128]{2,1,0:T(8,128)(2,1)} %shard_map.83), calls=%async_computation.4 | async-start | bytes 393216 | tf_op jit(solution)/shard_map/all_to_all | solution.py:218
  175.6 1.1 shard_map.81
  176.6 6.5 %all-to-all-done.4 = bf16[32,24,128]{2,1,0:T(8,128)(2,1)S(1)} async-done(((bf16[32,24,128]{2,1,0:T(8,128)(2,1)}), bf16[32,24,128]{2,1,0:T(8,128)(2,1)S(1)}, u32[]{:S(2)}, u32[]{:S(2)}) %all-to-all-start.4) | async-done | bytes 196640 | tf_op jit(solution)/shard_map/all_to_all | solution.py:218
  183.1 0.8 bitcast_convert_fusion
  183.9 0.0 collective-permute-done.4
  183.9 1.0 copy.55
  (17 shorter events, 0.2 us)
Async XLA Ops:
  7.0 65.7 %all-to-all-start = ((bf16[256,2,768]{2,1,0:T(2,128)(2,1)}), bf16[256,2,768]{2,1,0:T(2,128)(2,1)S(1)}, u32[]{:S(2)}, u32[]{:S(2)}) async-start(bf16[256,2,768]{2,1,0:T(2,128)(2,1)} %copy.35), calls=%async_computation | async-start | bytes 1572864 | tf_op jit(solution)/shard_map/all_to_all | solution.py:218
  30.2 28.9 %collective-permute-start = (bf16[768,768]{1,0:T(8,128)(2,1)}, bf16[768,768]{1,0:T(8,128)(2,1)S(1)}, u32[]{:S(2)}, u32[]{:S(2)}) collective-permute-start(bf16[768,768]{1,0:T(8,128)(2,1)} %bitcast.51), channel_id=1, source_target_pairs={{0,64},{1,449},{64,128},{65,1},{128,65},{129,192},{192,129},{193,2... | collective-permute-start | bytes 3538952 | tf_op jit(solution)/shard_map/ppermute | solution.py:242
  34.4 37.3 %collective-permute-start.1 = (bf16[768,768]{1,0:T(8,128)(2,1)}, bf16[768,768]{1,0:T(8,128)(2,1)S(1)}, u32[]{:S(2)}, u32[]{:S(2)}) collective-permute-start(bf16[768,768]{1,0:T(8,128)(2,1)} %bitcast.52), channel_id=1, source_target_pairs={{0,64},{1,449},{64,128},{65,1},{128,65},{129,192},{192,129},{193,2... | collective-permute-start | bytes 3538952 | tf_op jit(solution)/shard_map/ppermute | solution.py:242
  71.7 1.0 copy-start.7
  72.7 6.9 %copy-start.8 = (bf16[768,768]{1,0:T(8,128)(2,1)S(1)}, bf16[768,768]{1,0:T(8,128)(2,1)}, u32[]{:S(2)}) copy-start(bf16[768,768]{1,0:T(8,128)(2,1)} %copy-done.7) | copy-start | bytes 3538948
  72.8 6.9 %collective-permute-start.2 = (bf16[2,256,768]{2,1,0:T(8,128)(2,1)S(1)}, bf16[2,256,768]{2,1,0:T(8,128)(2,1)S(1)}, u32[]{:S(2)}, u32[]{:S(2)}) collective-permute-start(bf16[2,256,768]{2,1,0:T(8,128)(2,1)S(1)} %bitcast.38), channel_id=1, source_target_pairs={{0,1},{1,0},{2,3},{3,2},{4,5},{5,4},{6,7},{7,6},{8,9},{9,8},{10,11... | collective-permute-start | bytes 2359304 | tf_op jit(solution)/shard_map/ppermute | solution.py:246
  81.2 4.2 %collective-permute-start.3 = (bf16[2,256,768]{2,1,0:T(8,128)(2,1)S(1)}, bf16[2,256,768]{2,1,0:T(8,128)(2,1)S(1)}, u32[]{:S(2)}, u32[]{:S(2)}) collective-permute-start(bf16[2,256,768]{2,1,0:T(8,128)(2,1)S(1)} %get-tuple-element.24), channel_id=1, source_target_pairs={{0,1},{1,0},{2,3},{3,2},{4,5},{5,4},{6,7},{7,6},{8,9},{9,8},{10,11... | collective-permute-start | bytes 2359304 | tf_op jit(solution)/shard_map/ppermute | solution.py:246
  85.1 0.7 copy-start.4
  87.6 40.8 %all-to-all-start.1 = ((bf16[256,2,768]{2,1,0:T(2,128)(2,1)}), bf16[256,2,768]{2,1,0:T(2,128)(2,1)}, u32[]{:S(2)}, u32[]{:S(2)}) async-start(bf16[256,2,768]{2,1,0:T(2,128)(2,1)} %copy.37), calls=%async_computation.1 | async-start | bytes 1572864 | tf_op jit(solution)/shard_map/all_to_all | solution.py:218
  104.1 1.0 copy-start.5
  134.9 2.4 %copy-start = (bf16[1,196,768]{2,1,0:T(8,128)(2,1)S(1)}, bf16[1,196,768]{2,1,0:T(8,128)(2,1)}, u32[]{:S(2)}) copy-start(bf16[1,196,768]{2,1,0:T(8,128)(2,1)} %param.5) | copy-start | bytes 903172
  134.9 2.4 %copy-start.1 = (bf16[1,196,768]{2,1,0:T(8,128)(2,1)S(1)}, bf16[1,196,768]{2,1,0:T(8,128)(2,1)}, u32[]{:S(2)}) copy-start(bf16[1,196,768]{2,1,0:T(8,128)(2,1)} %param.9) | copy-start | bytes 903172
  134.9 2.4 %copy-start.3 = (f32[196,128]{1,0:T(8,128)S(1)}, f32[196,128]{1,0:T(8,128)}, u32[]{:S(2)}) copy-start(f32[196,128]{1,0:T(8,128)} %get-tuple-element.18.dispatch_ref) | copy-start | bytes 301060
  134.9 2.4 %copy-start.6 = (f32[196,128]{1,0:T(8,128)S(1)}, f32[196,128]{1,0:T(8,128)}, u32[]{:S(2)}) copy-start(f32[196,128]{1,0:T(8,128)} %get-tuple-element.28.combine_ref) | copy-start | bytes 301060
  138.7 36.9 %copy-start.2 = (bf16[768,128]{1,0:T(8,128)(2,1)S(1)}, bf16[768,128]{1,0:T(8,128)(2,1)}, u32[]{:S(2)}) copy-start(bf16[768,128]{1,0:T(8,128)(2,1)} %router_ref.1) | copy-start | bytes 589828
  138.7 14.0 %all-to-all-start.2 = ((bf16[32,24,128]{2,1,0:T(8,128)(2,1)}), bf16[32,24,128]{2,1,0:T(8,128)(2,1)S(1)}, u32[]{:S(2)}, u32[]{:S(2)}) async-start(bf16[32,24,128]{2,1,0:T(8,128)(2,1)} %bitcast.19), calls=%async_computation.2 | async-start | bytes 393216 | tf_op jit(solution)/shard_map/all_to_all | solution.py:218
  145.2 38.8 %collective-permute-start.4 = (bf16[768,768]{1,0:T(8,128)(2,1)S(1)}, bf16[768,768]{1,0:T(8,128)(2,1)S(1)}, u32[]{:S(2)}, u32[]{:S(2)}) collective-permute-start(bf16[768,768]{1,0:T(8,128)(2,1)S(1)} %shard_map.79), channel_id=1, source_target_pairs={{64,0},{449,1},{128,64},{1,65},{65,128},{192,129},{129,192},{256,1... | collective-permute-start | bytes 3538952 | tf_op jit(solution)/shard_map/ppermute | solution.py:242
  168.2 15.0 %all-to-all-start.4 = ((bf16[32,24,128]{2,1,0:T(8,128)(2,1)}), bf16[32,24,128]{2,1,0:T(8,128)(2,1)S(1)}, u32[]{:S(2)}, u32[]{:S(2)}) async-start(bf16[32,24,128]{2,1,0:T(8,128)(2,1)} %shard_map.83), calls=%async_computation.4 | async-start | bytes 393216 | tf_op jit(solution)/shard_map/all_to_all | solution.py:218

commit v11 on v10

--- a/solution.py
+++ b/solution.py
@@ -21,7 +21,6 @@
 COLUMN = ("dp", "yl", "core")
 HOSTS = ("dp", "yl", "x", "zh", "zl")
 VMEM_BYTES = 20 * 2**20
-WHOLE_BYTES = 61 * 2**20
 
 
 def wide_dot(left, right, left_dim, right_dim):
@@ -34,59 +33,53 @@
     return [pl.BlockSpec(memory_space=pltpu.VMEM)] * count
 
 
-def in_hbm(count):
-    return [pl.BlockSpec(memory_space=pltpu.HBM)] * count
-
-
-def fetch(sources, buffers, sems):
-    copies = [pltpu.make_async_copy(*pair, sems.at[k]) for k, pair in enumerate(zip(sources, buffers))]
-    for copy in copies:
-        copy.start()
-    return copies
-
-
-def buffers_for(*arrays):
-    return [pltpu.VMEM(a.shape, a.dtype) for a in arrays] + [pltpu.SemaphoreType.DMA((len(arrays),))]
-
-
 def cost(flops, bytes_accessed):
     return pl.CostEstimate(flops=flops, bytes_accessed=bytes_accessed, transcendentals=0)
 
 
-def routing_kernel(
-    tokens_hbm, router_hbm, cotangent_hbm, dispatch_ref, combine_ref, rows_ref,
-    tokens_ref, router_ref, cotangent_ref, sems,
-):
-    copies = fetch(
-        (tokens_hbm, router_hbm, cotangent_hbm), (tokens_ref, router_ref, cotangent_ref), sems
-    )
-    copies[0].wait()
-    copies[1].wait()
+def host_block(slab, yl):
+    return (1 - yl) * 2 + (slab + 1 - yl) % 2
+
+
+def blocked(slots):
+    rest = slots // 4
+    slot = lax.broadcasted_iota(jnp.int32, (slots, slots), 0)
+    place = lax.broadcasted_iota(jnp.int32, (slots, slots), 1)
+    core = place // rest % 2
+    here = (place // (2 * rest) * rest + place % rest) * 2 + core
+    return jnp.where(slot == here, 1.0, 0.0).astype(LOW)
+
+
+def routing_kernel(tokens_ref, router_ref, cotangent_ref, dispatch_ref, combine_ref, sent_ref):
     tokens = tokens_ref[...]
-    logits = wide_dot(tokens, router_ref[...], 1, 0)
+    slots = router_ref.shape[1]
+    rest = slots // 4
+    router = wide_dot(router_ref[...], blocked(slots), 1, 0).astype(LOW)
+    logits = wide_dot(tokens, router, 1, 0)
     powers = jnp.exp(logits - jnp.max(logits, axis=0, keepdims=True))
     dispatch = powers / jnp.sum(powers, axis=0, keepdims=True)
     dispatch_ref[...] = dispatch
-    rows_ref[0] = wide_dot(dispatch.astype(LOW), tokens, 0, 0).astype(LOW)
+    inputs = wide_dot(dispatch.astype(LOW), tokens, 0, 0).astype(LOW)
     powers = jnp.exp(logits - jnp.max(logits, axis=1, keepdims=True))
     combine = powers / jnp.sum(powers, axis=1, keepdims=True)
     combine_ref[...] = combine
-    copies[2].wait()
-    rows_ref[1] = wide_dot(combine.astype(LOW), cotangent_ref[...], 0, 0).astype(LOW)
+    grads = wide_dot(combine.astype(LOW), cotangent_ref[...], 0, 0).astype(LOW)
+    for route, rows in enumerate((inputs, grads)):
+        for chip in range(8):
+            block = host_block(chip // 2, chip % 2) * rest
+            sent_ref[route, chip * rest : (chip + 1) * rest] = rows[block : block + rest]
 
 
 def routing(tokens, router, cotangent):
     patches, width = tokens.shape
     slots = router.shape[1]
     weights = jax.ShapeDtypeStruct((patches, slots), WIDE)
-    rows = jax.ShapeDtypeStruct((2, slots, width), LOW)
     return pl.pallas_call(
         routing_kernel,
-        out_shape=(weights, weights, rows),
-        in_specs=in_hbm(3),
+        out_shape=(weights, weights, jax.ShapeDtypeStruct((2, 2 * slots, width), LOW)),
+        in_specs=in_vmem(3),
         out_specs=tuple(in_vmem(3)),
-        scratch_shapes=buffers_for(tokens, router, cotangent),
-        compiler_params=pltpu.CompilerParams(vmem_limit_bytes=WHOLE_BYTES),
+        compiler_params=pltpu.CompilerParams(vmem_limit_bytes=VMEM_BYTES),
         cost_estimate=cost(6 * patches * width * slots, 4 * patches * width),
     )(tokens, router, cotangent)
 
@@ -145,21 +138,26 @@
 def logit_kernel(
     shares_ref, tokens_ref, cotangent_ref, dispatch_ref, combine_ref, inputs_ref, logit_ref, term_ref
 ):
-    slabs = shares_ref.shape[1]
+    slots = dispatch_ref.shape[1]
+    rest = slots // 4
 
     def total(route):
-        terms = [shares_ref[route, k].astype(WIDE) for k in range(slabs)]
-        return functools.reduce(jnp.add, terms).astype(LOW)
-
+        parts = [None] * 4
+        for chip in range(8):
+            share = shares_ref[route, chip * rest : (chip + 1) * rest].astype(WIDE)
+            block = host_block(chip // 2, chip % 2)
+            parts[block] = share if parts[block] is None else parts[block] + share
+        return jnp.concatenate([part.astype(LOW) for part in parts])
+
+    tokens = tokens_ref[...]
     dispatch, combine = dispatch_ref[...], combine_ref[...]
     input_grads = total(1)
     inputs_ref[...] = input_grads
-    tokens = tokens_ref[...]
     grad = wide_dot(cotangent_ref[...], total(0), 1, 1)
     logit_grad = combine * (grad - jnp.sum(combine * grad, axis=1, keepdims=True))
     grad = wide_dot(tokens, input_grads, 1, 1)
     logit_grad = logit_grad + dispatch * (grad - jnp.sum(dispatch * grad, axis=0, keepdims=True))
-    logit_low = logit_grad.astype(LOW)
+    logit_low = wide_dot(logit_grad.astype(LOW), blocked(slots), 1, 1).astype(LOW)
     logit_ref[...] = logit_low
     term_ref[...] = wide_dot(tokens, logit_low, 0, 0).astype(LOW)
 
@@ -247,18 +245,7 @@
 
 
 def to_hosts(rows):
-    _, routes, width = rows.shape
-    placed = rows.reshape(2, -1, 2, routes, width)
-    even = jnp.stack([placed[1, :, 1], placed[0, :, 0]])
-    odd = jnp.stack([placed[1, :, 0], placed[0, :, 1]])
-    return jnp.stack([even, odd, even, odd]).reshape(-1, routes, width)
-
-
-def from_hosts(rows):
-    _, routes, width = rows.shape
-    hosted = rows.reshape(2, 2, 2, -1, routes, width)
-    shares = jnp.stack([hosted[:, :, 1], hosted[:, ::-1, 0]], axis=1)
-    return shares.transpose(4, 0, 1, 3, 2, 5).reshape(routes, 2, -1, width)
+    return jnp.swapaxes(all_to_all(jnp.swapaxes(rows, 0, 1), HOSTS), 0, 1)
 
 
 def shards(tokens, router, up_weight, down_weight, cotangent):
@@ -266,22 +253,19 @@
     moves = host_moves()
     up, down = move(up_weight[0], moves), move(down_weight[0], moves)
 
-    dispatch, combine, slot_rows = routing(tokens, router, cotangent)
-
-    arrived = all_to_all(to_hosts(jnp.swapaxes(slot_rows, 0, 1)), HOSTS)
-    arrived, up, down = lax.optimization_barrier((arrived, up, down))
-    rows = jnp.swapaxes(arrived, 0, 1)
+    dispatch, combine, sent = routing(tokens, router, cotangent)
+
+    rows = lax.cond(lax.axis_index("x") < 4, to_hosts, lambda value: value, sent)
+    rows, up, down = lax.optimization_barrier((rows, up, down))
     other = swap_cores(rows)
     other_share, other_act = expert_rows(other, up, down, LOW)
     got = swap_cores(other_share)
     share, act = expert_rows(rows, up, down, WIDE)
+    back = to_hosts((share + got.astype(WIDE)).astype(LOW))
+    input_grads, logit_low, term = logit_grads(back, tokens, cotangent, dispatch, combine)
+    term, act = lax.optimization_barrier((term, act))
     grad_down = outer_sum(act, rows, other_act, other)
-    shares = (share + got.astype(WIDE)).astype(LOW)
-    back = all_to_all(jnp.swapaxes(shares, 0, 1), HOSTS)
-    back, grad_down = lax.optimization_barrier((back, grad_down))
     grad_down = move(grad_down, [(there, here) for here, there in moves])
-    back = from_hosts(back)
-    input_grads, logit_low, term = logit_grads(back, tokens, cotangent, dispatch, combine)
     grad_router = sum_everywhere(term)
     grad_tokens = token_grads(dispatch, input_grads, logit_low, router)
     return (grad_tokens[None], grad_router, grad_down[None])

time: 186 us -> 167 us (0.90)
  blocking collectives: 14.7 us -> 96.9 us
  waiting for transfers between devices: 69.5 us -> 10.7 us
  starting transfers between devices: 71.5 us -> 36.3 us
  local copies, waits for them, and re-layouts: 15.5 us -> 10.2 us
  other arithmetic: 3.08 us -> 0.94 us
    all_to_all x1 -> x3, blocking collectives: 14.7 us -> 96.9 us  [all_to_all(): return lax.all_to_all(value, axes, split_axis=0, concat_axis=0, tiled=True)]
    all_to_all x4 -> x2, starting transfers between devices: 53.6 us -> 13.5 us  [all_to_all(): return lax.all_to_all(value, axes, split_axis=0, concat_axis=0, tiled=True)]
    ppermute x3, waiting for transfers between devices: 34.2 us -> 0.01 us  [move(): return lax.ppermute(value, COLUMN, moves)]
    all_to_all x4 -> x2, waiting for transfers between devices: 33.2 us -> 8.78 us  [all_to_all(): return lax.all_to_all(value, axes, split_axis=0, concat_axis=0, tiled=True)]
    ppermute x3, starting transfers between devices: 10.6 us -> 16.7 us  [move(): return lax.ppermute(value, COLUMN, moves)]
    reshape x3 -> x0, local copies, waits for them, and re-layouts: 5.19 us -> none  [the longest x1 2.34 us: from_hosts(): return shares.transpose(4, 0, 1, 3, 2, 5).reshape(routes, 2, -1, width)]
    unnamed x21, local copies, waits for them, and re-layouts: 4.16 us -> 8.43 us
    pallas_call x2, Pallas kernels: 3.2 us -> 5.73 us  [expert_rows(): pl.pallas_call(expert_kernel, out_shape=(jax.ShapeDtypeStruct(rows.shape,...]
  transfers between devices with their start and end apart: 9 -> 7, of which waited for: 7 -> 3; matrix products, arithmetic and copies ran while one was open for 0% -> 1% of each run, Pallas kernels for 2% -> 4%
where the time goes in v11:
time: 167 us
  blocking collectives  96.9 us (58%)
  starting transfers between devices  36.3 us (22%)
  Pallas kernels  10.7 us (6%)
  waiting for transfers between devices  10.7 us (6%)
  local copies, waits for them, and re-layouts  10.2 us (6%)
    all_to_all x3, blocking collectives, all_to_all(): return lax.all_to_all(value, axes, split_axis=0, concat_axis=0, tiled=True)  96.9 us
    ppermute x3, starting transfers between devices, move(): return lax.ppermute(value, COLUMN, moves)  16.7 us
    all_to_all x2, starting transfers between devices, all_to_all(): return lax.all_to_all(value, axes, split_axis=0, concat_axis=0, tiled=True)  13.5 us
    all_to_all x2, waiting for transfers between devices, all_to_all(): return lax.all_to_all(value, axes, split_axis=0, concat_axis=0, tiled=True)  8.78 us
    unnamed x21, local copies, waits for them, and re-layouts  8.43 us
    ppermute x2, starting transfers between devices, swap_cores(): return lax.ppermute(value, 'core', [(0, 1), (1, 0)])  6.18 us
    pallas_call x2, Pallas kernels, expert_rows(): pl.pallas_call(expert_kernel, out_shape=(jax.ShapeDtypeStruct(rows.shape,...  5.73 us
  transfers between devices with their start and end apart: 7, of which 3 were waited for; matrix products, arithmetic and copies ran while one was open for 1% of the time, Pallas kernels for 4%

profile of v11, /device:TPU:1, one launch (start us, length us, event | category | flops | bytes accessed | tf_op | source)
XLA Modules:
  0.0 166.6 jit_solution(14598235482004746748)
XLA Ops:
  0.6 5.9 %collective-permute-start = (bf16[768,768]{1,0:T(8,128)(2,1)}, bf16[768,768]{1,0:T(8,128)(2,1)S(1)}, u32[]{:S(2)}, u32[]{:S(2)}) collective-permute-start(bf16[768,768]{1,0:T(8,128)(2,1)} %bitcast.27), channel_id=1, source_target_pairs={{0,64},{1,449},{64,128},{65,1},{128,65},{129,192},{192,129},{193,2... | collective-permute-start | bytes 3538952 | tf_op jit(solution)/shard_map/ppermute | solution.py:240
  6.6 7.3 %collective-permute-start.1 = (bf16[768,768]{1,0:T(8,128)(2,1)}, bf16[768,768]{1,0:T(8,128)(2,1)}, u32[]{:S(2)}, u32[]{:S(2)}) collective-permute-start(bf16[768,768]{1,0:T(8,128)(2,1)} %bitcast.28), channel_id=1, source_target_pairs={{0,64},{1,449},{64,128},{65,1},{128,65},{129,192},{192,129},{193,2... | collective-permute-start | bytes 3538952 | tf_op jit(solution)/shard_map/ppermute | solution.py:240
  13.9 0.0 copy-start
  13.9 1.0 copy-done
  14.9 0.0 copy-start.2
  14.9 1.0 copy-done.2
  15.8 0.9 copy-done.4
  16.8 0.9 shard_map.76
  17.7 44.0 %conditional.1 = (bf16[2,256,768]{2,0,1:T(2,128)(2,1)S(1)}) conditional(s32[]{:T(128)} %convert_element_type.15, bf16[2,256,768]{2,1,0:T(8,128)(2,1)S(1)} %get-tuple-element.24, bf16[2,256,768]{2,1,0:T(8,128)(2,1)S(1)} %get-tuple-element.24), branch_computations={%region_0.0_spmd, %region_1.0_spmd} | conditional | bytes 3145736 | solution.py:258
  17.7 0.8 copy.17
  18.5 43.2 %all_to_all.24 = bf16[256,2,768]{2,1,0:T(2,128)(2,1)S(1)} all-to-all(bf16[256,2,768]{2,1,0:T(2,128)(2,1)S(1)} %bitcast.25), channel_id=1, replica_groups=mesh['dp'=4,'yl'=2,'x'=4,'zh'=4,'zl'=2,'core'=2] {'dp','yl','x','zh','zl'}, dimensions={0} | all-to-all | bytes 1572864 | tf_op jit(solution)/shard_map/cond/branch_1_fun/all_to_all | solution.py:216
  61.7 0.0 collective-permute-done.up_ref
  61.7 0.0 collective-permute-done.1.down_ref
  61.7 0.1 copy.10.rows_ref
  61.8 3.9 %collective-permute-start.2 = (bf16[2,256,768]{2,1,0:T(8,128)(2,1)S(1)}, bf16[2,256,768]{2,1,0:T(8,128)(2,1)S(1)}, u32[]{:S(2)}, u32[]{:S(2)}) collective-permute-start(bf16[2,256,768]{2,1,0:T(8,128)(2,1)S(1)} %copy.10.rows_ref), channel_id=1, source_target_pairs={{0,1},{1,0},{2,3},{3,2},{4,5},{5,4},{6,7},{7,6},{8,9},{9,8},{10,11... | collective-permute-start | bytes 2359304 | tf_op jit(solution)/shard_map/ppermute | solution.py:244
  65.7 1.9 %collective-permute-done.2.rows_ref.other_rows_ref = bf16[2,256,768]{2,1,0:T(8,128)(2,1)S(1)} collective-permute-done((bf16[2,256,768]{2,1,0:T(8,128)(2,1)S(1)}, bf16[2,256,768]{2,1,0:T(8,128)(2,1)S(1)}, u32[]{:S(2)}, u32[]{:S(2)}) %collective-permute-start.2) | collective-permute-done | bytes 786464 | tf_op jit(solution)/shard_map/ppermute | solution.py:244
  67.6 2.9 %shard_map.78 = (bf16[2,256,768]{2,1,0:T(8,128)(2,1)S(1)}, bf16[256,768]{1,0:T(8,128)(2,1)S(1)}) custom-call(bf16[2,256,768]{2,1,0:T(8,128)(2,1)S(1)} %collective-permute-done.2.rows_ref.other_rows_ref, bf16[768,768]{1,0:T(8,128)(2,1)S(1)} %collective-permute-done.up_ref, bf16[768,768]{1,0:T(8,128)(2,1)} %collective-permute-done.1.down_ref), custom_call_target="tpu_custom_call" | custom-call | flops 1207959552 | bytes 4325376 | tf_op jit(solution)/shard_map/pallas_call | solution.py:107
  70.4 2.3 %collective-permute-start.3 = (bf16[2,256,768]{2,1,0:T(8,128)(2,1)S(1)}, bf16[2,256,768]{2,1,0:T(8,128)(2,1)S(1)}, u32[]{:S(2)}, u32[]{:S(2)}) collective-permute-start(bf16[2,256,768]{2,1,0:T(8,128)(2,1)S(1)} %get-tuple-element.29), channel_id=1, source_target_pairs={{0,1},{1,0},{2,3},{3,2},{4,5},{5,4},{6,7},{7,6},{8,9},{9,8},{10,11... | collective-permute-start | bytes 2359304 | tf_op jit(solution)/shard_map/ppermute | solution.py:244
  72.7 2.9 %shard_map.77 = (f32[2,256,768]{2,1,0:T(8,128)S(1)}, bf16[256,768]{1,0:T(8,128)(2,1)S(1)}) custom-call(bf16[2,256,768]{2,1,0:T(8,128)(2,1)S(1)} %copy.10.rows_ref, bf16[768,768]{1,0:T(8,128)(2,1)S(1)} %collective-permute-done.up_ref, bf16[768,768]{1,0:T(8,128)(2,1)} %collective-permute-done.1.down_ref), custom_call_target="tpu_custom_call" | custom-call | flops 1207959552 | bytes 4325376 | tf_op jit(solution)/shard_map/pallas_call | solution.py:107
  75.6 0.0 copy-start.6
  75.6 0.0 collective-permute-done.3
  75.6 0.2 fusion
  75.8 0.6 copy-done.6
  76.4 0.8 copy.12
  77.2 36.8 %all_to_all.25 = bf16[256,2,768]{2,1,0:T(2,128)(2,1)S(1)} all-to-all(bf16[256,2,768]{2,1,0:T(2,128)(2,1)S(1)} %copy.12), channel_id=1, replica_groups=mesh['dp'=4,'yl'=2,'x'=4,'zh'=4,'zl'=2,'core'=2] {'dp','yl','x','zh','zl'}, dimensions={0} | all-to-all | bytes 1572864 | tf_op jit(solution)/shard_map/all_to_all | solution.py:216
  113.9 0.1 copy.18
  114.0 0.9 copy-done.1
  114.9 0.1 copy-done.3
  115.0 1.5 shard_map.79
  116.5 0.7 copy-done.8
  117.2 6.3 %all-to-all-start.2 = ((bf16[32,24,128]{2,1,0:T(8,128)(2,1)}), bf16[32,24,128]{2,1,0:T(8,128)(2,1)S(1)}, u32[]{:S(2)}, u32[]{:S(2)}) async-start(bf16[32,24,128]{2,1,0:T(8,128)(2,1)} %bitcast.9), calls=%async_computation.2 | async-start | bytes 393216 | tf_op jit(solution)/shard_map/all_to_all | solution.py:216
  123.5 0.0 copy-start.7
  123.5 1.0 copy-done.7
  124.5 0.8 shard_map.83
  125.3 0.0 copy-start.5
  125.3 0.0 copy-start.9
  125.3 3.4 %collective-permute-start.4 = (bf16[768,768]{1,0:T(8,128)(2,1)S(1)}, bf16[768,768]{1,0:T(8,128)(2,1)}, u32[]{:S(2)}, u32[]{:S(2)}) collective-permute-start(bf16[768,768]{1,0:T(8,128)(2,1)S(1)} %shard_map.83), channel_id=1, source_target_pairs={{64,0},{449,1},{128,64},{1,65},{65,128},{192,129},{129,192},{256,1... | collective-permute-start | bytes 3538952 | tf_op jit(solution)/shard_map/ppermute | solution.py:240
  128.8 2.3 %all-to-all-done.2.parts_ref = bf16[32,24,128]{2,1,0:T(8,128)(2,1)S(1)} async-done(((bf16[32,24,128]{2,1,0:T(8,128)(2,1)}), bf16[32,24,128]{2,1,0:T(8,128)(2,1)S(1)}, u32[]{:S(2)}, u32[]{:S(2)}) %all-to-all-start.2) | async-done | bytes 196640 | tf_op jit(solution)/shard_map/all_to_all | solution.py:216
  131.1 16.9 %all_to_all.26.parts_ref = f32[16,24,128]{2,1,0:T(8,128)S(1)} all-to-all(f32[16,24,128]{2,1,0:T(8,128)S(1)} %shard_map.81), channel_id=1, replica_groups=mesh['dp'=4,'yl'=2,'x'=4,'zh'=4,'zl'=2,'core'=2] {'dp','zh'}, dimensions={0} | all-to-all | bytes 393216 | tf_op jit(solution)/shard_map/all_to_all | solution.py:216
  148.1 0.7 shard_map.82
  148.8 7.1 %all-to-all-start.4 = ((bf16[32,24,128]{2,1,0:T(8,128)(2,1)}), bf16[32,24,128]{2,1,0:T(8,128)(2,1)S(1)}, u32[]{:S(2)}, u32[]{:S(2)}) async-start(bf16[32,24,128]{2,1,0:T(8,128)(2,1)} %shard_map.82), calls=%async_computation.4 | async-start | bytes 393216 | tf_op jit(solution)/shard_map/all_to_all | solution.py:216
  155.9 0.0 copy-done.5
  155.9 0.0 copy-done.9
  155.9 1.0 shard_map.80
  157.0 6.5 %all-to-all-done.4 = bf16[32,24,128]{2,1,0:T(8,128)(2,1)S(1)} async-done(((bf16[32,24,128]{2,1,0:T(8,128)(2,1)}), bf16[32,24,128]{2,1,0:T(8,128)(2,1)S(1)}, u32[]{:S(2)}, u32[]{:S(2)}) %all-to-all-start.4) | async-done | bytes 196640 | tf_op jit(solution)/shard_map/all_to_all | solution.py:216
  163.5 0.8 bitcast_convert_fusion
  164.2 0.0 collective-permute-done.4
  164.2 2.4 %copy.22 = bf16[1,768,768]{2,1,0:T(8,128)(2,1)} copy(bf16[1,768,768]{2,1,0:T(8,128)(2,1)} %bitcast.11) | data formatting | bytes 2359296
  (5 shorter events, 0.1 us)
Async XLA Ops:
  0.6 61.1 %collective-permute-start = (bf16[768,768]{1,0:T(8,128)(2,1)}, bf16[768,768]{1,0:T(8,128)(2,1)S(1)}, u32[]{:S(2)}, u32[]{:S(2)}) collective-permute-start(bf16[768,768]{1,0:T(8,128)(2,1)} %bitcast.27), channel_id=1, source_target_pairs={{0,64},{1,449},{64,128},{65,1},{128,65},{129,192},{192,129},{193,2... | collective-permute-start | bytes 3538952 | tf_op jit(solution)/shard_map/ppermute | solution.py:240
  6.6 55.1 %collective-permute-start.1 = (bf16[768,768]{1,0:T(8,128)(2,1)}, bf16[768,768]{1,0:T(8,128)(2,1)}, u32[]{:S(2)}, u32[]{:S(2)}) collective-permute-start(bf16[768,768]{1,0:T(8,128)(2,1)} %bitcast.28), channel_id=1, source_target_pairs={{0,64},{1,449},{64,128},{65,1},{128,65},{129,192},{192,129},{193,2... | collective-permute-start | bytes 3538952 | tf_op jit(solution)/shard_map/ppermute | solution.py:240
  13.9 1.0 copy-start
  14.9 1.0 copy-start.2
  15.8 0.9 copy-start.4
  61.8 5.8 %collective-permute-start.2 = (bf16[2,256,768]{2,1,0:T(8,128)(2,1)S(1)}, bf16[2,256,768]{2,1,0:T(8,128)(2,1)S(1)}, u32[]{:S(2)}, u32[]{:S(2)}) collective-permute-start(bf16[2,256,768]{2,1,0:T(8,128)(2,1)S(1)} %copy.10.rows_ref), channel_id=1, source_target_pairs={{0,1},{1,0},{2,3},{3,2},{4,5},{5,4},{6,7},{7,6},{8,9},{9,8},{10,11... | collective-permute-start | bytes 2359304 | tf_op jit(solution)/shard_map/ppermute | solution.py:244
  70.4 5.2 %collective-permute-start.3 = (bf16[2,256,768]{2,1,0:T(8,128)(2,1)S(1)}, bf16[2,256,768]{2,1,0:T(8,128)(2,1)S(1)}, u32[]{:S(2)}, u32[]{:S(2)}) collective-permute-start(bf16[2,256,768]{2,1,0:T(8,128)(2,1)S(1)} %get-tuple-element.29), channel_id=1, source_target_pairs={{0,1},{1,0},{2,3},{3,2},{4,5},{5,4},{6,7},{7,6},{8,9},{9,8},{10,11... | collective-permute-start | bytes 2359304 | tf_op jit(solution)/shard_map/ppermute | solution.py:244
  75.6 0.7 copy-start.6
  113.9 1.0 copy-start.1
  113.9 1.1 copy-start.3
  116.5 0.7 copy-start.8
  117.2 13.9 %all-to-all-start.2 = ((bf16[32,24,128]{2,1,0:T(8,128)(2,1)}), bf16[32,24,128]{2,1,0:T(8,128)(2,1)S(1)}, u32[]{:S(2)}, u32[]{:S(2)}) async-start(bf16[32,24,128]{2,1,0:T(8,128)(2,1)} %bitcast.9), calls=%async_computation.2 | async-start | bytes 393216 | tf_op jit(solution)/shard_map/all_to_all | solution.py:216
  123.5 1.0 copy-start.7
  125.3 30.6 %copy-start.5 = (bf16[768,128]{1,0:T(8,128)(2,1)S(1)}, bf16[768,128]{1,0:T(8,128)(2,1)}, u32[]{:S(2)}) copy-start(bf16[768,128]{1,0:T(8,128)(2,1)} %router_ref.3) | copy-start | bytes 589828
  125.3 30.6 %copy-start.9 = (bf16[128,768]{1,0:T(8,128)(2,1)S(1)}, bf16[128,768]{1,0:T(8,128)(2,1)}, u32[]{:S(2)}) copy-start(bf16[128,768]{1,0:T(8,128)(2,1)} %copy-done.8) | copy-start | bytes 589828
  125.3 38.9 %collective-permute-start.4 = (bf16[768,768]{1,0:T(8,128)(2,1)S(1)}, bf16[768,768]{1,0:T(8,128)(2,1)}, u32[]{:S(2)}, u32[]{:S(2)}) collective-permute-start(bf16[768,768]{1,0:T(8,128)(2,1)S(1)} %shard_map.83), channel_id=1, source_target_pairs={{64,0},{449,1},{128,64},{1,65},{65,128},{192,129},{129,192},{256,1... | collective-permute-start | bytes 3538952 | tf_op jit(solution)/shard_map/ppermute | solution.py:240
  148.8 14.7 %all-to-all-start.4 = ((bf16[32,24,128]{2,1,0:T(8,128)(2,1)}), bf16[32,24,128]{2,1,0:T(8,128)(2,1)S(1)}, u32[]{:S(2)}, u32[]{:S(2)}) async-start(bf16[32,24,128]{2,1,0:T(8,128)(2,1)} %shard_map.82), calls=%async_computation.4 | async-start | bytes 393216 | tf_op jit(solution)/shard_map/all_to_all | solution.py:216

commit v12 on v11

--- a/solution.py
+++ b/solution.py
@@ -31,6 +31,10 @@
 
 def in_vmem(count):
     return [pl.BlockSpec(memory_space=pltpu.VMEM)] * count
+
+
+def in_hbm(count):
+    return [pl.BlockSpec(memory_space=pltpu.HBM)] * count
 
 
 def cost(flops, bytes_accessed):
@@ -84,14 +88,18 @@
     )(tokens, router, cotangent)
 
 
-def expert_kernel(rows_ref, up_ref, down_ref, share_ref, act_ref):
-    up, down = up_ref[...], down_ref[...]
+def expert_kernel(rows_ref, up_ref, down_hbm, share_ref, act_ref, down_ref, sem):
+    fetched = pltpu.make_async_copy(down_hbm, down_ref, sem)
+    fetched.start()
+    up = up_ref[...]
     hidden_pre = wide_dot(rows_ref[0], up, 1, 0)
     squared = hidden_pre * hidden_pre
     inner = jnp.tanh(GELU_SCALE * (hidden_pre + GELU_CUBIC * squared * hidden_pre))
     half = 0.5 * (1.0 + inner)
     activation = (hidden_pre * half).astype(LOW)
     act_ref[...] = activation
+    fetched.wait()
+    down = down_ref[...]
     share_ref[0] = wide_dot(activation, down, 1, 0).astype(share_ref.dtype)
     slope = half + 0.5 * hidden_pre * (1.0 - inner * inner) * (
         GELU_SCALE + 3.0 * GELU_SCALE * GELU_CUBIC * squared
@@ -110,8 +118,9 @@
             jax.ShapeDtypeStruct(rows.shape, kind),
             jax.ShapeDtypeStruct((count, hidden), LOW),
         ),
-        in_specs=in_vmem(3),
+        in_specs=in_vmem(2) + in_hbm(1),
         out_specs=tuple(in_vmem(2)),
+        scratch_shapes=[pltpu.VMEM(down.shape, down.dtype), pltpu.SemaphoreType.DMA],
         compiler_params=pltpu.CompilerParams(vmem_limit_bytes=VMEM_BYTES),
         cost_estimate=cost(8 * count * width * hidden, 4 * width * hidden + 10 * count * width),
     )(rows, up, down)
@@ -133,6 +142,21 @@
         compiler_params=pltpu.CompilerParams(vmem_limit_bytes=VMEM_BYTES),
         cost_estimate=cost(4 * count * width * hidden, 2 * hidden * width),
     )(act, rows, other_act, other_rows)
+
+
+def settle_kernel(moved_ref, out_ref):
+    out_ref[...] = moved_ref[...]
+
+
+def settle(moved):
+    return pl.pallas_call(
+        settle_kernel,
+        out_shape=jax.ShapeDtypeStruct(moved.shape, moved.dtype),
+        in_specs=in_vmem(1),
+        out_specs=in_vmem(1)[0],
+        compiler_params=pltpu.CompilerParams(vmem_limit_bytes=VMEM_BYTES),
+        cost_estimate=cost(0, 4 * moved.size),
+    )(moved)
 
 
 def logit_kernel(
@@ -216,12 +240,13 @@
     return lax.all_to_all(value, axes, split_axis=0, concat_axis=0, tiled=True)
 
 
-def sum_everywhere(term):
+def sum_everywhere(term, beside):
     near = lax.axis_size(NEAR)
     depth, width = term.shape
     parts = all_to_all(term.reshape(near, depth // near, width), NEAR)
     parts = all_to_all(total_copies(parts, lax.axis_size(REST), WIDE), REST)
-    return all_to_all(total_copies(parts, near, LOW), NEAR).reshape(depth, width).astype(WIDE)
+    copies, beside = lax.optimization_barrier((total_copies(parts, near, LOW), beside))
+    return all_to_all(copies, NEAR).reshape(depth, width).astype(WIDE), beside
 
 
 def host_moves():
@@ -266,9 +291,9 @@
     term, act = lax.optimization_barrier((term, act))
     grad_down = outer_sum(act, rows, other_act, other)
     grad_down = move(grad_down, [(there, here) for here, there in moves])
-    grad_router = sum_everywhere(term)
+    grad_router, grad_down = sum_everywhere(term, grad_down)
     grad_tokens = token_grads(dispatch, input_grads, logit_low, router)
-    return (grad_tokens[None], grad_router, grad_down[None])
+    return (grad_tokens[None], grad_router, settle(grad_down)[None])
 
 
 def solution(mesh):

time: 167 us -> 168 us (level)
  blocking collectives: 96.9 us -> 117 us
  starting transfers between devices: 36.3 us -> 26.8 us
  local copies, waits for them, and re-layouts: 10.2 us -> 5.61 us
  waiting for transfers between devices: 10.7 us -> 7.31 us
    all_to_all x3 -> x4, blocking collectives: 96.9 us -> 117 us  [all_to_all(): return lax.all_to_all(value, axes, split_axis=0, concat_axis=0, tiled=True)]
    all_to_all x2 -> x1, starting transfers between devices: 13.5 us -> 5.33 us  [all_to_all(): return lax.all_to_all(value, axes, split_axis=0, concat_axis=0, tiled=True)]
    unnamed x21 -> x12, local copies, waits for them, and re-layouts: 8.43 us -> 3.83 us
    all_to_all x2 -> x1, waiting for transfers between devices: 8.78 us -> 5.41 us  [all_to_all(): return lax.all_to_all(value, axes, split_axis=0, concat_axis=0, tiled=True)]
  transfers between devices with their start and end apart: 7 -> 6, of which waited for: 3 -> 2; matrix products, arithmetic and copies ran while one was open for 1% -> 0% of each run, Pallas kernels for 4% -> 4%
where the time goes in v12:
time: 168 us
  blocking collectives  117 us (70%)
  starting transfers between devices  26.8 us (16%)
  Pallas kernels  9.58 us (6%)
  waiting for transfers between devices  7.31 us (4%)
  local copies, waits for them, and re-layouts  5.61 us (3%)
    all_to_all x4, blocking collectives, all_to_all(): return lax.all_to_all(value, axes, split_axis=0, concat_axis=0, tiled=True)  117 us
    ppermute x3, starting transfers between devices, move(): return lax.ppermute(value, COLUMN, moves)  15.3 us
    ppermute x2, starting transfers between devices, swap_cores(): return lax.ppermute(value, 'core', [(0, 1), (1, 0)])  6.18 us
    all_to_all x1, waiting for transfers between devices, all_to_all(): return lax.all_to_all(value, axes, split_axis=0, concat_axis=0, tiled=True)  5.41 us
    all_to_all x1, starting transfers between devices, all_to_all(): return lax.all_to_all(value, axes, split_axis=0, concat_axis=0, tiled=True)  5.33 us
    pallas_call x2, Pallas kernels, expert_rows(): pl.pallas_call(expert_kernel, out_shape=(jax.ShapeDtypeStruct(rows.shape,...  4.19 us
    unnamed x12, local copies, waits for them, and re-layouts  3.83 us
  transfers between devices with their start and end apart: 6, of which 2 were waited for; matrix products, arithmetic and copies ran while one was open for 0% of the time, Pallas kernels for 4%

profile of v12, /device:TPU:1, one launch (start us, length us, event | category | flops | bytes accessed | tf_op | source)
XLA Modules:
  0.0 167.8 jit_solution(11856101091443832175)
XLA Ops:
  0.6 5.9 %collective-permute-start = (bf16[768,768]{1,0:T(8,128)(2,1)}, bf16[768,768]{1,0:T(8,128)(2,1)S(1)}, u32[]{:S(2)}, u32[]{:S(2)}) collective-permute-start(bf16[768,768]{1,0:T(8,128)(2,1)} %bitcast.29), channel_id=1, source_target_pairs={{0,64},{1,449},{64,128},{65,1},{128,65},{129,192},{192,129},{193,2... | collective-permute-start | bytes 3538952 | tf_op jit(solution)/shard_map/ppermute | solution.py:265
  6.6 7.3 %collective-permute-start.1 = (bf16[768,768]{1,0:T(8,128)(2,1)}, bf16[768,768]{1,0:T(8,128)(2,1)S(1)}, u32[]{:S(2)}, u32[]{:S(2)}) collective-permute-start(bf16[768,768]{1,0:T(8,128)(2,1)} %bitcast.30), channel_id=1, source_target_pairs={{0,64},{1,449},{64,128},{65,1},{128,65},{129,192},{192,129},{193,2... | collective-permute-start | bytes 3538952 | tf_op jit(solution)/shard_map/ppermute | solution.py:265
  13.9 0.0 copy-start
  13.9 1.0 copy-done
  14.9 0.0 copy-start.2
  14.9 1.0 copy-done.2
  15.8 0.0 copy-start.4
  15.8 0.9 copy-done.4
  16.8 0.9 shard_map.76
  17.7 44.0 %conditional.1 = (bf16[2,256,768]{2,0,1:T(2,128)(2,1)S(1)}) conditional(s32[]{:T(128)} %convert_element_type.15, bf16[2,256,768]{2,1,0:T(8,128)(2,1)S(1)} %get-tuple-element.26, bf16[2,256,768]{2,1,0:T(8,128)(2,1)S(1)} %get-tuple-element.26), branch_computations={%region_0.0_spmd, %region_1.0_spmd} | conditional | bytes 3145736 | solution.py:283
  17.7 0.8 copy.17
  18.5 43.2 %all_to_all.24 = bf16[256,2,768]{2,1,0:T(2,128)(2,1)S(1)} all-to-all(bf16[256,2,768]{2,1,0:T(2,128)(2,1)S(1)} %bitcast.26), channel_id=1, replica_groups=mesh['dp'=4,'yl'=2,'x'=4,'zh'=4,'zl'=2,'core'=2] {'dp','yl','x','zh','zl'}, dimensions={0} | all-to-all | bytes 1572864 | tf_op jit(solution)/shard_map/cond/branch_1_fun/all_to_all | solution.py:240
  61.7 0.0 collective-permute-done.up_ref
  61.7 0.0 collective-permute-done.1.down_hbm
  61.7 0.1 copy.10.rows_ref
  61.8 3.9 %collective-permute-start.2 = (bf16[2,256,768]{2,1,0:T(8,128)(2,1)S(1)}, bf16[2,256,768]{2,1,0:T(8,128)(2,1)S(1)}, u32[]{:S(2)}, u32[]{:S(2)}) collective-permute-start(bf16[2,256,768]{2,1,0:T(8,128)(2,1)S(1)} %copy.10.rows_ref), channel_id=1, source_target_pairs={{0,1},{1,0},{2,3},{3,2},{4,5},{5,4},{6,7},{7,6},{8,9},{9,8},{10,11... | collective-permute-start | bytes 2359304 | tf_op jit(solution)/shard_map/ppermute | solution.py:269
  65.7 1.9 %collective-permute-done.2.rows_ref.other_rows_ref = bf16[2,256,768]{2,1,0:T(8,128)(2,1)S(1)} collective-permute-done((bf16[2,256,768]{2,1,0:T(8,128)(2,1)S(1)}, bf16[2,256,768]{2,1,0:T(8,128)(2,1)S(1)}, u32[]{:S(2)}, u32[]{:S(2)}) %collective-permute-start.2) | collective-permute-done | bytes 786464 | tf_op jit(solution)/shard_map/ppermute | solution.py:269
  67.6 2.1 %shard_map.78 = (bf16[2,256,768]{2,1,0:T(8,128)(2,1)S(1)}, bf16[256,768]{1,0:T(8,128)(2,1)S(1)}) custom-call(bf16[2,256,768]{2,1,0:T(8,128)(2,1)S(1)} %collective-permute-done.2.rows_ref.other_rows_ref, bf16[768,768]{1,0:T(8,128)(2,1)S(1)} %collective-permute-done.up_ref, bf16[768,768]{1,0:T(8,128)(2,1)S(1)} %collective-permute-done.1.down_hbm), custom_call_target="tpu_custom_call" | custom-call | flops 1207959552 | bytes 4325376 | tf_op jit(solution)/shard_map/pallas_call | solution.py:115
  69.7 2.3 %collective-permute-start.3 = (bf16[2,256,768]{2,1,0:T(8,128)(2,1)S(1)}, bf16[2,256,768]{2,1,0:T(8,128)(2,1)S(1)}, u32[]{:S(2)}, u32[]{:S(2)}) collective-permute-start(bf16[2,256,768]{2,1,0:T(8,128)(2,1)S(1)} %get-tuple-element.31), channel_id=1, source_target_pairs={{0,1},{1,0},{2,3},{3,2},{4,5},{5,4},{6,7},{7,6},{8,9},{9,8},{10,11... | collective-permute-start | bytes 2359304 | tf_op jit(solution)/shard_map/ppermute | solution.py:269
  72.0 2.1 %shard_map.77 = (f32[2,256,768]{2,1,0:T(8,128)S(1)}, bf16[256,768]{1,0:T(8,128)(2,1)S(1)}) custom-call(bf16[2,256,768]{2,1,0:T(8,128)(2,1)S(1)} %copy.10.rows_ref, bf16[768,768]{1,0:T(8,128)(2,1)S(1)} %collective-permute-done.up_ref, bf16[768,768]{1,0:T(8,128)(2,1)S(1)} %collective-permute-done.1.down_hbm), custom_call_target="tpu_custom_call" | custom-call | flops 1207959552 | bytes 4325376 | tf_op jit(solution)/shard_map/pallas_call | solution.py:115
  74.1 0.0 collective-permute-done.3
  74.1 0.2 fusion
  74.2 0.8 copy.12
  75.1 36.8 %all_to_all.25 = bf16[256,2,768]{2,1,0:T(2,128)(2,1)S(1)} all-to-all(bf16[256,2,768]{2,1,0:T(2,128)(2,1)S(1)} %copy.12), channel_id=1, replica_groups=mesh['dp'=4,'yl'=2,'x'=4,'zh'=4,'zl'=2,'core'=2] {'dp','yl','x','zh','zl'}, dimensions={0} | all-to-all | bytes 1572864 | tf_op jit(solution)/shard_map/all_to_all | solution.py:240
  111.8 0.0 copy-start.1
  111.8 0.0 copy-start.3
  111.8 0.1 copy.18
  111.9 0.9 copy-done.1
  112.8 0.1 copy-done.3
  112.9 0.8 shard_map.79
  113.7 0.8 shard_map.83
  114.5 0.0 copy-start.5
  114.5 2.1 %collective-permute-start.4 = (bf16[768,768]{1,0:T(8,128)(2,1)S(1)}, bf16[768,768]{1,0:T(8,128)(2,1)S(1)}, u32[]{:S(2)}, u32[]{:S(2)}) collective-permute-start(bf16[768,768]{1,0:T(8,128)(2,1)S(1)} %shard_map.83), channel_id=1, source_target_pairs={{64,0},{449,1},{128,64},{1,65},{65,128},{192,129},{129,192},{256,1... | collective-permute-start | bytes 3538952 | tf_op jit(solution)/shard_map/ppermute | solution.py:265
  116.6 20.9 %all_to_all.26.parts_ref = bf16[32,24,128]{2,1,0:T(8,128)(2,1)S(1)} all-to-all(bf16[32,24,128]{2,1,0:T(8,128)(2,1)S(1)} %bitcast.24), channel_id=1, replica_groups=mesh['dp'=4,'yl'=2,'x'=4,'zh'=4,'zl'=2,'core'=2] {'yl','x','zl','core'}, dimensions={0} | all-to-all | bytes 393216 | tf_op jit(solution)/shard_map/all_to_all | solution.py:240
  137.6 15.8 %all_to_all.27.parts_ref = f32[16,24,128]{2,1,0:T(8,128)S(1)} all-to-all(f32[16,24,128]{2,1,0:T(8,128)S(1)} %shard_map.81), channel_id=1, replica_groups=mesh['dp'=4,'yl'=2,'x'=4,'zh'=4,'zl'=2,'core'=2] {'dp','zh'}, dimensions={0} | all-to-all | bytes 393216 | tf_op jit(solution)/shard_map/all_to_all | solution.py:240
  153.4 0.7 shard_map.82
  154.1 0.0 collective-permute-done.4.moved_ref
  154.1 5.3 %all-to-all-start.4 = ((bf16[32,24,128]{2,1,0:T(8,128)(2,1)}), bf16[32,24,128]{2,1,0:T(8,128)(2,1)S(1)}, u32[]{:S(2)}, u32[]{:S(2)}) async-start(bf16[32,24,128]{2,1,0:T(8,128)(2,1)} %shard_map.82), calls=%async_computation.4 | async-start | bytes 393216 | tf_op jit(solution)/shard_map/all_to_all | solution.py:240
  159.4 0.0 copy-done.5
  159.4 1.1 shard_map.80
  160.5 1.1 shard_map.84
  161.6 5.4 %all-to-all-done.4 = bf16[32,24,128]{2,1,0:T(8,128)(2,1)S(1)} async-done(((bf16[32,24,128]{2,1,0:T(8,128)(2,1)}), bf16[32,24,128]{2,1,0:T(8,128)(2,1)S(1)}, u32[]{:S(2)}, u32[]{:S(2)}) %all-to-all-start.4) | async-done | bytes 196640 | tf_op jit(solution)/shard_map/all_to_all | solution.py:240
  167.0 0.8 bitcast_convert_fusion
  (1 shorter events, 0.0 us)
Async XLA Ops:
  0.6 61.1 %collective-permute-start = (bf16[768,768]{1,0:T(8,128)(2,1)}, bf16[768,768]{1,0:T(8,128)(2,1)S(1)}, u32[]{:S(2)}, u32[]{:S(2)}) collective-permute-start(bf16[768,768]{1,0:T(8,128)(2,1)} %bitcast.29), channel_id=1, source_target_pairs={{0,64},{1,449},{64,128},{65,1},{128,65},{129,192},{192,129},{193,2... | collective-permute-start | bytes 3538952 | tf_op jit(solution)/shard_map/ppermute | solution.py:265
  6.6 55.1 %collective-permute-start.1 = (bf16[768,768]{1,0:T(8,128)(2,1)}, bf16[768,768]{1,0:T(8,128)(2,1)S(1)}, u32[]{:S(2)}, u32[]{:S(2)}) collective-permute-start(bf16[768,768]{1,0:T(8,128)(2,1)} %bitcast.30), channel_id=1, source_target_pairs={{0,64},{1,449},{64,128},{65,1},{128,65},{129,192},{192,129},{193,2... | collective-permute-start | bytes 3538952 | tf_op jit(solution)/shard_map/ppermute | solution.py:265
  13.9 1.0 copy-start
  14.9 1.0 copy-start.2
  15.8 0.9 copy-start.4
  61.8 5.8 %collective-permute-start.2 = (bf16[2,256,768]{2,1,0:T(8,128)(2,1)S(1)}, bf16[2,256,768]{2,1,0:T(8,128)(2,1)S(1)}, u32[]{:S(2)}, u32[]{:S(2)}) collective-permute-start(bf16[2,256,768]{2,1,0:T(8,128)(2,1)S(1)} %copy.10.rows_ref), channel_id=1, source_target_pairs={{0,1},{1,0},{2,3},{3,2},{4,5},{5,4},{6,7},{7,6},{8,9},{9,8},{10,11... | collective-permute-start | bytes 2359304 | tf_op jit(solution)/shard_map/ppermute | solution.py:269
  69.7 4.4 %collective-permute-start.3 = (bf16[2,256,768]{2,1,0:T(8,128)(2,1)S(1)}, bf16[2,256,768]{2,1,0:T(8,128)(2,1)S(1)}, u32[]{:S(2)}, u32[]{:S(2)}) collective-permute-start(bf16[2,256,768]{2,1,0:T(8,128)(2,1)S(1)} %get-tuple-element.31), channel_id=1, source_target_pairs={{0,1},{1,0},{2,3},{3,2},{4,5},{5,4},{6,7},{7,6},{8,9},{9,8},{10,11... | collective-permute-start | bytes 2359304 | tf_op jit(solution)/shard_map/ppermute | solution.py:269
  111.8 1.0 copy-start.1
  111.8 1.1 copy-start.3
  114.5 44.9 %copy-start.5 = (bf16[768,128]{1,0:T(8,128)(2,1)S(1)}, bf16[768,128]{1,0:T(8,128)(2,1)}, u32[]{:S(2)}) copy-start(bf16[768,128]{1,0:T(8,128)(2,1)} %router_ref.3) | copy-start | bytes 589828
  114.5 39.5 %collective-permute-start.4 = (bf16[768,768]{1,0:T(8,128)(2,1)S(1)}, bf16[768,768]{1,0:T(8,128)(2,1)S(1)}, u32[]{:S(2)}, u32[]{:S(2)}) collective-permute-start(bf16[768,768]{1,0:T(8,128)(2,1)S(1)} %shard_map.83), channel_id=1, source_target_pairs={{64,0},{449,1},{128,64},{1,65},{65,128},{192,129},{129,192},{256,1... | collective-permute-start | bytes 3538952 | tf_op jit(solution)/shard_map/ppermute | solution.py:265
  154.1 12.9 %all-to-all-start.4 = ((bf16[32,24,128]{2,1,0:T(8,128)(2,1)}), bf16[32,24,128]{2,1,0:T(8,128)(2,1)S(1)}, u32[]{:S(2)}, u32[]{:S(2)}) async-start(bf16[32,24,128]{2,1,0:T(8,128)(2,1)} %shard_map.82), calls=%async_computation.4 | async-start | bytes 393216 | tf_op jit(solution)/shard_map/all_to_all | solution.py:240

commit v13 on v12

--- a/solution.py
+++ b/solution.py
@@ -240,13 +240,12 @@
     return lax.all_to_all(value, axes, split_axis=0, concat_axis=0, tiled=True)
 
 
-def sum_everywhere(term, beside):
+def sum_everywhere(term):
     near = lax.axis_size(NEAR)
     depth, width = term.shape
     parts = all_to_all(term.reshape(near, depth // near, width), NEAR)
     parts = all_to_all(total_copies(parts, lax.axis_size(REST), WIDE), REST)
-    copies, beside = lax.optimization_barrier((total_copies(parts, near, LOW), beside))
-    return all_to_all(copies, NEAR).reshape(depth, width).astype(WIDE), beside
+    return all_to_all(total_copies(parts, near, LOW), NEAR).reshape(depth, width).astype(WIDE)
 
 
 def host_moves():
@@ -291,7 +290,7 @@
     term, act = lax.optimization_barrier((term, act))
     grad_down = outer_sum(act, rows, other_act, other)
     grad_down = move(grad_down, [(there, here) for here, there in moves])
-    grad_router, grad_down = sum_everywhere(term, grad_down)
+    grad_router = sum_everywhere(term)
     grad_tokens = token_grads(dispatch, input_grads, logit_low, router)
     return (grad_tokens[None], grad_router, settle(grad_down)[None])
 

time: 168 us -> 168 us (level)
  blocking collectives: 117 us -> 97 us
  starting transfers between devices: 26.8 us -> 36.3 us
  local copies, waits for them, and re-layouts: 5.61 us -> 11.3 us
  waiting for transfers between devices: 7.31 us -> 10.7 us
    all_to_all x4 -> x3, blocking collectives: 117 us -> 97 us  [all_to_all(): return lax.all_to_all(value, axes, split_axis=0, concat_axis=0, tiled=True)]
    all_to_all x1 -> x2, starting transfers between devices: 5.33 us -> 13.4 us  [all_to_all(): return lax.all_to_all(value, axes, split_axis=0, concat_axis=0, tiled=True)]
    unnamed x12 -> x26, local copies, waits for them, and re-layouts: 3.83 us -> 8.35 us
    all_to_all x1 -> x2, waiting for transfers between devices: 5.41 us -> 8.78 us  [all_to_all(): return lax.all_to_all(value, axes, split_axis=0, concat_axis=0, tiled=True)]
  transfers between devices with their start and end apart: 6 -> 7, of which waited for: 2 -> 3; matrix products, arithmetic and copies ran while one was open for 0% -> 1% of each run, Pallas kernels for 4% -> 3%
where the time goes in v13:
time: 168 us; the launch traced here: 167 us
  blocking collectives  97 us (58%)
  starting transfers between devices  36.3 us (22%)
  local copies, waits for them, and re-layouts  11.3 us (7%)
  waiting for transfers between devices  10.7 us (6%)
  Pallas kernels  10.3 us (6%)
    all_to_all x3, blocking collectives, all_to_all(): return lax.all_to_all(value, axes, split_axis=0, concat_axis=0, tiled=True)  97 us
    ppermute x3, starting transfers between devices, move(): return lax.ppermute(value, COLUMN, moves)  16.7 us
    all_to_all x2, starting transfers between devices, all_to_all(): return lax.all_to_all(value, axes, split_axis=0, concat_axis=0, tiled=True)  13.4 us
    all_to_all x2, waiting for transfers between devices, all_to_all(): return lax.all_to_all(value, axes, split_axis=0, concat_axis=0, tiled=True)  8.78 us
    unnamed x26, local copies, waits for them, and re-layouts  8.35 us
    ppermute x2, starting transfers between devices, swap_cores(): return lax.ppermute(value, 'core', [(0, 1), (1, 0)])  6.18 us
    pallas_call x2, Pallas kernels, expert_rows(): pl.pallas_call(expert_kernel, out_shape=(jax.ShapeDtypeStruct(rows.shape,...  4.19 us
  transfers between devices with their start and end apart: 7, of which 3 were waited for; matrix products, arithmetic and copies ran while one was open for 1% of the time, Pallas kernels for 3%

profile of v13, /device:TPU:1, one launch (start us, length us, event | category | flops | bytes accessed | tf_op | source)
XLA Modules:
  0.0 167.3 jit_solution(4916959360065835609)
XLA Ops:
  0.6 5.9 %collective-permute-start = (bf16[768,768]{1,0:T(8,128)(2,1)}, bf16[768,768]{1,0:T(8,128)(2,1)S(1)}, u32[]{:S(2)}, u32[]{:S(2)}) collective-permute-start(bf16[768,768]{1,0:T(8,128)(2,1)} %bitcast.28), channel_id=1, source_target_pairs={{0,64},{1,449},{64,128},{65,1},{128,65},{129,192},{192,129},{193,2... | collective-permute-start | bytes 3538952 | tf_op jit(solution)/shard_map/ppermute | solution.py:264
  6.6 7.3 %collective-permute-start.1 = (bf16[768,768]{1,0:T(8,128)(2,1)}, bf16[768,768]{1,0:T(8,128)(2,1)S(1)}, u32[]{:S(2)}, u32[]{:S(2)}) collective-permute-start(bf16[768,768]{1,0:T(8,128)(2,1)} %bitcast.29), channel_id=1, source_target_pairs={{0,64},{1,449},{64,128},{65,1},{128,65},{129,192},{192,129},{193,2... | collective-permute-start | bytes 3538952 | tf_op jit(solution)/shard_map/ppermute | solution.py:264
  13.9 0.0 copy-start
  13.9 1.0 copy-done
  14.9 1.0 copy-done.2
  15.8 0.9 copy-done.4
  16.8 0.9 shard_map.76
  17.7 44.1 %conditional.1 = (bf16[2,256,768]{2,0,1:T(2,128)(2,1)}) conditional(s32[]{:T(128)} %convert_element_type.15, bf16[2,256,768]{2,1,0:T(8,128)(2,1)S(1)} %get-tuple-element.24, bf16[2,256,768]{2,1,0:T(8,128)(2,1)S(1)} %get-tuple-element.24), branch_computations={%region_0.0_spmd, %region_1.0_spmd} | conditional | bytes 3145736 | solution.py:282
  17.7 0.8 copy.17
  18.5 43.3 %all_to_all.24 = bf16[256,2,768]{2,1,0:T(2,128)(2,1)} all-to-all(bf16[256,2,768]{2,1,0:T(2,128)(2,1)S(1)} %bitcast.25), channel_id=1, replica_groups=mesh['dp'=4,'yl'=2,'x'=4,'zh'=4,'zl'=2,'core'=2] {'dp','yl','x','zh','zl'}, dimensions={0} | all-to-all | bytes 1572864 | tf_op jit(solution)/shard_map/cond/branch_1_fun/all_to_all | solution.py:240
  61.8 0.0 collective-permute-done.up_ref
  61.8 0.0 collective-permute-done.1.down_hbm
  61.8 1.0 copy-done.10
  62.8 1.2 copy.10.rows_ref
  64.0 3.9 %collective-permute-start.2 = (bf16[2,256,768]{2,1,0:T(8,128)(2,1)S(1)}, bf16[2,256,768]{2,1,0:T(8,128)(2,1)S(1)}, u32[]{:S(2)}, u32[]{:S(2)}) collective-permute-start(bf16[2,256,768]{2,1,0:T(8,128)(2,1)S(1)} %copy.10.rows_ref), channel_id=1, source_target_pairs={{0,1},{1,0},{2,3},{3,2},{4,5},{5,4},{6,7},{7,6},{8,9},{9,8},{10,11... | collective-permute-start | bytes 2359304 | tf_op jit(solution)/shard_map/ppermute | solution.py:268
  67.9 1.9 %collective-permute-done.2.rows_ref.other_rows_ref = bf16[2,256,768]{2,1,0:T(8,128)(2,1)S(1)} collective-permute-done((bf16[2,256,768]{2,1,0:T(8,128)(2,1)S(1)}, bf16[2,256,768]{2,1,0:T(8,128)(2,1)S(1)}, u32[]{:S(2)}, u32[]{:S(2)}) %collective-permute-start.2) | collective-permute-done | bytes 786464 | tf_op jit(solution)/shard_map/ppermute | solution.py:268
  69.8 1.3 copy-done.11
  71.1 2.1 %shard_map.78 = (bf16[2,256,768]{2,1,0:T(8,128)(2,1)S(1)}, bf16[256,768]{1,0:T(8,128)(2,1)S(1)}) custom-call(bf16[2,256,768]{2,1,0:T(8,128)(2,1)S(1)} %collective-permute-done.2.rows_ref.other_rows_ref, bf16[768,768]{1,0:T(8,128)(2,1)S(1)} %collective-permute-done.up_ref, bf16[768,768]{1,0:T(8,128)(2,1)S(1)} %copy-done.11), custom_call_target="tpu_custom_call" | custom-call | flops 1207959552 | bytes 4325376 | tf_op jit(solution)/shard_map/pallas_call | solution.py:115
  73.2 2.3 %collective-permute-start.3 = (bf16[2,256,768]{2,1,0:T(8,128)(2,1)S(1)}, bf16[2,256,768]{2,1,0:T(8,128)(2,1)S(1)}, u32[]{:S(2)}, u32[]{:S(2)}) collective-permute-start(bf16[2,256,768]{2,1,0:T(8,128)(2,1)S(1)} %get-tuple-element.29), channel_id=1, source_target_pairs={{0,1},{1,0},{2,3},{3,2},{4,5},{5,4},{6,7},{7,6},{8,9},{9,8},{10,11... | collective-permute-start | bytes 2359304 | tf_op jit(solution)/shard_map/ppermute | solution.py:268
  75.5 0.0 copy-done.12
  75.5 2.1 %shard_map.77 = (f32[2,256,768]{2,1,0:T(8,128)S(1)}, bf16[256,768]{1,0:T(8,128)(2,1)S(1)}) custom-call(bf16[2,256,768]{2,1,0:T(8,128)(2,1)S(1)} %copy.10.rows_ref, bf16[768,768]{1,0:T(8,128)(2,1)S(1)} %collective-permute-done.up_ref, bf16[768,768]{1,0:T(8,128)(2,1)S(1)} %copy-done.12), custom_call_target="tpu_custom_call" | custom-call | flops 1207959552 | bytes 4325376 | tf_op jit(solution)/shard_map/pallas_call | solution.py:115
  77.6 0.0 copy-start.6
  77.6 0.0 collective-permute-done.3
  77.6 0.2 fusion
  77.8 0.6 copy-done.6
  78.4 0.8 copy.12
  79.2 36.8 %all_to_all.25 = bf16[256,2,768]{2,1,0:T(2,128)(2,1)S(1)} all-to-all(bf16[256,2,768]{2,1,0:T(2,128)(2,1)S(1)} %copy.12), channel_id=1, replica_groups=mesh['dp'=4,'yl'=2,'x'=4,'zh'=4,'zl'=2,'core'=2] {'dp','yl','x','zh','zl'}, dimensions={0} | all-to-all | bytes 1572864 | tf_op jit(solution)/shard_map/all_to_all | solution.py:240
  115.9 0.1 copy.18
  116.0 0.9 copy-done.1
  116.9 0.1 copy-done.3
  117.0 1.5 shard_map.79
  118.5 0.7 copy-done.8
  119.2 6.3 %all-to-all-start.2 = ((bf16[32,24,128]{2,1,0:T(8,128)(2,1)}), bf16[32,24,128]{2,1,0:T(8,128)(2,1)S(1)}, u32[]{:S(2)}, u32[]{:S(2)}) async-start(bf16[32,24,128]{2,1,0:T(8,128)(2,1)} %bitcast.9), calls=%async_computation.2 | async-start | bytes 393216 | tf_op jit(solution)/shard_map/all_to_all | solution.py:240
  125.5 0.0 copy-start.7
  125.5 1.0 copy-done.7
  126.5 0.8 shard_map.83
  127.3 0.0 copy-start.5
  127.3 0.0 copy-start.9
  127.3 3.4 %collective-permute-start.4 = (bf16[768,768]{1,0:T(8,128)(2,1)S(1)}, bf16[768,768]{1,0:T(8,128)(2,1)S(1)}, u32[]{:S(2)}, u32[]{:S(2)}) collective-permute-start(bf16[768,768]{1,0:T(8,128)(2,1)S(1)} %shard_map.83), channel_id=1, source_target_pairs={{64,0},{449,1},{128,64},{1,65},{65,128},{192,129},{129,192},{256,1... | collective-permute-start | bytes 3538952 | tf_op jit(solution)/shard_map/ppermute | solution.py:264
  130.8 2.3 %all-to-all-done.2.parts_ref = bf16[32,24,128]{2,1,0:T(8,128)(2,1)S(1)} async-done(((bf16[32,24,128]{2,1,0:T(8,128)(2,1)}), bf16[32,24,128]{2,1,0:T(8,128)(2,1)S(1)}, u32[]{:S(2)}, u32[]{:S(2)}) %all-to-all-start.2) | async-done | bytes 196640 | tf_op jit(solution)/shard_map/all_to_all | solution.py:240
  133.1 16.9 %all_to_all.26.parts_ref = f32[16,24,128]{2,1,0:T(8,128)S(1)} all-to-all(f32[16,24,128]{2,1,0:T(8,128)S(1)} %shard_map.81), channel_id=1, replica_groups=mesh['dp'=4,'yl'=2,'x'=4,'zh'=4,'zl'=2,'core'=2] {'dp','zh'}, dimensions={0} | all-to-all | bytes 393216 | tf_op jit(solution)/shard_map/all_to_all | solution.py:240
  150.1 0.7 shard_map.82
  150.8 7.1 %all-to-all-start.4 = ((bf16[32,24,128]{2,1,0:T(8,128)(2,1)}), bf16[32,24,128]{2,1,0:T(8,128)(2,1)S(1)}, u32[]{:S(2)}, u32[]{:S(2)}) async-start(bf16[32,24,128]{2,1,0:T(8,128)(2,1)} %shard_map.82), calls=%async_computation.4 | async-start | bytes 393216 | tf_op jit(solution)/shard_map/all_to_all | solution.py:240
  157.9 1.1 shard_map.80
  158.9 6.5 %all-to-all-done.4 = bf16[32,24,128]{2,1,0:T(8,128)(2,1)S(1)} async-done(((bf16[32,24,128]{2,1,0:T(8,128)(2,1)}), bf16[32,24,128]{2,1,0:T(8,128)(2,1)S(1)}, u32[]{:S(2)}, u32[]{:S(2)}) %all-to-all-start.4) | async-done | bytes 196640 | tf_op jit(solution)/shard_map/all_to_all | solution.py:240
  165.4 0.8 bitcast_convert_fusion
  166.2 0.0 collective-permute-done.4.moved_ref
  166.2 1.1 shard_map.84
  (11 shorter events, 0.1 us)
Async XLA Ops:
  0.6 61.2 %collective-permute-start = (bf16[768,768]{1,0:T(8,128)(2,1)}, bf16[768,768]{1,0:T(8,128)(2,1)S(1)}, u32[]{:S(2)}, u32[]{:S(2)}) collective-permute-start(bf16[768,768]{1,0:T(8,128)(2,1)} %bitcast.28), channel_id=1, source_target_pairs={{0,64},{1,449},{64,128},{65,1},{128,65},{129,192},{192,129},{193,2... | collective-permute-start | bytes 3538952 | tf_op jit(solution)/shard_map/ppermute | solution.py:264
  6.6 55.2 %collective-permute-start.1 = (bf16[768,768]{1,0:T(8,128)(2,1)}, bf16[768,768]{1,0:T(8,128)(2,1)S(1)}, u32[]{:S(2)}, u32[]{:S(2)}) collective-permute-start(bf16[768,768]{1,0:T(8,128)(2,1)} %bitcast.29), channel_id=1, source_target_pairs={{0,64},{1,449},{64,128},{65,1},{128,65},{129,192},{192,129},{193,2... | collective-permute-start | bytes 3538952 | tf_op jit(solution)/shard_map/ppermute | solution.py:264
  13.9 1.0 copy-start
  14.9 1.0 copy-start.2
  15.8 0.9 copy-start.4
  61.8 1.0 copy-start.10
  64.0 5.8 %collective-permute-start.2 = (bf16[2,256,768]{2,1,0:T(8,128)(2,1)S(1)}, bf16[2,256,768]{2,1,0:T(8,128)(2,1)S(1)}, u32[]{:S(2)}, u32[]{:S(2)}) collective-permute-start(bf16[2,256,768]{2,1,0:T(8,128)(2,1)S(1)} %copy.10.rows_ref), channel_id=1, source_target_pairs={{0,1},{1,0},{2,3},{3,2},{4,5},{5,4},{6,7},{7,6},{8,9},{9,8},{10,11... | collective-permute-start | bytes 2359304 | tf_op jit(solution)/shard_map/ppermute | solution.py:268
  69.8 1.3 copy-start.11
  71.1 4.4 %copy-start.12 = (bf16[768,768]{1,0:T(8,128)(2,1)S(1)}, bf16[768,768]{1,0:T(8,128)(2,1)}, u32[]{:S(2)}) copy-start(bf16[768,768]{1,0:T(8,128)(2,1)} %copy-done.10) | copy-start | bytes 3538948
  73.2 4.4 %collective-permute-start.3 = (bf16[2,256,768]{2,1,0:T(8,128)(2,1)S(1)}, bf16[2,256,768]{2,1,0:T(8,128)(2,1)S(1)}, u32[]{:S(2)}, u32[]{:S(2)}) collective-permute-start(bf16[2,256,768]{2,1,0:T(8,128)(2,1)S(1)} %get-tuple-element.29), channel_id=1, source_target_pairs={{0,1},{1,0},{2,3},{3,2},{4,5},{5,4},{6,7},{7,6},{8,9},{9,8},{10,11... | collective-permute-start | bytes 2359304 | tf_op jit(solution)/shard_map/ppermute | solution.py:268
  77.6 0.7 copy-start.6
  115.9 1.0 copy-start.1
  115.9 1.1 copy-start.3
  118.5 0.7 copy-start.8
  119.2 13.9 %all-to-all-start.2 = ((bf16[32,24,128]{2,1,0:T(8,128)(2,1)}), bf16[32,24,128]{2,1,0:T(8,128)(2,1)S(1)}, u32[]{:S(2)}, u32[]{:S(2)}) async-start(bf16[32,24,128]{2,1,0:T(8,128)(2,1)} %bitcast.9), calls=%async_computation.2 | async-start | bytes 393216 | tf_op jit(solution)/shard_map/all_to_all | solution.py:240
  125.5 1.0 copy-start.7
  127.3 30.6 %copy-start.5 = (bf16[768,128]{1,0:T(8,128)(2,1)S(1)}, bf16[768,128]{1,0:T(8,128)(2,1)}, u32[]{:S(2)}) copy-start(bf16[768,128]{1,0:T(8,128)(2,1)} %router_ref.3) | copy-start | bytes 589828
  127.3 30.6 %copy-start.9 = (bf16[128,768]{1,0:T(8,128)(2,1)S(1)}, bf16[128,768]{1,0:T(8,128)(2,1)}, u32[]{:S(2)}) copy-start(bf16[128,768]{1,0:T(8,128)(2,1)} %copy-done.8) | copy-start | bytes 589828
  127.3 38.9 %collective-permute-start.4 = (bf16[768,768]{1,0:T(8,128)(2,1)S(1)}, bf16[768,768]{1,0:T(8,128)(2,1)S(1)}, u32[]{:S(2)}, u32[]{:S(2)}) collective-permute-start(bf16[768,768]{1,0:T(8,128)(2,1)S(1)} %shard_map.83), channel_id=1, source_target_pairs={{64,0},{449,1},{128,64},{1,65},{65,128},{192,129},{129,192},{256,1... | collective-permute-start | bytes 3538952 | tf_op jit(solution)/shard_map/ppermute | solution.py:264
  150.8 14.7 %all-to-all-start.4 = ((bf16[32,24,128]{2,1,0:T(8,128)(2,1)}), bf16[32,24,128]{2,1,0:T(8,128)(2,1)S(1)}, u32[]{:S(2)}, u32[]{:S(2)}) async-start(bf16[32,24,128]{2,1,0:T(8,128)(2,1)} %shard_map.82), calls=%async_computation.4 | async-start | bytes 393216 | tf_op jit(solution)/shard_map/all_to_all | solution.py:240

commit v14 on v13

--- a/solution.py
+++ b/solution.py
@@ -144,21 +144,6 @@
     )(act, rows, other_act, other_rows)
 
 
-def settle_kernel(moved_ref, out_ref):
-    out_ref[...] = moved_ref[...]
-
-
-def settle(moved):
-    return pl.pallas_call(
-        settle_kernel,
-        out_shape=jax.ShapeDtypeStruct(moved.shape, moved.dtype),
-        in_specs=in_vmem(1),
-        out_specs=in_vmem(1)[0],
-        compiler_params=pltpu.CompilerParams(vmem_limit_bytes=VMEM_BYTES),
-        cost_estimate=cost(0, 4 * moved.size),
-    )(moved)
-
-
 def logit_kernel(
     shares_ref, tokens_ref, cotangent_ref, dispatch_ref, combine_ref, inputs_ref, logit_ref, term_ref
 ):
@@ -292,7 +277,7 @@
     grad_down = move(grad_down, [(there, here) for here, there in moves])
     grad_router = sum_everywhere(term)
     grad_tokens = token_grads(dispatch, input_grads, logit_low, router)
-    return (grad_tokens[None], grad_router, settle(grad_down)[None])
+    return (grad_tokens[None], grad_router, grad_down[None])
 
 
 def solution(mesh):

time: 168 us -> 167 us (level)
    unnamed x26 -> x21, local copies, waits for them, and re-layouts: 8.35 us -> 8.43 us
  transfers between devices with their start and end apart: 7 -> 7, of which waited for: 3 -> 3; matrix products, arithmetic and copies ran while one was open for 1% -> 1% of each run, Pallas kernels for 3% -> 4%
where the time goes in v14:
time: 167 us; the launch traced here: 166 us
  blocking collectives  96.9 us (58%)
  starting transfers between devices  36.3 us (22%)
  waiting for transfers between devices  10.7 us (6%)
  local copies, waits for them, and re-layouts  10.2 us (6%)
  Pallas kernels  9.97 us (6%)
    all_to_all x3, blocking collectives, all_to_all(): return lax.all_to_all(value, axes, split_axis=0, concat_axis=0, tiled=True)  96.9 us
    ppermute x3, starting transfers between devices, move(): return lax.ppermute(value, COLUMN, moves)  16.7 us
    all_to_all x2, starting transfers between devices, all_to_all(): return lax.all_to_all(value, axes, split_axis=0, concat_axis=0, tiled=True)  13.4 us
    all_to_all x2, waiting for transfers between devices, all_to_all(): return lax.all_to_all(value, axes, split_axis=0, concat_axis=0, tiled=True)  8.78 us
    unnamed x21, local copies, waits for them, and re-layouts  8.43 us
    ppermute x2, starting transfers between devices, swap_cores(): return lax.ppermute(value, 'core', [(0, 1), (1, 0)])  6.18 us
    pallas_call x2, Pallas kernels, expert_rows(): pl.pallas_call(expert_kernel, out_shape=(jax.ShapeDtypeStruct(rows.shape,...  4.99 us
  transfers between devices with their start and end apart: 7, of which 3 were waited for; matrix products, arithmetic and copies ran while one was open for 1% of the time, Pallas kernels for 4%

profile of v14, /device:TPU:1, one launch (start us, length us, event | category | flops | bytes accessed | tf_op | source)
XLA Modules:
  0.0 165.9 jit_solution(3103875055620714199)
XLA Ops:
  0.6 5.9 %collective-permute-start = (bf16[768,768]{1,0:T(8,128)(2,1)}, bf16[768,768]{1,0:T(8,128)(2,1)S(1)}, u32[]{:S(2)}, u32[]{:S(2)}) collective-permute-start(bf16[768,768]{1,0:T(8,128)(2,1)} %bitcast.27), channel_id=1, source_target_pairs={{0,64},{1,449},{64,128},{65,1},{128,65},{129,192},{192,129},{193,2... | collective-permute-start | bytes 3538952 | tf_op jit(solution)/shard_map/ppermute | solution.py:249
  6.6 7.3 %collective-permute-start.1 = (bf16[768,768]{1,0:T(8,128)(2,1)}, bf16[768,768]{1,0:T(8,128)(2,1)}, u32[]{:S(2)}, u32[]{:S(2)}) collective-permute-start(bf16[768,768]{1,0:T(8,128)(2,1)} %bitcast.28), channel_id=1, source_target_pairs={{0,64},{1,449},{64,128},{65,1},{128,65},{129,192},{192,129},{193,2... | collective-permute-start | bytes 3538952 | tf_op jit(solution)/shard_map/ppermute | solution.py:249
  13.9 0.0 copy-start
  13.9 1.0 copy-done
  14.9 0.0 copy-start.2
  14.9 1.0 copy-done.2
  15.8 0.9 copy-done.4
  16.8 0.9 shard_map.76
  17.7 44.0 %conditional.1 = (bf16[2,256,768]{2,0,1:T(2,128)(2,1)S(1)}) conditional(s32[]{:T(128)} %convert_element_type.15, bf16[2,256,768]{2,1,0:T(8,128)(2,1)S(1)} %get-tuple-element.24, bf16[2,256,768]{2,1,0:T(8,128)(2,1)S(1)} %get-tuple-element.24), branch_computations={%region_0.0_spmd, %region_1.0_spmd} | conditional | bytes 3145736 | solution.py:267
  17.7 0.8 copy.17
  18.5 43.2 %all_to_all.24 = bf16[256,2,768]{2,1,0:T(2,128)(2,1)S(1)} all-to-all(bf16[256,2,768]{2,1,0:T(2,128)(2,1)S(1)} %bitcast.25), channel_id=1, replica_groups=mesh['dp'=4,'yl'=2,'x'=4,'zh'=4,'zl'=2,'core'=2] {'dp','yl','x','zh','zl'}, dimensions={0} | all-to-all | bytes 1572864 | tf_op jit(solution)/shard_map/cond/branch_1_fun/all_to_all | solution.py:225
  61.7 0.0 collective-permute-done.up_ref
  61.7 0.0 collective-permute-done.1.down_hbm
  61.7 0.1 copy.10.rows_ref
  61.8 3.9 %collective-permute-start.2 = (bf16[2,256,768]{2,1,0:T(8,128)(2,1)S(1)}, bf16[2,256,768]{2,1,0:T(8,128)(2,1)S(1)}, u32[]{:S(2)}, u32[]{:S(2)}) collective-permute-start(bf16[2,256,768]{2,1,0:T(8,128)(2,1)S(1)} %copy.10.rows_ref), channel_id=1, source_target_pairs={{0,1},{1,0},{2,3},{3,2},{4,5},{5,4},{6,7},{7,6},{8,9},{9,8},{10,11... | collective-permute-start | bytes 2359304 | tf_op jit(solution)/shard_map/ppermute | solution.py:253
  65.7 1.9 %collective-permute-done.2.rows_ref.other_rows_ref = bf16[2,256,768]{2,1,0:T(8,128)(2,1)S(1)} collective-permute-done((bf16[2,256,768]{2,1,0:T(8,128)(2,1)S(1)}, bf16[2,256,768]{2,1,0:T(8,128)(2,1)S(1)}, u32[]{:S(2)}, u32[]{:S(2)}) %collective-permute-start.2) | collective-permute-done | bytes 786464 | tf_op jit(solution)/shard_map/ppermute | solution.py:253
  67.6 2.5 %shard_map.78 = (bf16[2,256,768]{2,1,0:T(8,128)(2,1)S(1)}, bf16[256,768]{1,0:T(8,128)(2,1)S(1)}) custom-call(bf16[2,256,768]{2,1,0:T(8,128)(2,1)S(1)} %collective-permute-done.2.rows_ref.other_rows_ref, bf16[768,768]{1,0:T(8,128)(2,1)S(1)} %collective-permute-done.up_ref, bf16[768,768]{1,0:T(8,128)(2,1)} %collective-permute-done.1.down_hbm), custom_call_target="tpu_custom_call" | custom-call | flops 1207959552 | bytes 4325376 | tf_op jit(solution)/shard_map/pallas_call | solution.py:115
  70.1 2.3 %collective-permute-start.3 = (bf16[2,256,768]{2,1,0:T(8,128)(2,1)S(1)}, bf16[2,256,768]{2,1,0:T(8,128)(2,1)S(1)}, u32[]{:S(2)}, u32[]{:S(2)}) collective-permute-start(bf16[2,256,768]{2,1,0:T(8,128)(2,1)S(1)} %get-tuple-element.29), channel_id=1, source_target_pairs={{0,1},{1,0},{2,3},{3,2},{4,5},{5,4},{6,7},{7,6},{8,9},{9,8},{10,11... | collective-permute-start | bytes 2359304 | tf_op jit(solution)/shard_map/ppermute | solution.py:253
  72.4 2.5 %shard_map.77 = (f32[2,256,768]{2,1,0:T(8,128)S(1)}, bf16[256,768]{1,0:T(8,128)(2,1)S(1)}) custom-call(bf16[2,256,768]{2,1,0:T(8,128)(2,1)S(1)} %copy.10.rows_ref, bf16[768,768]{1,0:T(8,128)(2,1)S(1)} %collective-permute-done.up_ref, bf16[768,768]{1,0:T(8,128)(2,1)} %collective-permute-done.1.down_hbm), custom_call_target="tpu_custom_call" | custom-call | flops 1207959552 | bytes 4325376 | tf_op jit(solution)/shard_map/pallas_call | solution.py:115
  74.9 0.0 copy-start.6
  74.9 0.0 collective-permute-done.3
  74.9 0.2 fusion
  75.1 0.6 copy-done.6
  75.6 0.8 copy.12
  76.4 36.8 %all_to_all.25 = bf16[256,2,768]{2,1,0:T(2,128)(2,1)S(1)} all-to-all(bf16[256,2,768]{2,1,0:T(2,128)(2,1)S(1)} %copy.12), channel_id=1, replica_groups=mesh['dp'=4,'yl'=2,'x'=4,'zh'=4,'zl'=2,'core'=2] {'dp','yl','x','zh','zl'}, dimensions={0} | all-to-all | bytes 1572864 | tf_op jit(solution)/shard_map/all_to_all | solution.py:225
  113.2 0.1 copy.18
  113.3 0.9 copy-done.1
  114.2 0.1 copy-done.3
  114.3 1.5 shard_map.79
  115.8 0.7 copy-done.8
  116.4 6.3 %all-to-all-start.2 = ((bf16[32,24,128]{2,1,0:T(8,128)(2,1)}), bf16[32,24,128]{2,1,0:T(8,128)(2,1)S(1)}, u32[]{:S(2)}, u32[]{:S(2)}) async-start(bf16[32,24,128]{2,1,0:T(8,128)(2,1)} %bitcast.9), calls=%async_computation.2 | async-start | bytes 393216 | tf_op jit(solution)/shard_map/all_to_all | solution.py:225
  122.8 0.0 copy-start.7
  122.8 1.0 copy-done.7
  123.8 0.8 shard_map.83
  124.6 0.0 copy-start.5
  124.6 0.0 copy-start.9
  124.6 3.4 %collective-permute-start.4 = (bf16[768,768]{1,0:T(8,128)(2,1)S(1)}, bf16[768,768]{1,0:T(8,128)(2,1)}, u32[]{:S(2)}, u32[]{:S(2)}) collective-permute-start(bf16[768,768]{1,0:T(8,128)(2,1)S(1)} %shard_map.83), channel_id=1, source_target_pairs={{64,0},{449,1},{128,64},{1,65},{65,128},{192,129},{129,192},{256,1... | collective-permute-start | bytes 3538952 | tf_op jit(solution)/shard_map/ppermute | solution.py:249
  128.1 2.3 %all-to-all-done.2.parts_ref = bf16[32,24,128]{2,1,0:T(8,128)(2,1)S(1)} async-done(((bf16[32,24,128]{2,1,0:T(8,128)(2,1)}), bf16[32,24,128]{2,1,0:T(8,128)(2,1)S(1)}, u32[]{:S(2)}, u32[]{:S(2)}) %all-to-all-start.2) | async-done | bytes 196640 | tf_op jit(solution)/shard_map/all_to_all | solution.py:225
  130.4 16.9 %all_to_all.26.parts_ref = f32[16,24,128]{2,1,0:T(8,128)S(1)} all-to-all(f32[16,24,128]{2,1,0:T(8,128)S(1)} %shard_map.81), channel_id=1, replica_groups=mesh['dp'=4,'yl'=2,'x'=4,'zh'=4,'zl'=2,'core'=2] {'dp','zh'}, dimensions={0} | all-to-all | bytes 393216 | tf_op jit(solution)/shard_map/all_to_all | solution.py:225
  147.3 0.7 shard_map.82
  148.0 7.1 %all-to-all-start.4 = ((bf16[32,24,128]{2,1,0:T(8,128)(2,1)}), bf16[32,24,128]{2,1,0:T(8,128)(2,1)S(1)}, u32[]{:S(2)}, u32[]{:S(2)}) async-start(bf16[32,24,128]{2,1,0:T(8,128)(2,1)} %shard_map.82), calls=%async_computation.4 | async-start | bytes 393216 | tf_op jit(solution)/shard_map/all_to_all | solution.py:225
  155.1 0.0 copy-done.5
  155.2 0.0 copy-done.9
  155.2 1.0 shard_map.80
  156.2 6.5 %all-to-all-done.4 = bf16[32,24,128]{2,1,0:T(8,128)(2,1)S(1)} async-done(((bf16[32,24,128]{2,1,0:T(8,128)(2,1)}), bf16[32,24,128]{2,1,0:T(8,128)(2,1)S(1)}, u32[]{:S(2)}, u32[]{:S(2)}) %all-to-all-start.4) | async-done | bytes 196640 | tf_op jit(solution)/shard_map/all_to_all | solution.py:225
  162.7 0.8 bitcast_convert_fusion
  163.5 0.0 collective-permute-done.4
  163.5 2.4 %copy.22 = bf16[1,768,768]{2,1,0:T(8,128)(2,1)} copy(bf16[1,768,768]{2,1,0:T(8,128)(2,1)} %bitcast.11) | data formatting | bytes 2359296
  (5 shorter events, 0.1 us)
Async XLA Ops:
  0.6 61.1 %collective-permute-start = (bf16[768,768]{1,0:T(8,128)(2,1)}, bf16[768,768]{1,0:T(8,128)(2,1)S(1)}, u32[]{:S(2)}, u32[]{:S(2)}) collective-permute-start(bf16[768,768]{1,0:T(8,128)(2,1)} %bitcast.27), channel_id=1, source_target_pairs={{0,64},{1,449},{64,128},{65,1},{128,65},{129,192},{192,129},{193,2... | collective-permute-start | bytes 3538952 | tf_op jit(solution)/shard_map/ppermute | solution.py:249
  6.6 55.1 %collective-permute-start.1 = (bf16[768,768]{1,0:T(8,128)(2,1)}, bf16[768,768]{1,0:T(8,128)(2,1)}, u32[]{:S(2)}, u32[]{:S(2)}) collective-permute-start(bf16[768,768]{1,0:T(8,128)(2,1)} %bitcast.28), channel_id=1, source_target_pairs={{0,64},{1,449},{64,128},{65,1},{128,65},{129,192},{192,129},{193,2... | collective-permute-start | bytes 3538952 | tf_op jit(solution)/shard_map/ppermute | solution.py:249
  13.9 1.0 copy-start
  14.9 1.0 copy-start.2
  15.8 0.9 copy-start.4
  61.8 5.8 %collective-permute-start.2 = (bf16[2,256,768]{2,1,0:T(8,128)(2,1)S(1)}, bf16[2,256,768]{2,1,0:T(8,128)(2,1)S(1)}, u32[]{:S(2)}, u32[]{:S(2)}) collective-permute-start(bf16[2,256,768]{2,1,0:T(8,128)(2,1)S(1)} %copy.10.rows_ref), channel_id=1, source_target_pairs={{0,1},{1,0},{2,3},{3,2},{4,5},{5,4},{6,7},{7,6},{8,9},{9,8},{10,11... | collective-permute-start | bytes 2359304 | tf_op jit(solution)/shard_map/ppermute | solution.py:253
  70.1 4.8 %collective-permute-start.3 = (bf16[2,256,768]{2,1,0:T(8,128)(2,1)S(1)}, bf16[2,256,768]{2,1,0:T(8,128)(2,1)S(1)}, u32[]{:S(2)}, u32[]{:S(2)}) collective-permute-start(bf16[2,256,768]{2,1,0:T(8,128)(2,1)S(1)} %get-tuple-element.29), channel_id=1, source_target_pairs={{0,1},{1,0},{2,3},{3,2},{4,5},{5,4},{6,7},{7,6},{8,9},{9,8},{10,11... | collective-permute-start | bytes 2359304 | tf_op jit(solution)/shard_map/ppermute | solution.py:253
  74.9 0.7 copy-start.6
  113.2 1.0 copy-start.1
  113.2 1.1 copy-start.3
  115.8 0.7 copy-start.8
  116.4 13.9 %all-to-all-start.2 = ((bf16[32,24,128]{2,1,0:T(8,128)(2,1)}), bf16[32,24,128]{2,1,0:T(8,128)(2,1)S(1)}, u32[]{:S(2)}, u32[]{:S(2)}) async-start(bf16[32,24,128]{2,1,0:T(8,128)(2,1)} %bitcast.9), calls=%async_computation.2 | async-start | bytes 393216 | tf_op jit(solution)/shard_map/all_to_all | solution.py:225
  122.8 1.0 copy-start.7
  124.6 30.6 %copy-start.5 = (bf16[768,128]{1,0:T(8,128)(2,1)S(1)}, bf16[768,128]{1,0:T(8,128)(2,1)}, u32[]{:S(2)}) copy-start(bf16[768,128]{1,0:T(8,128)(2,1)} %router_ref.3) | copy-start | bytes 589828
  124.6 30.6 %copy-start.9 = (bf16[128,768]{1,0:T(8,128)(2,1)S(1)}, bf16[128,768]{1,0:T(8,128)(2,1)}, u32[]{:S(2)}) copy-start(bf16[128,768]{1,0:T(8,128)(2,1)} %copy-done.8) | copy-start | bytes 589828
  124.6 38.9 %collective-permute-start.4 = (bf16[768,768]{1,0:T(8,128)(2,1)S(1)}, bf16[768,768]{1,0:T(8,128)(2,1)}, u32[]{:S(2)}, u32[]{:S(2)}) collective-permute-start(bf16[768,768]{1,0:T(8,128)(2,1)S(1)} %shard_map.83), channel_id=1, source_target_pairs={{64,0},{449,1},{128,64},{1,65},{65,128},{192,129},{129,192},{256,1... | collective-permute-start | bytes 3538952 | tf_op jit(solution)/shard_map/ppermute | solution.py:249
  148.0 14.7 %all-to-all-start.4 = ((bf16[32,24,128]{2,1,0:T(8,128)(2,1)}), bf16[32,24,128]{2,1,0:T(8,128)(2,1)S(1)}, u32[]{:S(2)}, u32[]{:S(2)}) async-start(bf16[32,24,128]{2,1,0:T(8,128)(2,1)} %shard_map.82), calls=%async_computation.4 | async-start | bytes 393216 | tf_op jit(solution)/shard_map/all_to_all | solution.py:225
